TPU v7x, 256 devices: a whole 4x4x8 slice. The times are simulated.
256 devices in a mesh: ctx: 64 (over z, y, core), batch: 4 (over x).
Axes of the slice: x: 4, y: 4, z: 8, core: 2. Of those that a mesh axis runs over, the one named last changes fastest.
Arguments:
- queries: bfloat16 [2048, 2, 8192], P(('ctx', 'batch')), may hold values from -40 to 40
- new_keys: bfloat16 [2048, 2, 1024], P(('ctx', 'batch')), may hold values from -18 to 18
- new_values: bfloat16 [2048, 2, 1024], P(('ctx', 'batch')), may hold values from -6 to 6
- suffix_keys: bfloat16 [2048, 32, 1024], P(('ctx', 'batch')), may hold values from -15 to 15
- suffix_values: bfloat16 [2048, 32, 1024], P(('ctx', 'batch')), may hold values from -6 to 6
- suffix_length: int32 [2048], P(('ctx', 'batch')), may hold values from 1 to 32
- group_ids: int32 [2048, 1], P('ctx'), may hold values from 0 to 63, as said below
- prefix_keys: bfloat16 [64, 256, 1024], P('ctx', None, 'batch'), may hold values from -6 to 6
- prefix_values: bfloat16 [64, 256, 1024], P('ctx', None, 'batch'), may hold values from -6 to 6
- prefix_length: int32 [64], P('ctx'), may hold values from 64 to 256
Outputs:
- attended: bfloat16 [2048, 2, 8192], P(('ctx', 'batch'))
Inputs may be any that keep to these rules, and one draw needn't show every extreme that they name: `group_ids`: in each aligned block of 32 rows no group is named more than 2 times, and some group is named exactly 2 times in every block.
All inputs are finite; a program needn't handle non-finite values.
Results may differ from a plain program's by a relative error of at most 0.0026.
Values may be sent and summed in bfloat16 or wider, within the bound.
No kernel may reach another device: no remote copies, remote signals or barrier semaphores. Data moves between devices by JAX's collectives and lax.ppermute only.
A program may use at most 128 MiB of HBM per device.

v0:
```python
import math

import jax
import jax.numpy as jnp
from jax import lax
from jax.sharding import PartitionSpec as P

HEADS = 64
KV_HEADS = 8
HEAD_DIM = 128
PREFIX_MAX = 256
STEPS = 2
SUFFIX_MAX = 32


def attend_prefix(arrived, prefix_keys, prefix_values, prefix_length):
    leading = arrived.shape[:-1]
    row_count = math.prod(leading)
    kv_here = prefix_keys.shape[2] // HEAD_DIM
    group_size = HEADS // KV_HEADS
    factor = 1.0 / math.sqrt(HEAD_DIM)
    query_rows = arrived.reshape(row_count, kv_here, group_size, HEAD_DIM)
    shared_keys = prefix_keys[0].reshape(PREFIX_MAX, kv_here, HEAD_DIM)
    shared_values = prefix_values[0].reshape(PREFIX_MAX, kv_here, HEAD_DIM)
    block_width = min(512, PREFIX_MAX)
    length = prefix_length[0]
    blocks = (length + block_width - 1) // block_width

    def scores_of(block_index):
        offset = block_index * block_width
        scores = (
            jnp.einsum(
                "qkgd,jkd->qkgj", query_rows, shared_keys, preferred_element_type=jnp.float32
            )
            * factor
        )
        usable = offset + jnp.arange(block_width, dtype=jnp.int32) < length
        return (scores, usable, offset)

    def find_highest(block_index, highest):
        scores, usable, offset = scores_of(block_index)
        return jnp.maximum(highest, jnp.max(jnp.where(usable, scores, -jnp.inf), axis=-1))

    highest = lax.fori_loop(
        0, blocks, find_highest, jnp.full((row_count, kv_here, group_size), -jnp.inf, jnp.float32)
    )

    def accumulate(block_index, carried):
        weight_sum, summed = carried
        scores, usable, offset = scores_of(block_index)
        weights = jnp.where(usable, jnp.exp(scores - highest[..., None]), 0.0)
        summed = summed + jnp.einsum(
            "qkgj,jkd->qkgd",
            weights.astype(jnp.bfloat16),
            shared_values,
            preferred_element_type=jnp.float32,
        )
        return (weight_sum + jnp.sum(weights, axis=-1), summed)

    starting = (
        jnp.zeros((row_count, kv_here, group_size), jnp.float32),
        jnp.zeros((row_count, kv_here, group_size, HEAD_DIM), jnp.float32),
    )
    weight_sum, summed = lax.fori_loop(0, blocks, accumulate, starting)
    output = (summed / weight_sum[..., None]).astype(jnp.bfloat16)
    log_total = highest + jnp.log(weight_sum)
    return (
        output.reshape(leading + (kv_here * group_size * HEAD_DIM,)),
        log_total.reshape(leading + (kv_here * group_size,)),
    )


def split_three(values):
    upper = values.astype(jnp.bfloat16)
    remain = values - lax.optimization_barrier(upper).astype(jnp.float32)
    middle = remain.astype(jnp.bfloat16)
    leftover = remain - lax.optimization_barrier(middle).astype(jnp.float32)
    lowest = leftover.astype(jnp.bfloat16)
    return jnp.concatenate([upper, middle, lowest], axis=-1)


def join_three(pieces, heads_here):
    leading = pieces.shape[:-1]
    parts = pieces.reshape(leading + (3, heads_here)).astype(jnp.float32)
    return parts[..., 0, :] + parts[..., 1, :] + parts[..., 2, :]


def attend_local(queries, new_keys, new_values, suffix_keys, suffix_values, suffix_length):
    local_rows = queries.shape[0]
    group_size = HEADS // KV_HEADS
    factor = 1.0 / math.sqrt(HEAD_DIM)
    query_rows = queries.reshape(local_rows, STEPS, KV_HEADS, group_size, HEAD_DIM)
    cached_keys = suffix_keys.reshape(local_rows, SUFFIX_MAX, KV_HEADS, HEAD_DIM)
    cached_values = suffix_values.reshape(local_rows, SUFFIX_MAX, KV_HEADS, HEAD_DIM)
    latest_keys = new_keys.reshape(local_rows, STEPS, KV_HEADS, HEAD_DIM)
    latest_values = new_values.reshape(local_rows, STEPS, KV_HEADS, HEAD_DIM)
    suffix_scores = (
        jnp.einsum("rtkgd,rjkd->rtkgj", query_rows, cached_keys, preferred_element_type=jnp.float32)
        * factor
    )
    latest_scores = (
        jnp.einsum("rtkgd,rjkd->rtkgj", query_rows, latest_keys, preferred_element_type=jnp.float32)
        * factor
    )
    suffix_usable = (jnp.arange(SUFFIX_MAX, dtype=jnp.int32)[None, :] < suffix_length[:, None])[
        :, None, None, None, :
    ]
    step_index = jnp.arange(STEPS, dtype=jnp.int32)
    latest_usable = (step_index[None, :] <= step_index[:, None])[None, :, None, None, :]
    highest = jnp.maximum(
        jnp.max(jnp.where(suffix_usable, suffix_scores, -jnp.inf), axis=-1),
        jnp.max(jnp.where(latest_usable, latest_scores, -jnp.inf), axis=-1),
    )
    suffix_weights = jnp.where(suffix_usable, jnp.exp(suffix_scores - highest[..., None]), 0.0)
    latest_weights = jnp.where(latest_usable, jnp.exp(latest_scores - highest[..., None]), 0.0)
    weight_sum = jnp.sum(suffix_weights, axis=-1) + jnp.sum(latest_weights, axis=-1)
    output = jnp.einsum(
        "rtkgj,rjkd->rtkgd",
        suffix_weights.astype(jnp.bfloat16),
        cached_values,
        preferred_element_type=jnp.float32,
    )
    output = output + jnp.einsum(
        "rtkgj,rjkd->rtkgd",
        latest_weights.astype(jnp.bfloat16),
        latest_values,
        preferred_element_type=jnp.float32,
    )
    return (highest, weight_sum, output)


def combine_parts(prefix_out, prefix_lse, local_max, local_total, local_out):
    local_rows = prefix_out.shape[0]
    group_size = HEADS // KV_HEADS
    prefix_float = prefix_out.reshape(local_rows, STEPS, KV_HEADS, group_size, HEAD_DIM).astype(
        jnp.float32
    )
    prefix_log = prefix_lse.reshape(local_rows, STEPS, KV_HEADS, group_size)
    highest = jnp.maximum(prefix_log, local_max)
    prefix_part = jnp.exp(prefix_log - highest)
    local_part = jnp.exp(local_max - highest)
    numerator = prefix_part[..., None] * prefix_float + local_part[..., None] * local_out
    denominator = prefix_part + local_part * local_total
    return (
        (numerator / denominator[..., None])
        .astype(jnp.bfloat16)
        .reshape(local_rows, STEPS, HEADS * HEAD_DIM)
    )


def slot_numbers(group_of, capacity):
    row_count = group_of.shape[0]
    matches = group_of[:, None] == group_of[None, :]
    earlier = (
        jnp.arange(row_count, dtype=jnp.int32)[:, None]
        > jnp.arange(row_count, dtype=jnp.int32)[None, :]
    )
    position = jnp.sum(jnp.logical_and(matches, earlier), axis=1)
    return group_of * capacity + position


def one_hot_table(slot_index, slot_count):
    return (jnp.arange(slot_count, dtype=jnp.int32)[:, None] == slot_index[None, :]).astype(
        jnp.bfloat16
    )


def per_device(
    queries,
    new_keys,
    new_values,
    suffix_keys,
    suffix_values,
    suffix_length,
    group_ids,
    prefix_keys,
    prefix_values,
    prefix_length,
):
    owners = lax.axis_size("ctx")
    splits = lax.axis_size("batch")
    local_rows = queries.shape[0]
    block_rows = group_ids.shape[0]
    capacity = max(2, 2 * block_rows // owners)
    columns = queries.shape[2]
    head_columns = columns // splits
    heads_here = HEADS // splits
    local_max, local_total, local_out = attend_local(
        queries, new_keys, new_values, suffix_keys, suffix_values, suffix_length
    )
    own_groups = lax.dynamic_slice_in_dim(
        group_ids[:, 0], lax.axis_index("batch") * local_rows, local_rows
    )
    slot_index = slot_numbers(own_groups, capacity)
    one_hot = one_hot_table(slot_index, owners * capacity)
    packed = jnp.dot(
        one_hot, queries.reshape(local_rows, STEPS * columns), preferred_element_type=jnp.float32
    )
    packed = packed.astype(jnp.bfloat16).reshape(owners, capacity, STEPS, columns)
    arrived = lax.all_to_all(packed, "ctx", split_axis=0, concat_axis=0, tiled=True)
    item_count = arrived.shape[1]
    by_heads = arrived.reshape(owners, item_count, STEPS, splits, head_columns)
    output, log_total = attend_prefix(
        lax.all_to_all(by_heads, "batch", split_axis=3, concat_axis=0, tiled=True),
        prefix_keys,
        prefix_values,
        prefix_length,
    )
    output, log_pieces = (
        lax.all_to_all(output, "batch", split_axis=0, concat_axis=3, tiled=True),
        lax.all_to_all(split_three(log_total), "batch", split_axis=0, concat_axis=3, tiled=True),
    )
    merged_out = output.reshape(owners, item_count, STEPS, columns)
    merged_log = log_pieces.reshape(owners, item_count, STEPS, 3 * HEADS)
    back_out = lax.all_to_all(merged_out, "ctx", split_axis=0, concat_axis=0, tiled=True)
    back_log = lax.all_to_all(merged_log, "ctx", split_axis=0, concat_axis=0, tiled=True)
    prefix_out = jnp.take(back_out.reshape(owners * capacity, STEPS, columns), slot_index, axis=0)
    picked_log = jnp.take(back_log.reshape(owners * capacity, STEPS, 3 * HEADS), slot_index, axis=0)
    prefix_lse = join_three(
        picked_log.reshape(local_rows, STEPS, splits, 3 * heads_here), heads_here
    ).reshape(local_rows, STEPS, HEADS)
    return combine_parts(prefix_out, prefix_lse, local_max, local_total, local_out)


def solution(mesh):
    placed = (
        P(("ctx", "batch"), None, None),
        P(("ctx", "batch"), None, None),
        P(("ctx", "batch"), None, None),
        P(("ctx", "batch"), None, None),
        P(("ctx", "batch"), None, None),
        P(("ctx", "batch")),
        P("ctx", None),
        P("ctx", None, "batch"),
        P("ctx", None, "batch"),
        P("ctx"),
    )
    return jax.shard_map(
        per_device,
        mesh=mesh,
        in_specs=placed,
        out_specs=P(("ctx", "batch"), None, None),
        check_vma=False,
    )
```

profile of v0, /device:TPU:6, one launch (start us, length us, event | category | flops | bytes accessed | tf_op | source)
XLA Modules:
  0.0 458.5 jit_solution(4386458193546215894)
XLA Ops:
  5.9 7.8 %reshape.182 = bf16[64,2,2,8192]{3,2,1,0:T(2,128)(2,1)} reshape(bf16[128,16384]{1,0:T(8,128)(2,1)} %convolution_convert_fusion) | data formatting | bytes 8388608 | tf_op jit(solution)/shard_map/reshape | solution.py:199
  13.7 108.5 %all_to_all.60 = bf16[64,2,2,8192]{3,2,1,0:T(2,128)(2,1)} all-to-all(bf16[64,2,2,8192]{3,2,1,0:T(2,128)(2,1)} %reshape.182), channel_id=1, replica_groups=mesh['ctx'=64,'batch'=4] {'ctx'}, dimensions={0} | all-to-all | bytes 8388608 | tf_op jit(solution)/shard_map/all_to_all | solution.py:200
  122.3 7.6 %reshape.220 = bf16[64,2,2,4,2048]{4,3,2,1,0:T(4,128)(2,1)} reshape(bf16[64,2,2,8192]{3,2,1,0:T(2,128)(2,1)} %all_to_all.60) | data formatting | bytes 8388608 | tf_op jit(solution)/shard_map/reshape | solution.py:202
  129.8 6.5 %copy.120 = bf16[64,2,2,4,2048]{4,0,2,1,3:T(8,128)(2,1)} copy(bf16[64,2,2,4,2048]{4,3,2,1,0:T(4,128)(2,1)} %reshape.220) | data formatting | bytes 8388608 | tf_op jit(solution)/shard_map/reshape | solution.py:202
  136.3 5.6 %all-to-all-start.1 = ((bf16[64,2,2,4,2048]{4,0,2,1,3:T(8,128)(2,1)}), bf16[64,2,2,4,2048]{4,0,2,1,3:T(8,128)(2,1)}, u32[]{:S(2)}, u32[]{:S(2)}) async-start(bf16[64,2,2,4,2048]{4,0,2,1,3:T(8,128)(2,1)} %copy.120), calls=%async_computation.1 | async-start | bytes 8388608 | tf_op jit(solution)/shard_map/all_to_all | solution.py:204
  143.1 44.5 %all-to-all-done.1 = bf16[64,2,2,4,2048]{4,0,2,1,3:T(8,128)(2,1)} async-done(((bf16[64,2,2,4,2048]{4,0,2,1,3:T(8,128)(2,1)}), bf16[64,2,2,4,2048]{4,0,2,1,3:T(8,128)(2,1)}, u32[]{:S(2)}, u32[]{:S(2)}) %all-to-all-start.1) | async-done | bytes 4194336 | tf_op jit(solution)/shard_map/all_to_all | solution.py:204
  187.6 8.5 %copy.121 = bf16[4,64,2,2,1,2048]{5,3,2,1,0,4:T(2,128)(2,1)} copy(bf16[4,64,2,2,1,2048]{5,1,3,2,0,4:T(8,128)(2,1)} %bitcast.15) | data formatting | bytes 8388608 | tf_op jit(solution)/shard_map/all_to_all | solution.py:204
  196.1 7.6 %reshape.184 = bf16[1024,2,8,128]{3,2,1,0:T(8,128)(2,1)} reshape(bf16[4,64,2,2,1,2048]{5,3,2,1,0,4:T(2,128)(2,1)} %copy.121) | data formatting | bytes 8388608 | tf_op jit(solution)/shard_map/reshape | solution.py:22
  203.7 5.2 %copy.123 = bf16[1024,2,8,128]{3,0,2,1:T(8,128)(2,1)} copy(bf16[1024,2,8,128]{3,2,1,0:T(8,128)(2,1)} %reshape.184) | data formatting | bytes 8388608 | tf_op jit(solution)/shard_map/while | solution.py:44
  208.9 5.5 %while.22 = (s32[]{:T(128)}, f32[1024,2,8]{0,2,1:T(8,128)S(1)}, s32[]{:T(128)}, s32[]{:T(128)}, bf16[256,2,128]{2,0,1:T(8,128)(2,1)S(1)}, /*index=5*/bf16[1024,2,8,128]{3,0,2,1:T(8,128)(2,1)}, s32[]{:T(128)}, s32[]{:T(128)}) while((s32[]{:T(128)}, f32[1024,2,8]{0,2,1:T(8,128)S(1)}, s32[]{:T(128)}, s32[]{:T(128)}, ...), condition=%wide.region_3.4_spmd, body=%wide.region_1.3_spmd.sunk | while | flops 1086325248 | bytes 4588137 | solution.py:44
  209.6 4.8 %select_reduce_fusion.4 = f32[2,1024,8]{1,2,0:T(8,128)S(1)} fusion(pred[256]{0:T(512)(128)(4,1)S(1)} %add_compare_fusion.4, bf16[1024,2,8,128]{3,0,2,1:T(8,128)(2,1)} %get-tuple-element.310, bf16[256,2,128]{2,0,1:T(8,128)(2,1)S(1)} %get-tuple-element.309), kind=kOutput, calls=%fused_computation.2.clone.1 | convolution fusion | flops 1086308352 | bytes 4391168 | tf_op jit(solution)/shard_map/while/body/qkgd,jkd->qkgj/dot_general | solution.py:32
  218.5 24.2 %while.23 = (s32[]{:T(128)}, f32[1024,2,8]{0,2,1:T(8,128)S(1)}, f32[1024,2,8,128]{3,0,2,1:T(8,128)}, s32[]{:T(128)}, s32[]{:T(128)}, /*index=5*/bf16[256,2,128]{...) while((s32[]{:T(128)}, f32[1024,2,8]{0,2,1:T(8,128)S(1)}, ...), condition=%wide.region_6.7_spmd, body=%wide.region_4.6_spmd.sunk | while | flops 2183135744 | bytes 55182208 | solution.py:64
  219.6 10.3 %fusion.66 = (f32[1024,2,8]{0,2,1:T(8,128)S(1)}, f32[2,256,1024,8]{2,1,3,0:T(8,128)}) fusion(f32[1024,2,8]{0,2,1:T(8,128)S(1)} %get-tuple-element.342, pred[256]{0:T(512)(128)(4,1)S(1)} %add_compare_fusion.5, bf16[1024,2,8,128]{3,0,2,1:T(8,128)(2,1)} %get-tuple-element.341, bf16[256,2,128]{2,0,1:T(8,128)(2,1)S(1)} %get-tuple-element.340), kind=kOutput, calls=%fused_computation.10.clone.1 | convolution fusion | flops 1090502656 | bytes 21233920 | tf_op jit(solution)/shard_map/while/body/qkgd,jkd->qkgj/dot_general | solution.py:32
  230.0 12.7 %bitcast_add_fusion.3 = f32[1024,2,8,128]{3,0,2,1:T(8,128)} fusion(f32[1024,2,8,128]{3,0,2,1:T(8,128)} %get-tuple-element.326, f32[2,256,1024,8]{2,1,3,0:T(8,128)} %get-tuple-element.288, f32[1024,2,8]{0,2,1:T(8,128)S(1)} %get-tuple-element.342, pred[256]{0:T(512)(128)(4,1)S(1)} %add_compare_fusion.5, bf16[256,2,128]{2,0,1:T(8,128)(2,1)S(1)} %get-tuple-element.343), kind=kOutput, calls=%fused_computation.12.clone.1 | convolution fusion | flops 1092616192 | bytes 33751296 | tf_op jit(solution)/shard_map/while/body/qkgj,jkd->qkgd/dot_general | solution.py:52
  247.3 5.5 %all-to-all-start.2 = ((bf16[4,2,6144]{2,1,0:T(2,128)(2,1)}), bf16[4,2,6144]{2,1,0:T(2,128)(2,1)S(1)}, u32[]{:S(2)}, u32[]{:S(2)}) async-start(bf16[4,2,6144]{2,1,0:T(2,128)(2,1)} %reshape.232), calls=%async_computation.2 | async-start | bytes 196608 | tf_op jit(solution)/shard_map/all_to_all | solution.py:211
  252.8 5.3 %divide_convert_fusion = bf16[1024,2,8,128]{3,0,2,1:T(8,128)(2,1)S(1)} fusion(f32[1024,2,8,128]{3,0,2,1:T(8,128)} %get-tuple-element.89, f32[1024,2,8]{0,2,1:T(8,128)S(1)} %get-tuple-element.88), kind=kLoop, calls=%fused_computation.24 | loop fusion | flops 4194304 | bytes 12648448 | tf_op jit(solution)/shard_map/convert_element_type | solution.py:65
  262.7 6.9 %reshape.191 = bf16[256,2,2,1,2048]{4,2,1,0,3:T(2,128)(2,1)} reshape(bf16[1024,2,8,128]{3,2,1,0:T(8,128)(2,1)} %copy.140) | data formatting | bytes 8388608 | tf_op jit(solution)/shard_map/reshape | solution.py:68
  269.6 4.9 %all-to-all-start.4 = ((bf16[256,2,2,1,2048]{4,2,1,3,0:T(2,128)(2,1)}), bf16[256,2,2,1,2048]{4,2,1,3,0:T(2,128)(2,1)}, u32[]{:S(2)}, u32[]{:S(2)}) async-start(bf16[256,2,2,1,2048]{4,2,1,3,0:T(2,128)(2,1)} %bitcast.151), calls=%async_computation.4 | async-start | bytes 8388608 | tf_op jit(solution)/shard_map/all_to_all | solution.py:210
  275.7 43.5 %all-to-all-done.4 = bf16[256,2,2,1,2048]{4,2,1,3,0:T(2,128)(2,1)} async-done(((bf16[256,2,2,1,2048]{4,2,1,3,0:T(2,128)(2,1)}), bf16[256,2,2,1,2048]{4,2,1,3,0:T(2,128)(2,1)}, u32[]{:S(2)}, u32[]{:S(2)}) %all-to-all-start.4) | async-done | bytes 4194336 | tf_op jit(solution)/shard_map/all_to_all | solution.py:210
  319.2 8.8 %all-to-all-start.3 = ((bf16[64,2,2,192]{3,2,1,0:T(2,128)(2,1)}), bf16[64,2,2,192]{3,2,1,0:T(2,128)(2,1)S(1)}, u32[]{:S(2)}, u32[]{:S(2)}) async-start(bf16[64,2,2,192]{3,2,1,0:T(2,128)(2,1)} %copy.131), calls=%async_computation.3 | async-start | bytes 262144 | tf_op jit(solution)/shard_map/all_to_all | solution.py:216
  332.5 5.2 %copy.163 = bf16[64,2,2,4,1,2048]{5,3,2,1,0,4:T(4,128)(2,1)} copy(bf16[64,2,2,4,1,2048]{5,0,3,2,1,4:T(8,128)(2,1)S(1)} %bitcast.152) | data formatting | bytes 8388608 | tf_op jit(solution)/shard_map/reshape | solution.py:213
  337.7 8.5 %reshape.221 = bf16[64,2,2,8192]{3,2,1,0:T(2,128)(2,1)} reshape(bf16[64,2,2,4,1,2048]{5,3,2,1,0,4:T(4,128)(2,1)} %copy.163) | data formatting | bytes 8388608 | tf_op jit(solution)/shard_map/reshape | solution.py:213
  346.3 10.8 %all-to-all-start.5 = ((bf16[64,2,2,8192]{3,2,1,0:T(2,128)(2,1)}), bf16[64,2,2,8192]{3,2,1,0:T(2,128)(2,1)}, u32[]{:S(2)}, u32[]{:S(2)}) async-start(bf16[64,2,2,8192]{3,2,1,0:T(2,128)(2,1)} %reshape.221), calls=%async_computation.5 | async-start | bytes 8388608 | tf_op jit(solution)/shard_map/all_to_all | solution.py:215
  361.9 91.4 %all-to-all-done.5 = bf16[64,2,2,8192]{3,2,1,0:T(2,128)(2,1)} async-done(((bf16[64,2,2,8192]{3,2,1,0:T(2,128)(2,1)}), bf16[64,2,2,8192]{3,2,1,0:T(2,128)(2,1)}, u32[]{:S(2)}, u32[]{:S(2)}) %all-to-all-start.5) | async-done | bytes 4194336 | tf_op jit(solution)/shard_map/all_to_all | solution.py:215
  (80 shorter events, 36.4 us)
Async XLA Ops:
  0.0 456.8 %copy-start = (bf16[8,2,1024]{2,1,0:T(2,128)(2,1)S(1)}, bf16[8,2,1024]{2,1,0:T(2,128)(2,1)}, u32[]{:S(2)}) copy-start(bf16[8,2,1024]{2,1,0:T(2,128)(2,1)} %param.16) | copy-start | bytes 98308
  0.9 0.7 copy-start.7
  129.8 12.7 %copy-start.4 = (bf16[1,256,256]{2,1,0:T(8,128)(2,1)S(1)}, bf16[1,256,256]{2,1,0:T(8,128)(2,1)}, u32[]{:S(2)}) copy-start(bf16[1,256,256]{2,1,0:T(8,128)(2,1)} %param.21) | copy-start | bytes 393220
  129.8 13.0 %copy-start.5 = (bf16[1,256,256]{2,1,0:T(8,128)(2,1)S(1)}, bf16[1,256,256]{2,1,0:T(8,128)(2,1)}, u32[]{:S(2)}) copy-start(bf16[1,256,256]{2,1,0:T(8,128)(2,1)} %param.22) | copy-start | bytes 393220
  136.3 51.2 %all-to-all-start.1 = ((bf16[64,2,2,4,2048]{4,0,2,1,3:T(8,128)(2,1)}), bf16[64,2,2,4,2048]{4,0,2,1,3:T(8,128)(2,1)}, u32[]{:S(2)}, u32[]{:S(2)}) async-start(bf16[64,2,2,4,2048]{4,0,2,1,3:T(8,128)(2,1)} %copy.120), calls=%async_computation.1 | async-start | bytes 8388608 | tf_op jit(solution)/shard_map/all_to_all | solution.py:204
  247.3 22.3 %all-to-all-start.2 = ((bf16[4,2,6144]{2,1,0:T(2,128)(2,1)}), bf16[4,2,6144]{2,1,0:T(2,128)(2,1)S(1)}, u32[]{:S(2)}, u32[]{:S(2)}) async-start(bf16[4,2,6144]{2,1,0:T(2,128)(2,1)} %reshape.232), calls=%async_computation.2 | async-start | bytes 196608 | tf_op jit(solution)/shard_map/all_to_all | solution.py:211
  269.6 49.6 %all-to-all-start.4 = ((bf16[256,2,2,1,2048]{4,2,1,3,0:T(2,128)(2,1)}), bf16[256,2,2,1,2048]{4,2,1,3,0:T(2,128)(2,1)}, u32[]{:S(2)}, u32[]{:S(2)}) async-start(bf16[256,2,2,1,2048]{4,2,1,3,0:T(2,128)(2,1)} %bitcast.151), calls=%async_computation.4 | async-start | bytes 8388608 | tf_op jit(solution)/shard_map/all_to_all | solution.py:210
  319.2 27.1 %all-to-all-start.3 = ((bf16[64,2,2,192]{3,2,1,0:T(2,128)(2,1)}), bf16[64,2,2,192]{3,2,1,0:T(2,128)(2,1)S(1)}, u32[]{:S(2)}, u32[]{:S(2)}) async-start(bf16[64,2,2,192]{3,2,1,0:T(2,128)(2,1)} %copy.131), calls=%async_computation.3 | async-start | bytes 262144 | tf_op jit(solution)/shard_map/all_to_all | solution.py:216
  337.7 19.3 %copy-start.1 = (bf16[8,2,8192]{2,1,0:T(2,128)(2,1)S(1)}, bf16[8,2,8192]{2,1,0:T(2,128)(2,1)}, u32[]{:S(2)}) copy-start(bf16[8,2,8192]{2,1,0:T(2,128)(2,1)} %param.14) | copy-start | bytes 786436
  337.7 19.6 %copy-start.2 = (bf16[8,32,1024]{2,1,0:T(8,128)(2,1)S(1)}, bf16[8,32,1024]{2,1,0:T(8,128)(2,1)}, u32[]{:S(2)}) copy-start(bf16[8,32,1024]{2,1,0:T(8,128)(2,1)} %param.17) | copy-start | bytes 1572868
  337.7 19.7 %copy-start.3 = (bf16[8,32,1024]{2,1,0:T(8,128)(2,1)S(1)}, bf16[8,32,1024]{2,1,0:T(8,128)(2,1)}, u32[]{:S(2)}) copy-start(bf16[8,32,1024]{2,1,0:T(8,128)(2,1)} %param.18) | copy-start | bytes 1572868
  337.7 19.8 %copy-start.10 = (s32[8]{0:T(128)S(1)}, s32[8]{0:T(128)}, u32[]{:S(2)}) copy-start(s32[8]{0:T(128)} %param.19) | copy-start | bytes 100
  337.7 19.9 %copy-start.9 = (bf16[8,2,1024]{2,1,0:T(2,128)(2,1)S(1)}, bf16[8,2,1024]{2,1,0:T(2,128)(2,1)}, u32[]{:S(2)}) copy-start(bf16[8,2,1024]{2,1,0:T(2,128)(2,1)} %param.15) | copy-start | bytes 98308
  346.3 13.2 %copy-start.6 = (s32[32,1]{0,1:T(1,128)S(1)}, s32[32,1]{0,1:T(1,128)}, u32[]{:S(2)}) copy-start(s32[32,1]{0,1:T(1,128)} %param.20) | copy-start | bytes 388
  346.3 13.2 %copy-start.8 = (s32[8]{0:T(128)S(1)}, s32[8]{0:T(128)}, u32[]{:S(2)}) copy-start(s32[8]{0:T(128)} %copy-done.7) | copy-start | bytes 100
  346.3 107.0 %all-to-all-start.5 = ((bf16[64,2,2,8192]{3,2,1,0:T(2,128)(2,1)}), bf16[64,2,2,8192]{3,2,1,0:T(2,128)(2,1)}, u32[]{:S(2)}, u32[]{:S(2)}) async-start(bf16[64,2,2,8192]{3,2,1,0:T(2,128)(2,1)} %reshape.221), calls=%async_computation.5 | async-start | bytes 8388608 | tf_op jit(solution)/shard_map/all_to_all | solution.py:215
where the time goes:
time: 466 us; the launch traced here: 459 us
  waiting for transfers between devices  179 us (38%)
  blocking collectives  109 us (23%)
  local copies, waits for them, and re-layouts  88.6 us (19%)
  starting transfers between devices  35.5 us (8%)
  matrix products  33.8 us (7%)
  other arithmetic  10.9 us (2%)
    all_to_all x1, blocking collectives, per_device(): lax.all_to_all(packed, 'ctx', split_axis=0, concat_axis=0, tiled=True)  109 us
    all_to_all x1, waiting for transfers between devices, per_device(): lax.all_to_all(merged_out, 'ctx', split_axis=0, concat_axis=0, tiled=True)  91.4 us
    all_to_all x1, waiting for transfers between devices, per_device(): lax.all_to_all(by_heads, 'batch', split_axis=3, concat_axis=0, tiled=True)  44.5 us
    all_to_all x1, waiting for transfers between devices, per_device(): lax.all_to_all(output, 'batch', split_axis=0, concat_axis=3, tiled=True)  43.5 us
    dot_general x2, matrix products, scores_of(): jnp.einsum('qkgd,jkd->qkgj', query_rows, shared_keys, preferred_element_t...  15.1 us
    reshape x2, local copies, waits for them, and re-layouts, per_device(): by_heads = arrived.reshape(owners, item_count, STEPS, splits, head_columns)  14.1 us
    reshape x2, local copies, waits for them, and re-layouts, per_device(): merged_out = output.reshape(owners, item_count, STEPS, columns)  13.7 us
    dot_general x1, matrix products, accumulate(): jnp.einsum('qkgj,jkd->qkgd', weights.astype(jnp.bfloat16), shared_values,...  12.7 us
  transfers between devices with their start and end apart: 5, of which 3 were waited for; matrix products, arithmetic and copies ran while one was open for 9% of the time, Pallas kernels for 0%

commit v1 on v0

v1 whole, which is shorter than its diff:
```python
import functools
import math

import jax
import jax.numpy as jnp
from jax import lax
from jax.experimental import pallas as pl
from jax.experimental.pallas import tpu as pltpu
from jax.sharding import Mesh, PartitionSpec as P

HEADS = 64
KV_HEADS = 8
HEAD_DIM = 128
PREFIX_MAX = 256
STEPS = 2
SUFFIX_MAX = 32
GROUP = HEADS // KV_HEADS
ROWS = GROUP * STEPS
FACTOR = 1.0 / math.sqrt(HEAD_DIM)
Z, Y, CORES, X = 8, 4, 2, 4
LOCAL = 8
HELD = KV_HEADS // X
OWNED = Z * CORES
EARLY = 10
PER_GROUP = 2
REQUESTS = X * LOCAL
BLOCK = PER_GROUP * ROWS
UNITS = OWNED * HELD
OUT_ROWS = UNITS * BLOCK
CACHE_ROWS = 2 * HELD * PREFIX_MAX
CACHE_BLOCK = CACHE_ROWS + 16
F32 = jnp.float32
BF16 = jnp.bfloat16
PARAMS = pltpu.CompilerParams(vmem_limit_bytes=10 * 1024 * 1024)
STAGING = pltpu.CompilerParams(vmem_limit_bytes=32 * 1024 * 1024)


def padded(count):
    return -(-count // 16) * 16


def dot_t(a, b):
    return lax.dot_general(a, b, (((1,), (1,)), ((), ())), preferred_element_type=F32)


def iota(shape, dim):
    return lax.broadcasted_iota(jnp.int32, shape, dim)


def local_kernel(length_ref, q_ref, sk_ref, sv_ref, nk_ref, nv_ref, out_ref, stat_ref):
    width = KV_HEADS * SUFFIX_MAX
    fresh = KV_HEADS * STEPS
    row = iota((HEADS * STEPS, width), 0)
    col = iota((HEADS * STEPS, width), 1)
    same_head = row // ROWS == col // SUFFIX_MAX
    position = col % SUFFIX_MAX
    row2 = iota((HEADS * STEPS, fresh), 0)
    col2 = iota((HEADS * STEPS, fresh), 1)
    seen = jnp.logical_and(row2 // ROWS == col2 // STEPS, col2 % STEPS <= row2 % STEPS)
    lane = iota((HEADS * STEPS, HEAD_DIM), 1)
    columns = jnp.zeros((HEADS * STEPS, HEAD_DIM), F32)
    for r in range(LOCAL):
        q = q_ref[r]
        keys = jnp.concatenate(
            [sk_ref[r, :, k * HEAD_DIM : (k + 1) * HEAD_DIM] for k in range(KV_HEADS)], axis=0
        )
        values = jnp.concatenate(
            [sv_ref[r, :, k * HEAD_DIM : (k + 1) * HEAD_DIM] for k in range(KV_HEADS)], axis=0
        )
        usable = jnp.logical_and(same_head, position < length_ref[r])
        old = jnp.where(usable, dot_t(q, keys) * FACTOR, -jnp.inf)
        new = jnp.where(seen, dot_t(q, nk_ref[r]) * FACTOR, -jnp.inf)
        highest = jnp.maximum(
            jnp.max(old, axis=1, keepdims=True), jnp.max(new, axis=1, keepdims=True)
        )
        old = jnp.exp(old - highest)
        new = jnp.exp(new - highest)
        total = jnp.sum(old, axis=1, keepdims=True) + jnp.sum(new, axis=1, keepdims=True)
        out = jnp.dot(old.astype(BF16), values, preferred_element_type=F32)
        out_ref[r] = out + jnp.dot(new.astype(BF16), nv_ref[r], preferred_element_type=F32)
        columns = jnp.where(lane == r, highest, jnp.where(lane == LOCAL + r, total, columns))
    stat_ref[...] = columns.T[: 2 * LOCAL]


def attend_local(lengths, q, sk, sv, nk, nv):
    vm = pl.BlockSpec(memory_space=pltpu.VMEM)
    shape = jax.ShapeDtypeStruct((LOCAL, HEADS * STEPS, HEAD_DIM), F32)
    return pl.pallas_call(
        local_kernel,
        out_shape=(shape, jax.ShapeDtypeStruct((2 * LOCAL, HEADS * STEPS), F32)),
        in_specs=[pl.BlockSpec(memory_space=pltpu.SMEM)] + [vm] * 5,
        out_specs=(vm, vm),
        compiler_params=PARAMS,
        name="local_attention",
    )(lengths, q, sk, sv, nk, nv)


def split_kernel(x_ref, q_ref, *refs):
    out_refs, sems = refs[:X], refs[X]
    wide = HELD * ROWS
    copies = []
    for s in range(X):
        head = pl.multiple_of(lax.rem(x_ref[0] + s, X) * wide, wide)
        for r in range(LOCAL):
            copies.append(
                pltpu.make_async_copy(
                    q_ref.at[r, pl.ds(head, wide), :],
                    out_refs[s].at[pl.ds(r * wide, wide), :],
                    sems.at[s, r],
                )
            )
    for copy in copies:
        copy.start()
    for copy in copies:
        copy.wait()


def split(x, q):
    part = jax.ShapeDtypeStruct((LOCAL * HELD * ROWS, HEAD_DIM), BF16)
    return pl.pallas_call(
        split_kernel,
        out_shape=[part] * X,
        in_specs=[pl.BlockSpec(memory_space=pltpu.SMEM), pl.BlockSpec(memory_space=pltpu.HBM)],
        out_specs=[pl.BlockSpec(memory_space=pltpu.VMEM)] * X,
        scratch_shapes=[pltpu.SemaphoreType.DMA((X, LOCAL))],
        compiler_params=STAGING,
        name="split_queries",
    )(x, q)


def cache_kernel(length_ref, k_ref, v_ref, cache_ref, sems):
    copies = []
    for i, ref in enumerate((k_ref, v_ref)):
        for h in range(HELD):
            at = (i * HELD + h) * PREFIX_MAX
            copies.append(
                pltpu.make_async_copy(
                    ref.at[0, :, pl.ds(h * HEAD_DIM, HEAD_DIM)],
                    cache_ref.at[pl.ds(at, PREFIX_MAX), :],
                    sems.at[i, h],
                )
            )
    for copy in copies:
        copy.start()
    length = jnp.full((16, HEAD_DIM), length_ref[0], jnp.int32)
    cache_ref[CACHE_ROWS:, :] = length.astype(F32).astype(BF16)
    for copy in copies:
        copy.wait()


def build_cache(length, keys, values):
    hbm = pl.BlockSpec(memory_space=pltpu.HBM)
    return pl.pallas_call(
        cache_kernel,
        out_shape=jax.ShapeDtypeStruct((CACHE_ROWS + 16, HEAD_DIM), BF16),
        in_specs=[pl.BlockSpec(memory_space=pltpu.SMEM)] + [hbm] * 2,
        out_specs=pl.BlockSpec(memory_space=pltpu.VMEM),
        scratch_shapes=[pltpu.SemaphoreType.DMA((2, HELD))],
        compiler_params=STAGING,
        name="build_cache",
    )(length, keys, values)


def stack_kernel(*refs):
    parts, out_ref = refs[:-1], refs[-1]
    size = parts[0].shape[0]
    for i, ref in enumerate(parts):
        out_ref[i * size : (i + 1) * size, :] = ref[...]


def stack(parts):
    vm = pl.BlockSpec(memory_space=pltpu.VMEM)
    size, width = parts[0].shape
    return pl.pallas_call(
        stack_kernel,
        out_shape=jax.ShapeDtypeStruct((len(parts) * size, width), parts[0].dtype),
        in_specs=[vm] * len(parts),
        out_specs=vm,
        compiler_params=PARAMS,
        name="stack_caches",
    )(*parts)


def pack_kernel(place_ref, *refs):
    q_refs, out_refs, packed_ref = refs[:X], refs[X : X + Y], refs[X + Y]
    packed_ref[...] = jnp.zeros(packed_ref.shape, BF16)
    for i in range(REQUESTS):
        for h in range(HELD):
            start = pl.multiple_of((place_ref[i] + h * PER_GROUP) * ROWS, ROWS)
            at = ((i % LOCAL) * HELD + h) * ROWS
            packed_ref[pl.ds(start, ROWS), :] = q_refs[i // LOCAL][at : at + ROWS, :]
    for s in range(Y):
        out_refs[s][...] = packed_ref[s * OUT_ROWS : (s + 1) * OUT_ROWS, :]


def pack(place, queries):
    vm = pl.BlockSpec(memory_space=pltpu.VMEM)
    return pl.pallas_call(
        pack_kernel,
        out_shape=[jax.ShapeDtypeStruct((OUT_ROWS, HEAD_DIM), BF16)] * Y,
        in_specs=[pl.BlockSpec(memory_space=pltpu.SMEM)] + [vm] * X,
        out_specs=[vm] * Y,
        scratch_shapes=[pltpu.VMEM((Y * OUT_ROWS, HEAD_DIM), BF16)],
        compiler_params=PARAMS,
        name="pack_queries",
    )(place, *queries)


def prefix_kernel(first, count, *refs):
    q_refs, caches, out_refs = refs[:Y], refs[Y:-Y], refs[-Y:]
    column = iota((1, PREFIX_MAX), 1).astype(F32)
    lane = iota((Y * BLOCK, HEAD_DIM), 1)
    diagonal = lane % ROWS == iota((Y * BLOCK, HEAD_DIM), 0) % ROWS
    piece = iota((Y * PER_GROUP, HEAD_DIM), 1) // ROWS
    lines = []
    for j in range(count):
        cache, base = caches[j // CORES], j % CORES * CACHE_BLOCK
        length = cache[base + CACHE_ROWS : base + CACHE_BLOCK, :].astype(F32)[:1, :1]
        usable = column < length
        for h in range(HELD):
            unit = (first + j) * HELD + h
            q = jnp.concatenate(
                [ref[unit * BLOCK : (unit + 1) * BLOCK, :] for ref in q_refs], axis=0
            )
            at = base + h * PREFIX_MAX
            keys = cache[at : at + PREFIX_MAX, :]
            at += HELD * PREFIX_MAX
            values = cache[at : at + PREFIX_MAX, :]
            scores = jnp.where(usable, dot_t(q, keys) * FACTOR, -jnp.inf)
            highest = jnp.max(scores, axis=1, keepdims=True)
            weights = jnp.exp(scores - highest)
            total = jnp.sum(weights, axis=1, keepdims=True)
            out = jnp.dot(weights.astype(BF16), values, preferred_element_type=F32)
            out = (out / total).astype(BF16)
            at = (j * HELD + h) * BLOCK
            for s in range(Y):
                out_refs[s][at : at + BLOCK, :] = out[s * BLOCK : (s + 1) * BLOCK]
            log_total = jnp.where(diagonal, highest + jnp.log(total), 0.0)
            line = jnp.sum(log_total.reshape(Y * PER_GROUP, ROWS, HEAD_DIM), axis=1)
            upper = line.astype(BF16).astype(F32)
            remain = line - upper
            middle = remain.astype(BF16).astype(F32)
            lowest = remain - middle
            lines.append(jnp.where(piece == 0, upper, jnp.where(piece == 1, middle, lowest)))
    units = count * HELD
    blank = padded(units * PER_GROUP) - units * PER_GROUP
    for s in range(Y):
        part = [x[s * PER_GROUP : (s + 1) * PER_GROUP] for x in lines]
        if blank:
            part.append(jnp.zeros((blank, HEAD_DIM), F32))
        out_refs[s][units * BLOCK :, :] = jnp.concatenate(part, axis=0).astype(BF16)


def attend_prefix(first, queries, caches):
    count = len(caches) * CORES
    units = count * HELD
    rows = units * BLOCK + padded(units * PER_GROUP)
    vm = pl.BlockSpec(memory_space=pltpu.VMEM)
    return pl.pallas_call(
        functools.partial(prefix_kernel, first, count),
        out_shape=[jax.ShapeDtypeStruct((rows, HEAD_DIM), BF16)] * Y,
        in_specs=[vm] * (Y + len(caches)),
        out_specs=[vm] * Y,
        compiler_params=PARAMS,
        name="prefix_attention_%d" % first,
    )(*queries, *caches)


def unpack_kernel(place_ref, line_ref, *refs):
    early, late = refs[:Y], refs[Y : 2 * Y]
    out_refs, all_ref = refs[2 * Y : 2 * Y + X], refs[2 * Y + X]
    cut = EARLY * HELD * BLOCK
    for s in range(Y):
        base = s * OUT_ROWS
        all_ref[base : base + cut, :] = early[s][:cut, :]
        all_ref[base + cut : base + OUT_ROWS, :] = late[s][: OUT_ROWS - cut, :]
    sources = jnp.concatenate(
        [ref[cut:, :] for ref in early] + [ref[OUT_ROWS - cut :, :] for ref in late], axis=0
    )
    size = LOCAL * HELD
    for i in range(REQUESTS):
        for h in range(HELD):
            rows = pl.ds(pl.multiple_of((place_ref[i] + h * PER_GROUP) * ROWS, ROWS), ROWS)
            at = ((i % LOCAL) * HELD + h) * ROWS
            out_refs[i // LOCAL][at : at + ROWS, :] = all_ref[rows, :]
    wanted = line_ref[...] == iota((REQUESTS * HELD, sources.shape[0]), 1)
    lines = jnp.dot(wanted.astype(BF16), sources, preferred_element_type=F32).astype(BF16)
    for x in range(X):
        out_refs[x][size * ROWS :, :] = lines[x * size : (x + 1) * size]


def unpack(place, line, parts):
    vm = pl.BlockSpec(memory_space=pltpu.VMEM)
    return pl.pallas_call(
        unpack_kernel,
        out_shape=[jax.ShapeDtypeStruct((LOCAL * HELD * (ROWS + 1), HEAD_DIM), BF16)] * X,
        in_specs=[pl.BlockSpec(memory_space=pltpu.SMEM)] + [vm] * (1 + 2 * Y),
        out_specs=[vm] * X,
        scratch_shapes=[pltpu.VMEM((Y * OUT_ROWS, HEAD_DIM), BF16)],
        compiler_params=PARAMS,
        name="unpack_results",
    )(place, line, *parts)


def combine_kernel(x_ref, *refs):
    parts, (local_ref, stat_ref, out_ref, weight_ref) = refs[:X], refs[X:]
    wide = HELD * ROWS
    lane_head = iota((LOCAL, HEAD_DIM), 1) // ROWS
    heads = [lax.rem(x_ref[0] + (X - s), X) * HELD for s in range(X)]
    log_total = jnp.zeros((LOCAL, HEAD_DIM), F32)
    for s in range(X):
        pieces = parts[s][LOCAL * wide :, :].astype(F32)
        lines = pieces + pltpu.roll(pieces, HEAD_DIM - ROWS, 1)
        lines = lines + pltpu.roll(pieces, HEAD_DIM - 2 * ROWS, 1)
        for h in range(HELD):
            head = heads[s] + h
            line = pltpu.roll(lines[h * LOCAL : (h + 1) * LOCAL], head * ROWS, 1)
            log_total = jnp.where(lane_head == head, line, log_total)
    local_max = stat_ref[:LOCAL, :]
    highest = jnp.maximum(log_total, local_max)
    prefix_part = jnp.exp(log_total - highest)
    local_part = jnp.exp(local_max - highest)
    whole = prefix_part + local_part * stat_ref[LOCAL:, :]
    blank = jnp.zeros((HEAD_DIM - 2 * LOCAL, HEAD_DIM), F32)
    weight_ref[...] = jnp.concatenate([prefix_part / whole, local_part / whole, blank], axis=0).T
    for s in range(X):
        rows = pl.ds(pl.multiple_of(heads[s] * ROWS, wide), wide)
        weights = weight_ref[rows, :]
        for r in range(LOCAL):
            prefix = parts[s][r * wide : (r + 1) * wide, :].astype(F32)
            out = weights[:, r : r + 1] * prefix
            out = out + weights[:, LOCAL + r : LOCAL + r + 1] * local_ref[r, rows, :]
            out_ref[r, rows, :] = out.astype(BF16)


def combine(x, parts, local_out, stats):
    vm = pl.BlockSpec(memory_space=pltpu.VMEM)
    return pl.pallas_call(
        combine_kernel,
        out_shape=jax.ShapeDtypeStruct((LOCAL, HEADS * STEPS, HEAD_DIM), BF16),
        in_specs=[pl.BlockSpec(memory_space=pltpu.SMEM)] + [vm] * (X + 2),
        out_specs=vm,
        scratch_shapes=[pltpu.VMEM((HEAD_DIM, HEAD_DIM), F32)],
        compiler_params=PARAMS,
        name="combine_parts",
    )(x, *parts, local_out, stats)


def turn_x(value, turns):
    return lax.ppermute(value, "x", [(i, (i + turns) % X) for i in range(X)])


def shift(value, turns):
    return lax.ppermute(value, "y", [(i, (i + turns) % Y) for i in range(Y)])


def swap_cores(value):
    return lax.ppermute(value, "core", [(i, 1 - i) for i in range(CORES)])


def onward(value):
    pairs = []
    for z in range(Z):
        pairs.append((z * CORES, (z + 1) % Z * CORES))
        pairs.append((z * CORES + 1, (z - 1) % Z * CORES + 1))
    return lax.ppermute(value, ("z", "core"), pairs)


def per_device(
    queries,
    new_keys,
    new_values,
    suffix_keys,
    suffix_values,
    suffix_length,
    group_ids,
    prefix_keys,
    prefix_values,
    prefix_length,
):
    z = lax.axis_index("z")
    core = lax.axis_index("core")
    x = lax.axis_index("x")
    at_x = x.reshape(1).astype(jnp.int32)

    def head_rows(value):
        heads = value.shape[2] // HEAD_DIM
        value = value.reshape(LOCAL, STEPS, heads, HEAD_DIM).transpose(0, 2, 1, 3)
        return value.reshape(LOCAL, heads * STEPS, HEAD_DIM)

    splits = split(at_x, head_rows(queries))
    mine = build_cache(prefix_length, prefix_keys, prefix_values)
    arrived = [splits[0]] + [turn_x(splits[s], s) for s in range(1, X)]

    ids = group_ids[:, 0]
    ids = lax.dynamic_slice_in_dim(jnp.concatenate([ids, ids]), x * LOCAL, REQUESTS)
    index = jnp.arange(REQUESTS, dtype=jnp.int32)
    same = jnp.logical_and(ids[:, None] == ids[None, :], index[:, None] > index[None, :])
    position = jnp.sum(same, axis=1, dtype=jnp.int32)
    turn = ((ids // CORES) % Y - lax.axis_index("y") + Y) % Y
    foreign = (ids % CORES != core).astype(jnp.int32)
    ahead = ids // (CORES * Y) - z
    ahead = (jnp.where(core == 0, -ahead, ahead) + Z) % Z
    near = jnp.where(ahead < Z // 2, 4 * ahead - 2 + foreign, 4 * (Z - ahead) + 1 - foreign)
    arrival = jnp.where(
        ahead == 0, foreign, jnp.where(ahead == Z // 2, OWNED - 2 + foreign, near)
    )
    unit = arrival * (HELD * PER_GROUP) + position
    place = turn * (UNITS * PER_GROUP) + unit
    counts = (EARLY * HELD * PER_GROUP, (OWNED - EARLY) * HELD * PER_GROUP)
    late_line = Y * padded(counts[0]) + turn * padded(counts[1]) + unit - counts[0]
    line = jnp.where(arrival < EARLY, turn * padded(counts[0]) + unit, late_line)
    line = line.reshape(X, 1, LOCAL) + jnp.arange(HELD, dtype=jnp.int32)[:, None] * PER_GROUP
    line = line.reshape(REQUESTS * HELD, 1)

    packed = pack(place, [arrived[-s % X] for s in range(X)])
    received = [packed[0]] + [shift(packed[s], s) for s in range(1, Y)]

    pair_0 = stack([mine, swap_cores(mine)])
    pair_1 = onward(pair_0)
    pair_2 = onward(pair_1)
    pair_2, received[1], received[3] = lax.optimization_barrier((pair_2, received[1], received[3]))
    pair_3 = onward(pair_2)
    local_queries, received[1] = lax.optimization_barrier((head_rows(queries), received[1]))
    local_out, stats = attend_local(
        suffix_length,
        local_queries,
        suffix_keys,
        suffix_values,
        head_rows(new_keys),
        head_rows(new_values),
    )
    pair_3, local_out, stats, *received = lax.optimization_barrier(
        (pair_3, local_out, stats, *received)
    )
    pair_4 = onward(pair_3)
    early = attend_prefix(0, received, [pair_0, pair_1, swap_cores(pair_1), pair_2, swap_cores(pair_2)])
    late = attend_prefix(EARLY, received, [pair_3, swap_cores(pair_3), pair_4])
    parts = []
    for results in (early, late):
        parts += [results[0]] + [shift(results[s], -s) for s in range(1, Y)]

    pieces = unpack(place, line, parts)
    got = [pieces[0]] + [turn_x(pieces[s], s) for s in range(1, X)]
    out = combine(at_x, got, local_out, stats)
    out = out.reshape(LOCAL, HEADS, STEPS, HEAD_DIM).transpose(0, 2, 1, 3)
    return out.reshape(LOCAL, STEPS, HEADS * HEAD_DIM)


def solution(mesh):
    axes = ("z", "y", "core", "x")
    fine = Mesh(mesh.devices.reshape(Z, Y, CORES, X), axes)
    rows = P(axes, None, None)
    groups = ("z", "y", "core")
    placed = (rows,) * 5 + (
        P(axes),
        P(groups, None),
        P(groups, None, "x"),
        P(groups, None, "x"),
        P(groups),
    )
    return jax.shard_map(
        per_device, mesh=fine, in_specs=placed, out_specs=rows, check_vma=False
    )
```

time: 466 us -> 73.9 us (0.16); the launches traced: 459 us -> 73.7 us
  waiting for transfers between devices: 179 us -> 30.7 us
  blocking collectives: 109 us -> 0 us
  local copies, waits for them, and re-layouts: 88.6 us -> 5.11 us
  matrix products: 33.8 us -> 0 us
  Pallas kernels: 0 us -> 11.6 us
  other arithmetic: 10.9 us -> 0.44 us
  starting transfers between devices: 35.5 us -> 25.1 us
    all_to_all x5 -> x0, waiting for transfers between devices: 179 us -> none  [the longest x1 91.4 us: per_device(): lax.all_to_all(merged_out, 'ctx', split_axis=0, concat_axis=0, tiled=True)]
    all_to_all x1 -> x0, blocking collectives: 109 us -> none  [per_device(): lax.all_to_all(packed, 'ctx', split_axis=0, concat_axis=0, tiled=True)]
    reshape x14 -> x0, local copies, waits for them, and re-layouts: 52.9 us -> none  [the longest x2 14.1 us: per_device(): by_heads = arrived.reshape(owners, item_count, STEPS, splits, head_columns)]
    all_to_all x5 -> x0, starting transfers between devices: 35.5 us -> none  [the longest x1 10.8 us: per_device(): lax.all_to_all(merged_out, 'ctx', split_axis=0, concat_axis=0, tiled=True)]
    dot_general x8 -> x0, matrix products: 33.8 us -> none  [the longest x2 15.1 us: scores_of(): jnp.einsum('qkgd,jkd->qkgj', query_rows, shared_keys, preferred_element_t...]
    ppermute x0 -> x23, waiting for transfers between devices: none -> 30.7 us  [the longest x9 15.4 us: shift(): return lax.ppermute(value, 'y', [(i, (i + turns) % Y) for i in range(Y)])]
    ppermute x0 -> x23, starting transfers between devices: none -> 25.1 us  [the longest x9 14.9 us: shift(): return lax.ppermute(value, 'y', [(i, (i + turns) % Y) for i in range(Y)])]
    all_to_all x3 -> x0, local copies, waits for them, and re-layouts: 13.2 us -> none  [the longest x1 8.54 us: per_device(): lax.all_to_all(by_heads, 'batch', split_axis=3, concat_axis=0, tiled=True)]
  transfers between devices with their start and end apart: 5 -> 23, of which waited for: 3 -> 13; matrix products, arithmetic and copies ran while one was open for 9% -> 1% of each run, Pallas kernels for 0% -> 12%
where the time goes in v1:
time: 73.9 us; the launch traced here: 73.7 us
  waiting for transfers between devices  30.7 us (42%)
  starting transfers between devices  25.1 us (34%)
  Pallas kernels  11.6 us (16%)
  local copies, waits for them, and re-layouts  5.11 us (7%)
  between operations  0.81 us (1%)
    ppermute x9, waiting for transfers between devices, shift(): return lax.ppermute(value, 'y', [(i, (i + turns) % Y) for i in range(Y)])  15.4 us
    ppermute x9, starting transfers between devices, shift(): return lax.ppermute(value, 'y', [(i, (i + turns) % Y) for i in range(Y)])  14.9 us
    ppermute x4, waiting for transfers between devices, onward(): return lax.ppermute(value, ('z', 'core'), pairs)  8.19 us
    ppermute x6, starting transfers between devices, turn_x(): return lax.ppermute(value, 'x', [(i, (i + turns) % X) for i in range(X)])  7.09 us
    ppermute x6, waiting for transfers between devices, turn_x(): return lax.ppermute(value, 'x', [(i, (i + turns) % X) for i in range(X)])  5.52 us
    pallas_call x2, Pallas kernels, attend_prefix(): pl.pallas_call(functools.partial(prefix_kernel, first, count), out_shape=...  4.9 us
    unnamed x26, local copies, waits for them, and re-layouts  4.87 us
    pallas_call x1, Pallas kernels, attend_local(): pl.pallas_call(local_kernel, out_shape=(shape, jax.ShapeDtypeStruct((2 *...  2.79 us
  transfers between devices with their start and end apart: 23, of which 13 were waited for; matrix products, arithmetic and copies ran while one was open for 1% of the time, Pallas kernels for 12%

profile of v1, /device:TPU:6, one launch (start us, length us, event | category | flops | bytes accessed | tf_op | source)
XLA Modules:
  0.0 73.7 jit_solution(16144221694222784400)
XLA Ops:
  2.7 1.5 %collective-permute-done.refs_1_ = bf16[1040,128]{1,0:T(8,128)(2,1)S(1)} collective-permute-done((bf16[1040,128]{1,0:T(8,128)(2,1)S(1)}, bf16[1040,128]{1,0:T(8,128)(2,1)S(1)}, u32[]{:S(2)}, u32[]{:S(2)}) %collective-permute-start) | collective-permute-done | bytes 266272 | tf_op jit(solution)/shard_map/ppermute | solution.py:358
  4.3 2.0 %collective-permute-start.1 = (bf16[2080,128]{1,0:T(8,128)(2,1)S(1)}, bf16[2080,128]{1,0:T(8,128)(2,1)S(1)}, u32[]{:S(2)}, u32[]{:S(2)}) collective-permute-start(bf16[2080,128]{1,0:T(8,128)(2,1)S(1)} %stack_caches.1.refs_4_), channel_id=1, source_target_pairs={{0,32},{4,228},{32,64},{36,4},{64,96},{68,36},{96,128},{100,68},{1... | collective-permute-start | bytes 1597448 | tf_op jit(solution)/shard_map/ppermute | solution.py:366
  7.8 1.1 %collective-permute-start.4 = (bf16[256,128]{1,0:T(8,128)(2,1)S(1)}, bf16[256,128]{1,0:T(8,128)(2,1)S(1)}, u32[]{:S(2)}, u32[]{:S(2)}) collective-permute-start(bf16[256,128]{1,0:T(8,128)(2,1)S(1)} %get-tuple-element.41), channel_id=1, source_target_pairs={{0,2},{1,3},{2,0},{3,1},{4,6},{5,7},{6,4},{7,5},{8,10},{9,11},{10,... | collective-permute-start | bytes 196616 | tf_op jit(solution)/shard_map/ppermute | solution.py:350
  8.9 2.1 %collective-permute-start.5 = (bf16[256,128]{1,0:T(8,128)(2,1)S(1)}, bf16[256,128]{1,0:T(8,128)(2,1)S(1)}, u32[]{:S(2)}, u32[]{:S(2)}) collective-permute-start(bf16[256,128]{1,0:T(8,128)(2,1)S(1)} %get-tuple-element.42), channel_id=1, source_target_pairs={{0,1},{1,2},{2,3},{3,0},{4,5},{5,6},{6,7},{7,4},{8,9},{9,10},{10,1... | collective-permute-start | bytes 196616 | tf_op jit(solution)/shard_map/ppermute | solution.py:350
  11.4 6.1 %collective-permute-done.1.refs_5_ = bf16[2080,128]{1,0:T(8,128)(2,1)S(1)} collective-permute-done((bf16[2080,128]{1,0:T(8,128)(2,1)S(1)}, bf16[2080,128]{1,0:T(8,128)(2,1)S(1)}, u32[]{:S(2)}, u32[]{:S(2)}) %collective-permute-start.1) | collective-permute-done | bytes 532512 | tf_op jit(solution)/shard_map/ppermute | solution.py:366
  18.4 1.7 %collective-permute-start.6 = (bf16[1024,128]{1,0:T(8,128)(2,1)S(1)}, bf16[1024,128]{1,0:T(8,128)(2,1)S(1)}, u32[]{:S(2)}, u32[]{:S(2)}) collective-permute-start(bf16[1024,128]{1,0:T(8,128)(2,1)S(1)} %get-tuple-element.43), channel_id=1, source_target_pairs={{0,8},{8,16},{16,24},{24,0},{1,9},{9,17},{17,25},{25,1},{2,10},{10... | collective-permute-start | bytes 786440 | tf_op jit(solution)/shard_map/ppermute | solution.py:354
  20.1 1.7 %collective-permute-start.7 = (bf16[1024,128]{1,0:T(8,128)(2,1)S(1)}, bf16[1024,128]{1,0:T(8,128)(2,1)S(1)}, u32[]{:S(2)}, u32[]{:S(2)}) collective-permute-start(bf16[1024,128]{1,0:T(8,128)(2,1)S(1)} %get-tuple-element.44), channel_id=1, source_target_pairs={{0,24},{8,0},{16,8},{24,16},{1,25},{9,1},{17,9},{25,17},{2,26},{10... | collective-permute-start | bytes 786440 | tf_op jit(solution)/shard_map/ppermute | solution.py:354
  21.8 6.1 %collective-permute-done.6.refs_1_ = bf16[1024,128]{1,0:T(8,128)(2,1)S(1)} collective-permute-done((bf16[1024,128]{1,0:T(8,128)(2,1)S(1)}, bf16[1024,128]{1,0:T(8,128)(2,1)S(1)}, u32[]{:S(2)}, u32[]{:S(2)}) %collective-permute-start.6) | collective-permute-done | bytes 262176 | tf_op jit(solution)/shard_map/ppermute | solution.py:354
  28.6 2.9 %collective-permute-start.9 = (bf16[1024,128]{1,0:T(8,128)(2,1)S(1)}, bf16[1024,128]{1,0:T(8,128)(2,1)S(1)}, u32[]{:S(2)}, u32[]{:S(2)}) collective-permute-start(bf16[1024,128]{1,0:T(8,128)(2,1)S(1)} %get-tuple-element.52), channel_id=1, source_target_pairs={{0,16},{8,24},{16,0},{24,8},{1,17},{9,25},{17,1},{25,9},{2,18},{10... | collective-permute-start | bytes 786440 | tf_op jit(solution)/shard_map/ppermute | solution.py:354
  32.7 1.0 %copy-done.2 = bf16[8,32,1024]{2,1,0:T(8,128)(2,1)S(1)} copy-done((bf16[8,32,1024]{2,1,0:T(8,128)(2,1)S(1)}, bf16[8,32,1024]{2,1,0:T(8,128)(2,1)}, u32[]{:S(2)}) %copy-start.2) | copy-done | bytes 524312
  33.8 2.8 %local_attention.1 = (f32[8,128,128]{2,1,0:T(8,128)S(1)}, f32[16,128]{1,0:T(8,128)S(1)}) custom-call(s32[8]{0:T(128)S(1)} %copy-done.9, bf16[8,128,128]{2,1,0:T(8,128)(2,1)S(1)} %bitcast.23, bf16[8,32,1024]{2,1,0:T(8,128)(2,1)S(1)} %copy-done.1, bf16[8,32,1024]{2,1,0:T(8,128)(2,1)S(1)} %copy-done.2, bf16[8,16,128]{2,1,0:T(8,128)(2,1)S(1)} %bitcast.24, ...), custom_call_target="tpu_custom_call" | custom-call | tf_op jit(solution)/shard_map/local_attention/pallas_call | solution.py:88
  36.5 2.3 %collective-permute-done.9.refs_2_ = bf16[1024,128]{1,0:T(8,128)(2,1)S(1)} collective-permute-done((bf16[1024,128]{1,0:T(8,128)(2,1)S(1)}, bf16[1024,128]{1,0:T(8,128)(2,1)S(1)}, u32[]{:S(2)}, u32[]{:S(2)}) %collective-permute-start.9) | collective-permute-done | bytes 262176 | tf_op jit(solution)/shard_map/ppermute | solution.py:354
  39.6 2.5 %prefix_attention_0.1 = (bf16[688,128]{1,0:T(8,128)(2,1)S(1)}, bf16[688,128]{1,0:T(8,128)(2,1)}, bf16[688,128]{1,0:T(8,128)(2,1)S(1)}, bf16[688,128]{1,0:T(8,128)(2,1)S(1)}) custom-call(bf16[1024,128]{1,0:T(8,128)(2,1)S(1)} %get-tuple-element.54.refs_0_, bf16[1024,128]{1,0:T(8,128)(2,1)S(1)} %collective-permute-done.6.refs_1_, ...), custom_call_target="tpu_custom_call" | custom-call | tf_op jit(solution)/shard_map/prefix_attention_0/pallas_call | solution.py:259
  43.4 2.9 %collective-permute-start.12 = (bf16[688,128]{1,0:T(8,128)(2,1)}, bf16[688,128]{1,0:T(8,128)(2,1)S(1)}, u32[]{:S(2)}, u32[]{:S(2)}) collective-permute-start(bf16[688,128]{1,0:T(8,128)(2,1)} %get-tuple-element.59), channel_id=1, source_target_pairs={{0,24},{8,0},{16,8},{24,16},{1,25},{9,1},{17,9},{25,17},{2,26},{10... | collective-permute-start | bytes 528392 | tf_op jit(solution)/shard_map/ppermute | solution.py:354
  47.9 1.8 %collective-permute-done.16.refs_6_ = bf16[2080,128]{1,0:T(8,128)(2,1)} collective-permute-done((bf16[2080,128]{1,0:T(8,128)(2,1)S(1)}, bf16[2080,128]{1,0:T(8,128)(2,1)}, u32[]{:S(2)}, u32[]{:S(2)}) %collective-permute-start.16) | collective-permute-done | bytes 532512 | tf_op jit(solution)/shard_map/ppermute | solution.py:366
  49.7 2.4 %prefix_attention_10.1 = (bf16[416,128]{1,0:T(8,128)(2,1)S(1)}, bf16[416,128]{1,0:T(8,128)(2,1)S(1)}, bf16[416,128]{1,0:T(8,128)(2,1)S(1)}, bf16[416,128]{1,0:T(8,128)(2,1)S(1)}) custom-call(bf16[1024,128]{1,0:T(8,128)(2,1)S(1)} %get-tuple-element.54.refs_0_, bf16[1024,128]{1,0:T(8,128)(2,1)S(1)} %collective-permute-done.6.refs_1_, ...), custom_call_target="tpu_custom_call" | custom-call | tf_op jit(solution)/shard_map/prefix_attention_10/pallas_call | solution.py:259
  52.1 2.8 %collective-permute-start.17 = (bf16[416,128]{1,0:T(8,128)(2,1)S(1)}, bf16[416,128]{1,0:T(8,128)(2,1)S(1)}, u32[]{:S(2)}, u32[]{:S(2)}) collective-permute-start(bf16[416,128]{1,0:T(8,128)(2,1)S(1)} %get-tuple-element.64), channel_id=1, source_target_pairs={{0,24},{8,0},{16,8},{24,16},{1,25},{9,1},{17,9},{25,17},{2,26},{10... | collective-permute-start | bytes 319496 | tf_op jit(solution)/shard_map/ppermute | solution.py:354
  56.6 2.7 %collective-permute-done.14.refs_3_ = bf16[688,128]{1,0:T(8,128)(2,1)S(1)} collective-permute-done((bf16[688,128]{1,0:T(8,128)(2,1)}, bf16[688,128]{1,0:T(8,128)(2,1)S(1)}, u32[]{:S(2)}, u32[]{:S(2)}) %collective-permute-start.14) | collective-permute-done | bytes 176160 | tf_op jit(solution)/shard_map/ppermute | solution.py:354
  59.3 2.8 %collective-permute-done.18.refs_6_ = bf16[416,128]{1,0:T(8,128)(2,1)S(1)} collective-permute-done((bf16[416,128]{1,0:T(8,128)(2,1)S(1)}, bf16[416,128]{1,0:T(8,128)(2,1)S(1)}, u32[]{:S(2)}, u32[]{:S(2)}) %collective-permute-start.18) | collective-permute-done | bytes 106528 | tf_op jit(solution)/shard_map/ppermute | solution.py:354
  63.7 1.5 %collective-permute-start.20 = (bf16[272,128]{1,0:T(8,128)(2,1)S(1)}, bf16[272,128]{1,0:T(8,128)(2,1)S(1)}, u32[]{:S(2)}, u32[]{:S(2)}) collective-permute-start(bf16[272,128]{1,0:T(8,128)(2,1)S(1)} %get-tuple-element.68), channel_id=1, source_target_pairs={{0,1},{1,2},{2,3},{3,0},{4,5},{5,6},{6,7},{7,4},{8,9},{9,10},{10,1... | collective-permute-start | bytes 208904 | tf_op jit(solution)/shard_map/ppermute | solution.py:350
  65.2 1.5 %collective-permute-start.21 = (bf16[272,128]{1,0:T(8,128)(2,1)S(1)}, bf16[272,128]{1,0:T(8,128)(2,1)S(1)}, u32[]{:S(2)}, u32[]{:S(2)}) collective-permute-start(bf16[272,128]{1,0:T(8,128)(2,1)S(1)} %get-tuple-element.69), channel_id=1, source_target_pairs={{0,2},{1,3},{2,0},{3,1},{4,6},{5,7},{6,4},{7,5},{8,10},{9,11},{10,... | collective-permute-start | bytes 208904 | tf_op jit(solution)/shard_map/ppermute | solution.py:350
  66.7 1.7 %collective-permute-done.20.refs_1_ = bf16[272,128]{1,0:T(8,128)(2,1)S(1)} collective-permute-done((bf16[272,128]{1,0:T(8,128)(2,1)S(1)}, bf16[272,128]{1,0:T(8,128)(2,1)S(1)}, u32[]{:S(2)}, u32[]{:S(2)}) %collective-permute-start.20) | collective-permute-done | bytes 69664 | tf_op jit(solution)/shard_map/ppermute | solution.py:350
  68.3 2.9 %collective-permute-done.21.refs_2_ = bf16[272,128]{1,0:T(8,128)(2,1)S(1)} collective-permute-done((bf16[272,128]{1,0:T(8,128)(2,1)S(1)}, bf16[272,128]{1,0:T(8,128)(2,1)S(1)}, u32[]{:S(2)}, u32[]{:S(2)}) %collective-permute-start.21) | collective-permute-done | bytes 69664 | tf_op jit(solution)/shard_map/ppermute | solution.py:350
  72.2 1.5 %combine_parts.1 = bf16[8,128,128]{2,1,0:T(8,128)(2,1)} custom-call(s32[1]{0:T(128)} %bitcast.x_ref, bf16[272,128]{1,0:T(8,128)(2,1)S(1)} %get-tuple-element.67.refs_0_, bf16[272,128]{1,0:T(8,128)(2,1)S(1)} %collective-permute-done.20.refs_1_, bf16[272,128]{1,0:T(8,128)(2,1)S(1)} %collective-permute-done.21.refs_2_, ...), custom_call_target="tpu_custom_call" | custom-call | tf_op jit(solution)/shard_map/combine_parts/pallas_call | solution.py:338
  (66 shorter events, 14.7 us)
Async XLA Ops:
  2.6 1.6 %collective-permute-start = (bf16[1040,128]{1,0:T(8,128)(2,1)S(1)}, bf16[1040,128]{1,0:T(8,128)(2,1)S(1)}, u32[]{:S(2)}, u32[]{:S(2)}) collective-permute-start(bf16[1040,128]{1,0:T(8,128)(2,1)S(1)} %build_cache.1.refs_0_), channel_id=1, source_target_pairs={{0,4},{4,0},{1,5},{5,1},{2,6},{6,2},{3,7},{7,3},{8,12},{12,8},{9,1... | collective-permute-start | bytes 798728 | tf_op jit(solution)/shard_map/ppermute | solution.py:358
  4.2 27.8 %copy-start.1 = (bf16[8,32,1024]{2,1,0:T(8,128)(2,1)S(1)}, bf16[8,32,1024]{2,1,0:T(8,128)(2,1)}, u32[]{:S(2)}) copy-start(bf16[8,32,1024]{2,1,0:T(8,128)(2,1)} %sk_ref.1) | copy-start | bytes 1572868
  4.3 13.2 %collective-permute-start.1 = (bf16[2080,128]{1,0:T(8,128)(2,1)S(1)}, bf16[2080,128]{1,0:T(8,128)(2,1)S(1)}, u32[]{:S(2)}, u32[]{:S(2)}) collective-permute-start(bf16[2080,128]{1,0:T(8,128)(2,1)S(1)} %stack_caches.1.refs_4_), channel_id=1, source_target_pairs={{0,32},{4,228},{32,64},{36,4},{64,96},{68,36},{96,128},{100,68},{1... | collective-permute-start | bytes 1597448 | tf_op jit(solution)/shard_map/ppermute | solution.py:366
  6.9 10.6 %collective-permute-start.3 = (bf16[256,128]{1,0:T(8,128)(2,1)S(1)}, bf16[256,128]{1,0:T(8,128)(2,1)S(1)}, u32[]{:S(2)}, u32[]{:S(2)}) collective-permute-start(bf16[256,128]{1,0:T(8,128)(2,1)S(1)} %get-tuple-element.40), channel_id=1, source_target_pairs={{0,3},{1,0},{2,1},{3,2},{4,7},{5,4},{6,5},{7,6},{8,11},{9,8},{10,9... | collective-permute-start | bytes 196616 | tf_op jit(solution)/shard_map/ppermute | solution.py:350
  7.8 9.7 %collective-permute-start.4 = (bf16[256,128]{1,0:T(8,128)(2,1)S(1)}, bf16[256,128]{1,0:T(8,128)(2,1)S(1)}, u32[]{:S(2)}, u32[]{:S(2)}) collective-permute-start(bf16[256,128]{1,0:T(8,128)(2,1)S(1)} %get-tuple-element.41), channel_id=1, source_target_pairs={{0,2},{1,3},{2,0},{3,1},{4,6},{5,7},{6,4},{7,5},{8,10},{9,11},{10,... | collective-permute-start | bytes 196616 | tf_op jit(solution)/shard_map/ppermute | solution.py:350
  8.9 8.6 %collective-permute-start.5 = (bf16[256,128]{1,0:T(8,128)(2,1)S(1)}, bf16[256,128]{1,0:T(8,128)(2,1)S(1)}, u32[]{:S(2)}, u32[]{:S(2)}) collective-permute-start(bf16[256,128]{1,0:T(8,128)(2,1)S(1)} %get-tuple-element.42), channel_id=1, source_target_pairs={{0,1},{1,2},{2,3},{3,0},{4,5},{5,6},{6,7},{7,4},{8,9},{9,10},{10,1... | collective-permute-start | bytes 196616 | tf_op jit(solution)/shard_map/ppermute | solution.py:350
  17.4 11.2 %collective-permute-start.2 = (bf16[2080,128]{1,0:T(8,128)(2,1)S(1)}, bf16[2080,128]{1,0:T(8,128)(2,1)S(1)}, u32[]{:S(2)}, u32[]{:S(2)}) collective-permute-start(bf16[2080,128]{1,0:T(8,128)(2,1)S(1)} %collective-permute-done.1.refs_5_), channel_id=1, source_target_pairs={{0,32},{4,228},{32,64},{36,4},{64,96},{68,36},{96,128},{100,68},{1... | collective-permute-start | bytes 1597448 | tf_op jit(solution)/shard_map/ppermute | solution.py:366
  18.4 9.4 %collective-permute-start.6 = (bf16[1024,128]{1,0:T(8,128)(2,1)S(1)}, bf16[1024,128]{1,0:T(8,128)(2,1)S(1)}, u32[]{:S(2)}, u32[]{:S(2)}) collective-permute-start(bf16[1024,128]{1,0:T(8,128)(2,1)S(1)} %get-tuple-element.43), channel_id=1, source_target_pairs={{0,8},{8,16},{16,24},{24,0},{1,9},{9,17},{17,25},{25,1},{2,10},{10... | collective-permute-start | bytes 786440 | tf_op jit(solution)/shard_map/ppermute | solution.py:354
  20.1 8.5 %collective-permute-start.7 = (bf16[1024,128]{1,0:T(8,128)(2,1)S(1)}, bf16[1024,128]{1,0:T(8,128)(2,1)S(1)}, u32[]{:S(2)}, u32[]{:S(2)}) collective-permute-start(bf16[1024,128]{1,0:T(8,128)(2,1)S(1)} %get-tuple-element.44), channel_id=1, source_target_pairs={{0,24},{8,0},{16,8},{24,16},{1,25},{9,1},{17,9},{25,17},{2,26},{10... | collective-permute-start | bytes 786440 | tf_op jit(solution)/shard_map/ppermute | solution.py:354
  28.6 10.5 %collective-permute-start.8 = (bf16[2080,128]{1,0:T(8,128)(2,1)S(1)}, bf16[2080,128]{1,0:T(8,128)(2,1)S(1)}, u32[]{:S(2)}, u32[]{:S(2)}) collective-permute-start(bf16[2080,128]{1,0:T(8,128)(2,1)S(1)} %collective-permute-done.2.refs_7_), channel_id=1, source_target_pairs={{0,32},{4,228},{32,64},{36,4},{64,96},{68,36},{96,128},{100,68},{1... | collective-permute-start | bytes 1597448 | tf_op jit(solution)/shard_map/ppermute | solution.py:366
  28.6 10.2 %collective-permute-start.9 = (bf16[1024,128]{1,0:T(8,128)(2,1)S(1)}, bf16[1024,128]{1,0:T(8,128)(2,1)S(1)}, u32[]{:S(2)}, u32[]{:S(2)}) collective-permute-start(bf16[1024,128]{1,0:T(8,128)(2,1)S(1)} %get-tuple-element.52), channel_id=1, source_target_pairs={{0,16},{8,24},{16,0},{24,8},{1,17},{9,25},{17,1},{25,9},{2,18},{10... | collective-permute-start | bytes 786440 | tf_op jit(solution)/shard_map/ppermute | solution.py:354
  31.5 8.0 %collective-permute-start.10 = (bf16[2080,128]{1,0:T(8,128)(2,1)S(1)}, bf16[2080,128]{1,0:T(8,128)(2,1)S(1)}, u32[]{:S(2)}, u32[]{:S(2)}) collective-permute-start(bf16[2080,128]{1,0:T(8,128)(2,1)S(1)} %collective-permute-done.1.refs_5_), channel_id=1, source_target_pairs={{0,4},{4,0},{1,5},{5,1},{2,6},{6,2},{3,7},{7,3},{8,12},{12,8},{9,1... | collective-permute-start | bytes 1597448 | tf_op jit(solution)/shard_map/ppermute | solution.py:358
  31.7 7.8 %collective-permute-start.11 = (bf16[2080,128]{1,0:T(8,128)(2,1)S(1)}, bf16[2080,128]{1,0:T(8,128)(2,1)S(1)}, u32[]{:S(2)}, u32[]{:S(2)}) collective-permute-start(bf16[2080,128]{1,0:T(8,128)(2,1)S(1)} %collective-permute-done.2.refs_7_), channel_id=1, source_target_pairs={{0,4},{4,0},{1,5},{5,1},{2,6},{6,2},{3,7},{7,3},{8,12},{12,8},{9,1... | collective-permute-start | bytes 1597448 | tf_op jit(solution)/shard_map/ppermute | solution.py:358
  39.1 8.8 %collective-permute-start.15 = (bf16[2080,128]{1,0:T(8,128)(2,1)S(1)}, bf16[2080,128]{1,0:T(8,128)(2,1)S(1)}, u32[]{:S(2)}, u32[]{:S(2)}) collective-permute-start(bf16[2080,128]{1,0:T(8,128)(2,1)S(1)} %collective-permute-done.8.refs_4_), channel_id=1, source_target_pairs={{0,4},{4,0},{1,5},{5,1},{2,6},{6,2},{3,7},{7,3},{8,12},{12,8},{9,1... | collective-permute-start | bytes 1597448 | tf_op jit(solution)/shard_map/ppermute | solution.py:358
  39.1 10.6 %collective-permute-start.16 = (bf16[2080,128]{1,0:T(8,128)(2,1)S(1)}, bf16[2080,128]{1,0:T(8,128)(2,1)}, u32[]{:S(2)}, u32[]{:S(2)}) collective-permute-start(bf16[2080,128]{1,0:T(8,128)(2,1)S(1)} %collective-permute-done.8.refs_4_), channel_id=1, source_target_pairs={{0,32},{4,228},{32,64},{36,4},{64,96},{68,36},{96,128},{100,68},{1... | collective-permute-start | bytes 1597448 | tf_op jit(solution)/shard_map/ppermute | solution.py:366
  43.4 12.4 %collective-permute-start.12 = (bf16[688,128]{1,0:T(8,128)(2,1)}, bf16[688,128]{1,0:T(8,128)(2,1)S(1)}, u32[]{:S(2)}, u32[]{:S(2)}) collective-permute-start(bf16[688,128]{1,0:T(8,128)(2,1)} %get-tuple-element.59), channel_id=1, source_target_pairs={{0,24},{8,0},{16,8},{24,16},{1,25},{9,1},{17,9},{25,17},{2,26},{10... | collective-permute-start | bytes 528392 | tf_op jit(solution)/shard_map/ppermute | solution.py:354
  46.4 10.2 %collective-permute-start.13 = (bf16[688,128]{1,0:T(8,128)(2,1)}, bf16[688,128]{1,0:T(8,128)(2,1)S(1)}, u32[]{:S(2)}, u32[]{:S(2)}) collective-permute-start(bf16[688,128]{1,0:T(8,128)(2,1)} %copy-done.11), channel_id=1, source_target_pairs={{0,16},{8,24},{16,0},{24,8},{1,17},{9,25},{17,1},{25,9},{2,18},{10... | collective-permute-start | bytes 528392 | tf_op jit(solution)/shard_map/ppermute | solution.py:354
  47.2 12.1 %collective-permute-start.14 = (bf16[688,128]{1,0:T(8,128)(2,1)}, bf16[688,128]{1,0:T(8,128)(2,1)S(1)}, u32[]{:S(2)}, u32[]{:S(2)}) collective-permute-start(bf16[688,128]{1,0:T(8,128)(2,1)} %copy-done.10), channel_id=1, source_target_pairs={{0,8},{8,16},{16,24},{24,0},{1,9},{9,17},{17,25},{25,1},{2,10},{10... | collective-permute-start | bytes 528392 | tf_op jit(solution)/shard_map/ppermute | solution.py:354
  52.1 7.3 %collective-permute-start.17 = (bf16[416,128]{1,0:T(8,128)(2,1)S(1)}, bf16[416,128]{1,0:T(8,128)(2,1)S(1)}, u32[]{:S(2)}, u32[]{:S(2)}) collective-permute-start(bf16[416,128]{1,0:T(8,128)(2,1)S(1)} %get-tuple-element.64), channel_id=1, source_target_pairs={{0,24},{8,0},{16,8},{24,16},{1,25},{9,1},{17,9},{25,17},{2,26},{10... | collective-permute-start | bytes 319496 | tf_op jit(solution)/shard_map/ppermute | solution.py:354
  54.9 7.2 %collective-permute-start.18 = (bf16[416,128]{1,0:T(8,128)(2,1)S(1)}, bf16[416,128]{1,0:T(8,128)(2,1)S(1)}, u32[]{:S(2)}, u32[]{:S(2)}) collective-permute-start(bf16[416,128]{1,0:T(8,128)(2,1)S(1)} %get-tuple-element.65), channel_id=1, source_target_pairs={{0,16},{8,24},{16,0},{24,8},{1,17},{9,25},{17,1},{25,9},{2,18},{10... | collective-permute-start | bytes 319496 | tf_op jit(solution)/shard_map/ppermute | solution.py:354
  55.8 7.1 %collective-permute-start.19 = (bf16[416,128]{1,0:T(8,128)(2,1)S(1)}, bf16[416,128]{1,0:T(8,128)(2,1)S(1)}, u32[]{:S(2)}, u32[]{:S(2)}) collective-permute-start(bf16[416,128]{1,0:T(8,128)(2,1)S(1)} %get-tuple-element.66), channel_id=1, source_target_pairs={{0,8},{8,16},{16,24},{24,0},{1,9},{9,17},{17,25},{25,1},{2,10},{10... | collective-permute-start | bytes 319496 | tf_op jit(solution)/shard_map/ppermute | solution.py:354
  63.7 4.6 %collective-permute-start.20 = (bf16[272,128]{1,0:T(8,128)(2,1)S(1)}, bf16[272,128]{1,0:T(8,128)(2,1)S(1)}, u32[]{:S(2)}, u32[]{:S(2)}) collective-permute-start(bf16[272,128]{1,0:T(8,128)(2,1)S(1)} %get-tuple-element.68), channel_id=1, source_target_pairs={{0,1},{1,2},{2,3},{3,0},{4,5},{5,6},{6,7},{7,4},{8,9},{9,10},{10,1... | collective-permute-start | bytes 208904 | tf_op jit(solution)/shard_map/ppermute | solution.py:350
  65.2 6.1 %collective-permute-start.21 = (bf16[272,128]{1,0:T(8,128)(2,1)S(1)}, bf16[272,128]{1,0:T(8,128)(2,1)S(1)}, u32[]{:S(2)}, u32[]{:S(2)}) collective-permute-start(bf16[272,128]{1,0:T(8,128)(2,1)S(1)} %get-tuple-element.69), channel_id=1, source_target_pairs={{0,2},{1,3},{2,0},{3,1},{4,6},{5,7},{6,4},{7,5},{8,10},{9,11},{10,... | collective-permute-start | bytes 208904 | tf_op jit(solution)/shard_map/ppermute | solution.py:350
  66.7 5.5 %collective-permute-start.22 = (bf16[272,128]{1,0:T(8,128)(2,1)S(1)}, bf16[272,128]{1,0:T(8,128)(2,1)S(1)}, u32[]{:S(2)}, u32[]{:S(2)}) collective-permute-start(bf16[272,128]{1,0:T(8,128)(2,1)S(1)} %get-tuple-element.70), channel_id=1, source_target_pairs={{0,3},{1,0},{2,1},{3,2},{4,7},{5,4},{6,5},{7,6},{8,11},{9,8},{10,9... | collective-permute-start | bytes 208904 | tf_op jit(solution)/shard_map/ppermute | solution.py:350
  (12 other events, 59.2 us)

commit v2 on v1

--- a/solution.py
+++ b/solution.py
@@ -388,7 +388,7 @@
         value = value.reshape(LOCAL, STEPS, heads, HEAD_DIM).transpose(0, 2, 1, 3)
         return value.reshape(LOCAL, heads * STEPS, HEAD_DIM)
 
-    splits = split(at_x, head_rows(queries))
+    splits = list(split(at_x, head_rows(queries)))
     mine = build_cache(prefix_length, prefix_keys, prefix_values)
     arrived = [splits[0]] + [turn_x(splits[s], s) for s in range(1, X)]
 
@@ -418,10 +418,7 @@
 
     pair_0 = stack([mine, swap_cores(mine)])
     pair_1 = onward(pair_0)
-    pair_2 = onward(pair_1)
-    pair_2, received[1], received[3] = lax.optimization_barrier((pair_2, received[1], received[3]))
-    pair_3 = onward(pair_2)
-    local_queries, received[1] = lax.optimization_barrier((head_rows(queries), received[1]))
+    local_queries, splits[0] = lax.optimization_barrier((head_rows(queries), splits[0]))
     local_out, stats = attend_local(
         suffix_length,
         local_queries,
@@ -430,9 +427,11 @@
         head_rows(new_keys),
         head_rows(new_values),
     )
-    pair_3, local_out, stats, *received = lax.optimization_barrier(
-        (pair_3, local_out, stats, *received)
-    )
+    pair_1, local_out, stats = lax.optimization_barrier((pair_1, local_out, stats))
+    pair_2 = onward(pair_1)
+    pair_2, received[1], received[3] = lax.optimization_barrier((pair_2, received[1], received[3]))
+    pair_3 = onward(pair_2)
+    pair_3, *received = lax.optimization_barrier((pair_3, *received))
     pair_4 = onward(pair_3)
     early = attend_prefix(0, received, [pair_0, pair_1, swap_cores(pair_1), pair_2, swap_cores(pair_2)])
     late = attend_prefix(EARLY, received, [pair_3, swap_cores(pair_3), pair_4])

time: 73.9 us -> 73.7 us (level)
  starting transfers between devices: 25.1 us -> 29.1 us
  waiting for transfers between devices: 30.7 us -> 27.4 us
  local copies, waits for them, and re-layouts: 5.11 us -> 4.19 us
    ppermute x4, waiting for transfers between devices: 8.19 us -> 3.59 us  [onward(): return lax.ppermute(value, ('z', 'core'), pairs)]
    ppermute x4, starting transfers between devices: 2.42 us -> 5.57 us  [onward(): return lax.ppermute(value, ('z', 'core'), pairs)]
    ppermute x9, waiting for transfers between devices: 15.4 us -> 18 us  [shift(): return lax.ppermute(value, 'y', [(i, (i + turns) % Y) for i in range(Y)])]
    ppermute x6, waiting for transfers between devices: 5.52 us -> 4.21 us  [turn_x(): return lax.ppermute(value, 'x', [(i, (i + turns) % X) for i in range(X)])]
    ppermute x6, starting transfers between devices: 7.09 us -> 8.1 us  [turn_x(): return lax.ppermute(value, 'x', [(i, (i + turns) % X) for i in range(X)])]
    unnamed x26 -> x24, local copies, waits for them, and re-layouts: 4.87 us -> 3.95 us
  transfers between devices with their start and end apart: 23 -> 23, of which waited for: 13 -> 13; matrix products, arithmetic and copies ran while one was open for 1% -> 1% of each run, Pallas kernels for 12% -> 13%
where the time goes in v2:
time: 73.7 us; the launch traced here: 73.5 us
  starting transfers between devices  29.1 us (39%)
  waiting for transfers between devices  27.4 us (37%)
  Pallas kernels  11.6 us (16%)
  local copies, waits for them, and re-layouts  4.19 us (6%)
  between operations  0.82 us (1%)
    ppermute x9, waiting for transfers between devices, shift(): return lax.ppermute(value, 'y', [(i, (i + turns) % Y) for i in range(Y)])  18 us
    ppermute x9, starting transfers between devices, shift(): return lax.ppermute(value, 'y', [(i, (i + turns) % Y) for i in range(Y)])  14.8 us
    ppermute x6, starting transfers between devices, turn_x(): return lax.ppermute(value, 'x', [(i, (i + turns) % X) for i in range(X)])  8.1 us
    ppermute x4, starting transfers between devices, onward(): return lax.ppermute(value, ('z', 'core'), pairs)  5.57 us
    pallas_call x2, Pallas kernels, attend_prefix(): pl.pallas_call(functools.partial(prefix_kernel, first, count), out_shape=...  4.91 us
    ppermute x6, waiting for transfers between devices, turn_x(): return lax.ppermute(value, 'x', [(i, (i + turns) % X) for i in range(X)])  4.21 us
    unnamed x24, local copies, waits for them, and re-layouts  3.95 us
    ppermute x4, waiting for transfers between devices, onward(): return lax.ppermute(value, ('z', 'core'), pairs)  3.59 us
  transfers between devices with their start and end apart: 23, of which 13 were waited for; matrix products, arithmetic and copies ran while one was open for 1% of the time, Pallas kernels for 13%

profile of v2, /device:TPU:6, one launch (start us, length us, event | category | flops | bytes accessed | tf_op | source)
XLA Modules:
  0.0 73.5 jit_solution(10691082096375403945)
XLA Ops:
  2.7 1.5 %collective-permute-done.refs_1_ = bf16[1040,128]{1,0:T(8,128)(2,1)S(1)} collective-permute-done((bf16[1040,128]{1,0:T(8,128)(2,1)S(1)}, bf16[1040,128]{1,0:T(8,128)(2,1)S(1)}, u32[]{:S(2)}, u32[]{:S(2)}) %collective-permute-start) | collective-permute-done | bytes 266272 | tf_op jit(solution)/shard_map/ppermute | solution.py:358
  4.3 2.0 %collective-permute-start.1 = (bf16[2080,128]{1,0:T(8,128)(2,1)S(1)}, bf16[2080,128]{1,0:T(8,128)(2,1)S(1)}, u32[]{:S(2)}, u32[]{:S(2)}) collective-permute-start(bf16[2080,128]{1,0:T(8,128)(2,1)S(1)} %stack_caches.1.refs_4_), channel_id=1, source_target_pairs={{0,32},{4,228},{32,64},{36,4},{64,96},{68,36},{96,128},{100,68},{1... | collective-permute-start | bytes 1597448 | tf_op jit(solution)/shard_map/ppermute | solution.py:366
  9.0 2.1 %collective-permute-start.5 = (bf16[256,128]{1,0:T(8,128)(2,1)S(1)}, bf16[256,128]{1,0:T(8,128)(2,1)S(1)}, u32[]{:S(2)}, u32[]{:S(2)}) collective-permute-start(bf16[256,128]{1,0:T(8,128)(2,1)S(1)} %get-tuple-element.46), channel_id=1, source_target_pairs={{0,1},{1,2},{2,3},{3,0},{4,5},{5,6},{6,7},{7,4},{8,9},{9,10},{10,1... | collective-permute-start | bytes 196616 | tf_op jit(solution)/shard_map/ppermute | solution.py:350
  11.9 2.8 %local_attention.1 = (f32[8,128,128]{2,1,0:T(8,128)S(1)}, f32[16,128]{1,0:T(8,128)S(1)}) custom-call(s32[8]{0:T(128)S(1)} %copy-done.9, bf16[8,128,128]{2,1,0:T(8,128)(2,1)S(1)} %bitcast.23, bf16[8,32,1024]{2,1,0:T(8,128)(2,1)S(1)} %copy-done.1, bf16[8,32,1024]{2,1,0:T(8,128)(2,1)S(1)} %copy-done.2, bf16[8,16,128]{2,1,0:T(8,128)(2,1)S(1)} %bitcast.24, ...), custom_call_target="tpu_custom_call" | custom-call | tf_op jit(solution)/shard_map/local_attention/pallas_call | solution.py:88
  15.7 1.8 %collective-permute-done.1.refs_5_ = bf16[2080,128]{1,0:T(8,128)(2,1)S(1)} collective-permute-done((bf16[2080,128]{1,0:T(8,128)(2,1)S(1)}, bf16[2080,128]{1,0:T(8,128)(2,1)S(1)}, u32[]{:S(2)}, u32[]{:S(2)}) %collective-permute-start.1) | collective-permute-done | bytes 532512 | tf_op jit(solution)/shard_map/ppermute | solution.py:366
  18.7 1.7 %collective-permute-start.6 = (bf16[1024,128]{1,0:T(8,128)(2,1)S(1)}, bf16[1024,128]{1,0:T(8,128)(2,1)S(1)}, u32[]{:S(2)}, u32[]{:S(2)}) collective-permute-start(bf16[1024,128]{1,0:T(8,128)(2,1)S(1)} %get-tuple-element.47), channel_id=1, source_target_pairs={{0,8},{8,16},{16,24},{24,0},{1,9},{9,17},{17,25},{25,1},{2,10},{10... | collective-permute-start | bytes 786440 | tf_op jit(solution)/shard_map/ppermute | solution.py:354
  20.3 1.7 %collective-permute-start.7 = (bf16[1024,128]{1,0:T(8,128)(2,1)S(1)}, bf16[1024,128]{1,0:T(8,128)(2,1)S(1)}, u32[]{:S(2)}, u32[]{:S(2)}) collective-permute-start(bf16[1024,128]{1,0:T(8,128)(2,1)S(1)} %get-tuple-element.48), channel_id=1, source_target_pairs={{0,24},{8,0},{16,8},{24,16},{1,25},{9,1},{17,9},{25,17},{2,26},{10... | collective-permute-start | bytes 786440 | tf_op jit(solution)/shard_map/ppermute | solution.py:354
  22.0 6.3 %collective-permute-done.6.refs_1_ = bf16[1024,128]{1,0:T(8,128)(2,1)S(1)} collective-permute-done((bf16[1024,128]{1,0:T(8,128)(2,1)S(1)}, bf16[1024,128]{1,0:T(8,128)(2,1)S(1)}, u32[]{:S(2)}, u32[]{:S(2)}) %collective-permute-start.6) | collective-permute-done | bytes 262176 | tf_op jit(solution)/shard_map/ppermute | solution.py:354
  29.1 2.0 %collective-permute-start.8 = (bf16[2080,128]{1,0:T(8,128)(2,1)S(1)}, bf16[2080,128]{1,0:T(8,128)(2,1)S(1)}, u32[]{:S(2)}, u32[]{:S(2)}) collective-permute-start(bf16[2080,128]{1,0:T(8,128)(2,1)S(1)} %collective-permute-done.2.refs_7_), channel_id=1, source_target_pairs={{0,32},{4,228},{32,64},{36,4},{64,96},{68,36},{96,128},{100,68},{1... | collective-permute-start | bytes 1597448 | tf_op jit(solution)/shard_map/ppermute | solution.py:366
  31.0 2.9 %collective-permute-start.9 = (bf16[1024,128]{1,0:T(8,128)(2,1)S(1)}, bf16[1024,128]{1,0:T(8,128)(2,1)S(1)}, u32[]{:S(2)}, u32[]{:S(2)}) collective-permute-start(bf16[1024,128]{1,0:T(8,128)(2,1)S(1)} %get-tuple-element.52), channel_id=1, source_target_pairs={{0,16},{8,24},{16,0},{24,8},{1,17},{9,25},{17,1},{25,9},{2,18},{10... | collective-permute-start | bytes 786440 | tf_op jit(solution)/shard_map/ppermute | solution.py:354
  34.4 5.0 %collective-permute-done.9.refs_2_ = bf16[1024,128]{1,0:T(8,128)(2,1)S(1)} collective-permute-done((bf16[1024,128]{1,0:T(8,128)(2,1)S(1)}, bf16[1024,128]{1,0:T(8,128)(2,1)S(1)}, u32[]{:S(2)}, u32[]{:S(2)}) %collective-permute-start.9) | collective-permute-done | bytes 262176 | tf_op jit(solution)/shard_map/ppermute | solution.py:354
  39.5 1.4 %collective-permute-start.16 = (bf16[2080,128]{1,0:T(8,128)(2,1)S(1)}, bf16[2080,128]{1,0:T(8,128)(2,1)}, u32[]{:S(2)}, u32[]{:S(2)}) collective-permute-start(bf16[2080,128]{1,0:T(8,128)(2,1)S(1)} %collective-permute-done.8.refs_4_), channel_id=1, source_target_pairs={{0,32},{4,228},{32,64},{36,4},{64,96},{68,36},{96,128},{100,68},{1... | collective-permute-start | bytes 1597448 | tf_op jit(solution)/shard_map/ppermute | solution.py:366
  40.9 2.5 %prefix_attention_0.1 = (bf16[688,128]{1,0:T(8,128)(2,1)S(1)}, bf16[688,128]{1,0:T(8,128)(2,1)}, bf16[688,128]{1,0:T(8,128)(2,1)S(1)}, bf16[688,128]{1,0:T(8,128)(2,1)S(1)}) custom-call(bf16[1024,128]{1,0:T(8,128)(2,1)S(1)} %get-tuple-element.54.refs_0_, bf16[1024,128]{1,0:T(8,128)(2,1)S(1)} %collective-permute-done.6.refs_1_, ...), custom_call_target="tpu_custom_call" | custom-call | tf_op jit(solution)/shard_map/prefix_attention_0/pallas_call | solution.py:259
  44.1 2.8 %collective-permute-start.12 = (bf16[688,128]{1,0:T(8,128)(2,1)}, bf16[688,128]{1,0:T(8,128)(2,1)S(1)}, u32[]{:S(2)}, u32[]{:S(2)}) collective-permute-start(bf16[688,128]{1,0:T(8,128)(2,1)} %get-tuple-element.59), channel_id=1, source_target_pairs={{0,24},{8,0},{16,8},{24,16},{1,25},{9,1},{17,9},{25,17},{2,26},{10... | collective-permute-start | bytes 528392 | tf_op jit(solution)/shard_map/ppermute | solution.py:354
  48.4 1.7 %collective-permute-done.16.refs_6_ = bf16[2080,128]{1,0:T(8,128)(2,1)} collective-permute-done((bf16[2080,128]{1,0:T(8,128)(2,1)S(1)}, bf16[2080,128]{1,0:T(8,128)(2,1)}, u32[]{:S(2)}, u32[]{:S(2)}) %collective-permute-start.16) | collective-permute-done | bytes 532512 | tf_op jit(solution)/shard_map/ppermute | solution.py:366
  50.1 2.4 %prefix_attention_10.1 = (bf16[416,128]{1,0:T(8,128)(2,1)S(1)}, bf16[416,128]{1,0:T(8,128)(2,1)S(1)}, bf16[416,128]{1,0:T(8,128)(2,1)S(1)}, bf16[416,128]{1,0:T(8,128)(2,1)S(1)}) custom-call(bf16[1024,128]{1,0:T(8,128)(2,1)S(1)} %get-tuple-element.54.refs_0_, bf16[1024,128]{1,0:T(8,128)(2,1)S(1)} %collective-permute-done.6.refs_1_, ...), custom_call_target="tpu_custom_call" | custom-call | tf_op jit(solution)/shard_map/prefix_attention_10/pallas_call | solution.py:259
  52.5 2.8 %collective-permute-start.17 = (bf16[416,128]{1,0:T(8,128)(2,1)S(1)}, bf16[416,128]{1,0:T(8,128)(2,1)S(1)}, u32[]{:S(2)}, u32[]{:S(2)}) collective-permute-start(bf16[416,128]{1,0:T(8,128)(2,1)S(1)} %get-tuple-element.64), channel_id=1, source_target_pairs={{0,24},{8,0},{16,8},{24,16},{1,25},{9,1},{17,9},{25,17},{2,26},{10... | collective-permute-start | bytes 319496 | tf_op jit(solution)/shard_map/ppermute | solution.py:354
  57.0 2.4 %collective-permute-done.14.refs_3_ = bf16[688,128]{1,0:T(8,128)(2,1)S(1)} collective-permute-done((bf16[688,128]{1,0:T(8,128)(2,1)S(1)}, bf16[688,128]{1,0:T(8,128)(2,1)S(1)}, u32[]{:S(2)}, u32[]{:S(2)}) %collective-permute-start.14) | collective-permute-done | bytes 176160 | tf_op jit(solution)/shard_map/ppermute | solution.py:354
  59.4 2.5 %collective-permute-done.18.refs_6_ = bf16[416,128]{1,0:T(8,128)(2,1)S(1)} collective-permute-done((bf16[416,128]{1,0:T(8,128)(2,1)S(1)}, bf16[416,128]{1,0:T(8,128)(2,1)S(1)}, u32[]{:S(2)}, u32[]{:S(2)}) %collective-permute-start.18) | collective-permute-done | bytes 106528 | tf_op jit(solution)/shard_map/ppermute | solution.py:354
  63.8 1.3 %collective-permute-start.20 = (bf16[272,128]{1,0:T(8,128)(2,1)S(1)}, bf16[272,128]{1,0:T(8,128)(2,1)S(1)}, u32[]{:S(2)}, u32[]{:S(2)}) collective-permute-start(bf16[272,128]{1,0:T(8,128)(2,1)S(1)} %get-tuple-element.68), channel_id=1, source_target_pairs={{0,1},{1,2},{2,3},{3,0},{4,5},{5,6},{6,7},{7,4},{8,9},{9,10},{10,1... | collective-permute-start | bytes 208904 | tf_op jit(solution)/shard_map/ppermute | solution.py:350
  65.1 1.4 %collective-permute-start.21 = (bf16[272,128]{1,0:T(8,128)(2,1)S(1)}, bf16[272,128]{1,0:T(8,128)(2,1)S(1)}, u32[]{:S(2)}, u32[]{:S(2)}) collective-permute-start(bf16[272,128]{1,0:T(8,128)(2,1)S(1)} %get-tuple-element.69), channel_id=1, source_target_pairs={{0,2},{1,3},{2,0},{3,1},{4,6},{5,7},{6,4},{7,5},{8,10},{9,11},{10,... | collective-permute-start | bytes 208904 | tf_op jit(solution)/shard_map/ppermute | solution.py:350
  66.5 1.3 %collective-permute-start.22 = (bf16[272,128]{1,0:T(8,128)(2,1)S(1)}, bf16[272,128]{1,0:T(8,128)(2,1)S(1)}, u32[]{:S(2)}, u32[]{:S(2)}) collective-permute-start(bf16[272,128]{1,0:T(8,128)(2,1)S(1)} %get-tuple-element.70), channel_id=1, source_target_pairs={{0,3},{1,0},{2,1},{3,2},{4,7},{5,4},{6,5},{7,6},{8,11},{9,8},{10,9... | collective-permute-start | bytes 208904 | tf_op jit(solution)/shard_map/ppermute | solution.py:350
  68.2 2.7 %collective-permute-done.21.refs_2_ = bf16[272,128]{1,0:T(8,128)(2,1)S(1)} collective-permute-done((bf16[272,128]{1,0:T(8,128)(2,1)S(1)}, bf16[272,128]{1,0:T(8,128)(2,1)S(1)}, u32[]{:S(2)}, u32[]{:S(2)}) %collective-permute-start.21) | collective-permute-done | bytes 69664 | tf_op jit(solution)/shard_map/ppermute | solution.py:350
  72.0 1.5 %combine_parts.1 = bf16[8,128,128]{2,1,0:T(8,128)(2,1)} custom-call(s32[1]{0:T(128)} %bitcast.x_ref, bf16[272,128]{1,0:T(8,128)(2,1)S(1)} %get-tuple-element.67.refs_0_, bf16[272,128]{1,0:T(8,128)(2,1)S(1)} %collective-permute-done.20.refs_1_, bf16[272,128]{1,0:T(8,128)(2,1)S(1)} %collective-permute-done.21.refs_2_, ...), custom_call_target="tpu_custom_call" | custom-call | tf_op jit(solution)/shard_map/combine_parts/pallas_call | solution.py:338
  (64 shorter events, 16.5 us)
Async XLA Ops:
  2.6 1.6 %collective-permute-start = (bf16[1040,128]{1,0:T(8,128)(2,1)S(1)}, bf16[1040,128]{1,0:T(8,128)(2,1)S(1)}, u32[]{:S(2)}, u32[]{:S(2)}) collective-permute-start(bf16[1040,128]{1,0:T(8,128)(2,1)S(1)} %build_cache.1.refs_0_), channel_id=1, source_target_pairs={{0,4},{4,0},{1,5},{5,1},{2,6},{6,2},{3,7},{7,3},{8,12},{12,8},{9,1... | collective-permute-start | bytes 798728 | tf_op jit(solution)/shard_map/ppermute | solution.py:358
  4.3 13.2 %collective-permute-start.1 = (bf16[2080,128]{1,0:T(8,128)(2,1)S(1)}, bf16[2080,128]{1,0:T(8,128)(2,1)S(1)}, u32[]{:S(2)}, u32[]{:S(2)}) collective-permute-start(bf16[2080,128]{1,0:T(8,128)(2,1)S(1)} %stack_caches.1.refs_4_), channel_id=1, source_target_pairs={{0,32},{4,228},{32,64},{36,4},{64,96},{68,36},{96,128},{100,68},{1... | collective-permute-start | bytes 1597448 | tf_op jit(solution)/shard_map/ppermute | solution.py:366
  7.0 10.8 %collective-permute-start.3 = (bf16[256,128]{1,0:T(8,128)(2,1)S(1)}, bf16[256,128]{1,0:T(8,128)(2,1)S(1)}, u32[]{:S(2)}, u32[]{:S(2)}) collective-permute-start(bf16[256,128]{1,0:T(8,128)(2,1)S(1)} %get-tuple-element.44), channel_id=1, source_target_pairs={{0,3},{1,0},{2,1},{3,2},{4,7},{5,4},{6,5},{7,6},{8,11},{9,8},{10,9... | collective-permute-start | bytes 196616 | tf_op jit(solution)/shard_map/ppermute | solution.py:350
  7.9 9.9 %collective-permute-start.4 = (bf16[256,128]{1,0:T(8,128)(2,1)S(1)}, bf16[256,128]{1,0:T(8,128)(2,1)S(1)}, u32[]{:S(2)}, u32[]{:S(2)}) collective-permute-start(bf16[256,128]{1,0:T(8,128)(2,1)S(1)} %get-tuple-element.45), channel_id=1, source_target_pairs={{0,2},{1,3},{2,0},{3,1},{4,6},{5,7},{6,4},{7,5},{8,10},{9,11},{10,... | collective-permute-start | bytes 196616 | tf_op jit(solution)/shard_map/ppermute | solution.py:350
  9.0 8.8 %collective-permute-start.5 = (bf16[256,128]{1,0:T(8,128)(2,1)S(1)}, bf16[256,128]{1,0:T(8,128)(2,1)S(1)}, u32[]{:S(2)}, u32[]{:S(2)}) collective-permute-start(bf16[256,128]{1,0:T(8,128)(2,1)S(1)} %get-tuple-element.46), channel_id=1, source_target_pairs={{0,1},{1,2},{2,3},{3,0},{4,5},{5,6},{6,7},{7,4},{8,9},{9,10},{10,1... | collective-permute-start | bytes 196616 | tf_op jit(solution)/shard_map/ppermute | solution.py:350
  17.4 11.6 %collective-permute-start.2 = (bf16[2080,128]{1,0:T(8,128)(2,1)S(1)}, bf16[2080,128]{1,0:T(8,128)(2,1)S(1)}, u32[]{:S(2)}, u32[]{:S(2)}) collective-permute-start(bf16[2080,128]{1,0:T(8,128)(2,1)S(1)} %collective-permute-done.1.refs_5_), channel_id=1, source_target_pairs={{0,32},{4,228},{32,64},{36,4},{64,96},{68,36},{96,128},{100,68},{1... | collective-permute-start | bytes 1597448 | tf_op jit(solution)/shard_map/ppermute | solution.py:366
  18.7 9.6 %collective-permute-start.6 = (bf16[1024,128]{1,0:T(8,128)(2,1)S(1)}, bf16[1024,128]{1,0:T(8,128)(2,1)S(1)}, u32[]{:S(2)}, u32[]{:S(2)}) collective-permute-start(bf16[1024,128]{1,0:T(8,128)(2,1)S(1)} %get-tuple-element.47), channel_id=1, source_target_pairs={{0,8},{8,16},{16,24},{24,0},{1,9},{9,17},{17,25},{25,1},{2,10},{10... | collective-permute-start | bytes 786440 | tf_op jit(solution)/shard_map/ppermute | solution.py:354
  20.3 8.7 %collective-permute-start.7 = (bf16[1024,128]{1,0:T(8,128)(2,1)S(1)}, bf16[1024,128]{1,0:T(8,128)(2,1)S(1)}, u32[]{:S(2)}, u32[]{:S(2)}) collective-permute-start(bf16[1024,128]{1,0:T(8,128)(2,1)S(1)} %get-tuple-element.48), channel_id=1, source_target_pairs={{0,24},{8,0},{16,8},{24,16},{1,25},{9,1},{17,9},{25,17},{2,26},{10... | collective-permute-start | bytes 786440 | tf_op jit(solution)/shard_map/ppermute | solution.py:354
  29.1 10.5 %collective-permute-start.8 = (bf16[2080,128]{1,0:T(8,128)(2,1)S(1)}, bf16[2080,128]{1,0:T(8,128)(2,1)S(1)}, u32[]{:S(2)}, u32[]{:S(2)}) collective-permute-start(bf16[2080,128]{1,0:T(8,128)(2,1)S(1)} %collective-permute-done.2.refs_7_), channel_id=1, source_target_pairs={{0,32},{4,228},{32,64},{36,4},{64,96},{68,36},{96,128},{100,68},{1... | collective-permute-start | bytes 1597448 | tf_op jit(solution)/shard_map/ppermute | solution.py:366
  31.0 8.4 %collective-permute-start.9 = (bf16[1024,128]{1,0:T(8,128)(2,1)S(1)}, bf16[1024,128]{1,0:T(8,128)(2,1)S(1)}, u32[]{:S(2)}, u32[]{:S(2)}) collective-permute-start(bf16[1024,128]{1,0:T(8,128)(2,1)S(1)} %get-tuple-element.52), channel_id=1, source_target_pairs={{0,16},{8,24},{16,0},{24,8},{1,17},{9,25},{17,1},{25,9},{2,18},{10... | collective-permute-start | bytes 786440 | tf_op jit(solution)/shard_map/ppermute | solution.py:354
  33.9 7.0 %collective-permute-start.10 = (bf16[2080,128]{1,0:T(8,128)(2,1)S(1)}, bf16[2080,128]{1,0:T(8,128)(2,1)S(1)}, u32[]{:S(2)}, u32[]{:S(2)}) collective-permute-start(bf16[2080,128]{1,0:T(8,128)(2,1)S(1)} %collective-permute-done.1.refs_5_), channel_id=1, source_target_pairs={{0,4},{4,0},{1,5},{5,1},{2,6},{6,2},{3,7},{7,3},{8,12},{12,8},{9,1... | collective-permute-start | bytes 1597448 | tf_op jit(solution)/shard_map/ppermute | solution.py:358
  33.9 7.0 %collective-permute-start.11 = (bf16[2080,128]{1,0:T(8,128)(2,1)S(1)}, bf16[2080,128]{1,0:T(8,128)(2,1)S(1)}, u32[]{:S(2)}, u32[]{:S(2)}) collective-permute-start(bf16[2080,128]{1,0:T(8,128)(2,1)S(1)} %collective-permute-done.2.refs_7_), channel_id=1, source_target_pairs={{0,4},{4,0},{1,5},{5,1},{2,6},{6,2},{3,7},{7,3},{8,12},{12,8},{9,1... | collective-permute-start | bytes 1597448 | tf_op jit(solution)/shard_map/ppermute | solution.py:358
  39.5 8.9 %collective-permute-start.15 = (bf16[2080,128]{1,0:T(8,128)(2,1)S(1)}, bf16[2080,128]{1,0:T(8,128)(2,1)S(1)}, u32[]{:S(2)}, u32[]{:S(2)}) collective-permute-start(bf16[2080,128]{1,0:T(8,128)(2,1)S(1)} %collective-permute-done.8.refs_4_), channel_id=1, source_target_pairs={{0,4},{4,0},{1,5},{5,1},{2,6},{6,2},{3,7},{7,3},{8,12},{12,8},{9,1... | collective-permute-start | bytes 1597448 | tf_op jit(solution)/shard_map/ppermute | solution.py:358
  39.5 10.6 %collective-permute-start.16 = (bf16[2080,128]{1,0:T(8,128)(2,1)S(1)}, bf16[2080,128]{1,0:T(8,128)(2,1)}, u32[]{:S(2)}, u32[]{:S(2)}) collective-permute-start(bf16[2080,128]{1,0:T(8,128)(2,1)S(1)} %collective-permute-done.8.refs_4_), channel_id=1, source_target_pairs={{0,32},{4,228},{32,64},{36,4},{64,96},{68,36},{96,128},{100,68},{1... | collective-permute-start | bytes 1597448 | tf_op jit(solution)/shard_map/ppermute | solution.py:366
  44.1 12.1 %collective-permute-start.12 = (bf16[688,128]{1,0:T(8,128)(2,1)}, bf16[688,128]{1,0:T(8,128)(2,1)S(1)}, u32[]{:S(2)}, u32[]{:S(2)}) collective-permute-start(bf16[688,128]{1,0:T(8,128)(2,1)} %get-tuple-element.59), channel_id=1, source_target_pairs={{0,24},{8,0},{16,8},{24,16},{1,25},{9,1},{17,9},{25,17},{2,26},{10... | collective-permute-start | bytes 528392 | tf_op jit(solution)/shard_map/ppermute | solution.py:354
  47.0 10.1 %collective-permute-start.13 = (bf16[688,128]{1,0:T(8,128)(2,1)}, bf16[688,128]{1,0:T(8,128)(2,1)S(1)}, u32[]{:S(2)}, u32[]{:S(2)}) collective-permute-start(bf16[688,128]{1,0:T(8,128)(2,1)} %copy-done.10), channel_id=1, source_target_pairs={{0,16},{8,24},{16,0},{24,8},{1,17},{9,25},{17,1},{25,9},{2,18},{10... | collective-permute-start | bytes 528392 | tf_op jit(solution)/shard_map/ppermute | solution.py:354
  47.8 11.7 %collective-permute-start.14 = (bf16[688,128]{1,0:T(8,128)(2,1)S(1)}, bf16[688,128]{1,0:T(8,128)(2,1)S(1)}, u32[]{:S(2)}, u32[]{:S(2)}) collective-permute-start(bf16[688,128]{1,0:T(8,128)(2,1)S(1)} %get-tuple-element.61), channel_id=1, source_target_pairs={{0,8},{8,16},{16,24},{24,0},{1,9},{9,17},{17,25},{25,1},{2,10},{10... | collective-permute-start | bytes 528392 | tf_op jit(solution)/shard_map/ppermute | solution.py:354
  52.5 6.9 %collective-permute-start.17 = (bf16[416,128]{1,0:T(8,128)(2,1)S(1)}, bf16[416,128]{1,0:T(8,128)(2,1)S(1)}, u32[]{:S(2)}, u32[]{:S(2)}) collective-permute-start(bf16[416,128]{1,0:T(8,128)(2,1)S(1)} %get-tuple-element.64), channel_id=1, source_target_pairs={{0,24},{8,0},{16,8},{24,16},{1,25},{9,1},{17,9},{25,17},{2,26},{10... | collective-permute-start | bytes 319496 | tf_op jit(solution)/shard_map/ppermute | solution.py:354
  55.3 6.7 %collective-permute-start.18 = (bf16[416,128]{1,0:T(8,128)(2,1)S(1)}, bf16[416,128]{1,0:T(8,128)(2,1)S(1)}, u32[]{:S(2)}, u32[]{:S(2)}) collective-permute-start(bf16[416,128]{1,0:T(8,128)(2,1)S(1)} %get-tuple-element.65), channel_id=1, source_target_pairs={{0,16},{8,24},{16,0},{24,8},{1,17},{9,25},{17,1},{25,9},{2,18},{10... | collective-permute-start | bytes 319496 | tf_op jit(solution)/shard_map/ppermute | solution.py:354
  56.2 6.8 %collective-permute-start.19 = (bf16[416,128]{1,0:T(8,128)(2,1)S(1)}, bf16[416,128]{1,0:T(8,128)(2,1)S(1)}, u32[]{:S(2)}, u32[]{:S(2)}) collective-permute-start(bf16[416,128]{1,0:T(8,128)(2,1)S(1)} %get-tuple-element.66), channel_id=1, source_target_pairs={{0,8},{8,16},{16,24},{24,0},{1,9},{9,17},{17,25},{25,1},{2,10},{10... | collective-permute-start | bytes 319496 | tf_op jit(solution)/shard_map/ppermute | solution.py:354
  63.0 9.0 %copy-start.4 = (f32[8,128,128]{2,1,0:T(8,128)S(1)}, f32[8,128,128]{2,1,0:T(8,128)}, u32[]{:S(2)}) copy-start(f32[8,128,128]{2,1,0:T(8,128)} %copy-done.3) | copy-start | bytes 1572868
  63.8 4.4 %collective-permute-start.20 = (bf16[272,128]{1,0:T(8,128)(2,1)S(1)}, bf16[272,128]{1,0:T(8,128)(2,1)S(1)}, u32[]{:S(2)}, u32[]{:S(2)}) collective-permute-start(bf16[272,128]{1,0:T(8,128)(2,1)S(1)} %get-tuple-element.68), channel_id=1, source_target_pairs={{0,1},{1,2},{2,3},{3,0},{4,5},{5,6},{6,7},{7,4},{8,9},{9,10},{10,1... | collective-permute-start | bytes 208904 | tf_op jit(solution)/shard_map/ppermute | solution.py:350
  65.1 5.8 %collective-permute-start.21 = (bf16[272,128]{1,0:T(8,128)(2,1)S(1)}, bf16[272,128]{1,0:T(8,128)(2,1)S(1)}, u32[]{:S(2)}, u32[]{:S(2)}) collective-permute-start(bf16[272,128]{1,0:T(8,128)(2,1)S(1)} %get-tuple-element.69), channel_id=1, source_target_pairs={{0,2},{1,3},{2,0},{3,1},{4,6},{5,7},{6,4},{7,5},{8,10},{9,11},{10,... | collective-permute-start | bytes 208904 | tf_op jit(solution)/shard_map/ppermute | solution.py:350
  66.5 5.5 %collective-permute-start.22 = (bf16[272,128]{1,0:T(8,128)(2,1)S(1)}, bf16[272,128]{1,0:T(8,128)(2,1)S(1)}, u32[]{:S(2)}, u32[]{:S(2)}) collective-permute-start(bf16[272,128]{1,0:T(8,128)(2,1)S(1)} %get-tuple-element.70), channel_id=1, source_target_pairs={{0,3},{1,0},{2,1},{3,2},{4,7},{5,4},{6,5},{7,6},{8,11},{9,8},{10,9... | collective-permute-start | bytes 208904 | tf_op jit(solution)/shard_map/ppermute | solution.py:350
  (11 other events, 39.1 us)

commit v3 on v1

--- a/solution.py
+++ b/solution.py
@@ -18,21 +18,21 @@
 ROWS = GROUP * STEPS
 FACTOR = 1.0 / math.sqrt(HEAD_DIM)
 Z, Y, CORES, X = 8, 4, 2, 4
+PEERS = CORES * X
 LOCAL = 8
+COLUMN = PEERS * LOCAL
 HELD = KV_HEADS // X
-OWNED = Z * CORES
-EARLY = 10
-PER_GROUP = 2
-REQUESTS = X * LOCAL
+OWNED = Z
+EARLY = 5
+PER_GROUP = 4
 BLOCK = PER_GROUP * ROWS
 UNITS = OWNED * HELD
 OUT_ROWS = UNITS * BLOCK
+DUMP = Y * OUT_ROWS // ROWS
 CACHE_ROWS = 2 * HELD * PREFIX_MAX
-CACHE_BLOCK = CACHE_ROWS + 16
 F32 = jnp.float32
 BF16 = jnp.bfloat16
-PARAMS = pltpu.CompilerParams(vmem_limit_bytes=10 * 1024 * 1024)
-STAGING = pltpu.CompilerParams(vmem_limit_bytes=32 * 1024 * 1024)
+PARAMS = pltpu.CompilerParams(vmem_limit_bytes=32 * 1024 * 1024)
 
 
 def padded(count):
@@ -120,15 +120,15 @@
     return pl.pallas_call(
         split_kernel,
         out_shape=[part] * X,
-        in_specs=[pl.BlockSpec(memory_space=pltpu.SMEM), pl.BlockSpec(memory_space=pltpu.HBM)],
+        in_specs=[pl.BlockSpec(memory_space=pltpu.SMEM), pl.BlockSpec(memory_space=pl.ANY)],
         out_specs=[pl.BlockSpec(memory_space=pltpu.VMEM)] * X,
         scratch_shapes=[pltpu.SemaphoreType.DMA((X, LOCAL))],
-        compiler_params=STAGING,
+        compiler_params=PARAMS,
         name="split_queries",
     )(x, q)
 
 
-def cache_kernel(length_ref, k_ref, v_ref, cache_ref, sems):
+def cache_kernel(length_ref, k_ref, v_ref, after_ref, cache_ref, sems):
     copies = []
     for i, ref in enumerate((k_ref, v_ref)):
         for h in range(HELD):
@@ -148,17 +148,17 @@
         copy.wait()
 
 
-def build_cache(length, keys, values):
-    hbm = pl.BlockSpec(memory_space=pltpu.HBM)
+def build_cache(length, keys, values, after):
+    anywhere = pl.BlockSpec(memory_space=pl.ANY)
     return pl.pallas_call(
         cache_kernel,
         out_shape=jax.ShapeDtypeStruct((CACHE_ROWS + 16, HEAD_DIM), BF16),
-        in_specs=[pl.BlockSpec(memory_space=pltpu.SMEM)] + [hbm] * 2,
+        in_specs=[pl.BlockSpec(memory_space=pltpu.SMEM)] + [anywhere] * 3,
         out_specs=pl.BlockSpec(memory_space=pltpu.VMEM),
         scratch_shapes=[pltpu.SemaphoreType.DMA((2, HELD))],
-        compiler_params=STAGING,
+        compiler_params=PARAMS,
         name="build_cache",
-    )(length, keys, values)
+    )(length, keys, values, after)
 
 
 def stack_kernel(*refs):
@@ -177,55 +177,54 @@
         in_specs=[vm] * len(parts),
         out_specs=vm,
         compiler_params=PARAMS,
-        name="stack_caches",
+        name="stack_queries",
     )(*parts)
 
 
-def pack_kernel(place_ref, *refs):
-    q_refs, out_refs, packed_ref = refs[:X], refs[X : X + Y], refs[X + Y]
+def pack_kernel(place_ref, own_ref, other_ref, *out_refs):
+    packed_ref = out_refs[Y]
     packed_ref[...] = jnp.zeros(packed_ref.shape, BF16)
-    for i in range(REQUESTS):
+    half = COLUMN // CORES
+    for i in range(COLUMN):
+        q_ref = own_ref if i < half else other_ref
         for h in range(HELD):
             start = pl.multiple_of((place_ref[i] + h * PER_GROUP) * ROWS, ROWS)
-            at = ((i % LOCAL) * HELD + h) * ROWS
-            packed_ref[pl.ds(start, ROWS), :] = q_refs[i // LOCAL][at : at + ROWS, :]
+            at = ((i % half) * HELD + h) * ROWS
+            packed_ref[pl.ds(start, ROWS), :] = q_ref[at : at + ROWS, :]
     for s in range(Y):
         out_refs[s][...] = packed_ref[s * OUT_ROWS : (s + 1) * OUT_ROWS, :]
 
 
-def pack(place, queries):
+def pack(place, own, other):
     vm = pl.BlockSpec(memory_space=pltpu.VMEM)
     return pl.pallas_call(
         pack_kernel,
         out_shape=[jax.ShapeDtypeStruct((OUT_ROWS, HEAD_DIM), BF16)] * Y,
-        in_specs=[pl.BlockSpec(memory_space=pltpu.SMEM)] + [vm] * X,
+        in_specs=[pl.BlockSpec(memory_space=pltpu.SMEM), vm, vm],
         out_specs=[vm] * Y,
-        scratch_shapes=[pltpu.VMEM((Y * OUT_ROWS, HEAD_DIM), BF16)],
+        scratch_shapes=[pltpu.VMEM((Y * OUT_ROWS + 2 * BLOCK, HEAD_DIM), BF16)],
         compiler_params=PARAMS,
         name="pack_queries",
-    )(place, *queries)
+    )(place, own, other)
 
 
 def prefix_kernel(first, count, *refs):
-    q_refs, caches, out_refs = refs[:Y], refs[Y:-Y], refs[-Y:]
+    q_refs, caches, out_refs = refs[:Y], refs[Y : Y + count], refs[Y + count :]
     column = iota((1, PREFIX_MAX), 1).astype(F32)
     lane = iota((Y * BLOCK, HEAD_DIM), 1)
     diagonal = lane % ROWS == iota((Y * BLOCK, HEAD_DIM), 0) % ROWS
     piece = iota((Y * PER_GROUP, HEAD_DIM), 1) // ROWS
     lines = []
     for j in range(count):
-        cache, base = caches[j // CORES], j % CORES * CACHE_BLOCK
-        length = cache[base + CACHE_ROWS : base + CACHE_BLOCK, :].astype(F32)[:1, :1]
+        length = caches[j][CACHE_ROWS:, :].astype(F32)[:1, :1]
         usable = column < length
         for h in range(HELD):
             unit = (first + j) * HELD + h
             q = jnp.concatenate(
                 [ref[unit * BLOCK : (unit + 1) * BLOCK, :] for ref in q_refs], axis=0
             )
-            at = base + h * PREFIX_MAX
-            keys = cache[at : at + PREFIX_MAX, :]
-            at += HELD * PREFIX_MAX
-            values = cache[at : at + PREFIX_MAX, :]
+            keys = caches[j][h * PREFIX_MAX : (h + 1) * PREFIX_MAX, :]
+            values = caches[j][(HELD + h) * PREFIX_MAX : (HELD + h + 1) * PREFIX_MAX, :]
             scores = jnp.where(usable, dot_t(q, keys) * FACTOR, -jnp.inf)
             highest = jnp.max(scores, axis=1, keepdims=True)
             weights = jnp.exp(scores - highest)
@@ -252,54 +251,89 @@
 
 
 def attend_prefix(first, queries, caches):
-    count = len(caches) * CORES
+    count = len(caches)
     units = count * HELD
     rows = units * BLOCK + padded(units * PER_GROUP)
     vm = pl.BlockSpec(memory_space=pltpu.VMEM)
     return pl.pallas_call(
         functools.partial(prefix_kernel, first, count),
         out_shape=[jax.ShapeDtypeStruct((rows, HEAD_DIM), BF16)] * Y,
-        in_specs=[vm] * (Y + len(caches)),
+        in_specs=[vm] * (Y + count),
         out_specs=[vm] * Y,
         compiler_params=PARAMS,
         name="prefix_attention_%d" % first,
     )(*queries, *caches)
 
 
+PIECE = LOCAL * HELD * (ROWS + 1)
+
+
 def unpack_kernel(place_ref, line_ref, *refs):
     early, late = refs[:Y], refs[Y : 2 * Y]
-    out_refs, all_ref = refs[2 * Y : 2 * Y + X], refs[2 * Y + X]
-    cut = EARLY * HELD * BLOCK
+    own_ref, other_ref, all_ref = refs[2 * Y :]
     for s in range(Y):
         base = s * OUT_ROWS
+        cut = EARLY * HELD * BLOCK
         all_ref[base : base + cut, :] = early[s][:cut, :]
         all_ref[base + cut : base + OUT_ROWS, :] = late[s][: OUT_ROWS - cut, :]
     sources = jnp.concatenate(
-        [ref[cut:, :] for ref in early] + [ref[OUT_ROWS - cut :, :] for ref in late], axis=0
+        [ref[EARLY * HELD * BLOCK :, :] for ref in early]
+        + [ref[(OWNED - EARLY) * HELD * BLOCK :, :] for ref in late],
+        axis=0,
     )
+    half = COLUMN // CORES
     size = LOCAL * HELD
-    for i in range(REQUESTS):
+    for i in range(COLUMN):
+        out_ref = own_ref if i < half else other_ref
+        base = (i % half) // LOCAL * PIECE
         for h in range(HELD):
             rows = pl.ds(pl.multiple_of((place_ref[i] + h * PER_GROUP) * ROWS, ROWS), ROWS)
-            at = ((i % LOCAL) * HELD + h) * ROWS
-            out_refs[i // LOCAL][at : at + ROWS, :] = all_ref[rows, :]
-    wanted = line_ref[...] == iota((REQUESTS * HELD, sources.shape[0]), 1)
+            at = base + ((i % LOCAL) * HELD + h) * ROWS
+            out_ref[at : at + ROWS, :] = all_ref[rows, :]
+    wanted = line_ref[...] == iota((COLUMN * HELD, sources.shape[0]), 1)
     lines = jnp.dot(wanted.astype(BF16), sources, preferred_element_type=F32).astype(BF16)
-    for x in range(X):
-        out_refs[x][size * ROWS :, :] = lines[x * size : (x + 1) * size]
+    for i, out_ref in enumerate((own_ref, other_ref)):
+        for x in range(X):
+            at = (i * X + x) * size
+            out_ref[x * PIECE + size * ROWS : (x + 1) * PIECE, :] = lines[at : at + size]
 
 
 def unpack(place, line, parts):
     vm = pl.BlockSpec(memory_space=pltpu.VMEM)
     return pl.pallas_call(
         unpack_kernel,
-        out_shape=[jax.ShapeDtypeStruct((LOCAL * HELD * (ROWS + 1), HEAD_DIM), BF16)] * X,
+        out_shape=[jax.ShapeDtypeStruct((X * PIECE, HEAD_DIM), BF16)] * CORES,
         in_specs=[pl.BlockSpec(memory_space=pltpu.SMEM)] + [vm] * (1 + 2 * Y),
-        out_specs=[vm] * X,
+        out_specs=[vm] * CORES,
         scratch_shapes=[pltpu.VMEM((Y * OUT_ROWS, HEAD_DIM), BF16)],
         compiler_params=PARAMS,
         name="unpack_results",
     )(place, line, *parts)
+
+
+def merge_kernel(ours_ref, own_ref, got_ref, *out_refs):
+    wide = HELD * ROWS
+    for x in range(X):
+        for r in range(LOCAL):
+            rows = slice(x * PIECE + r * wide, x * PIECE + (r + 1) * wide)
+            mine = ours_ref[x * LOCAL + r] == 1
+            out_refs[x][r * wide : (r + 1) * wide, :] = jnp.where(
+                mine, own_ref[rows, :], got_ref[rows, :]
+            )
+        rows = slice(x * PIECE + LOCAL * wide, (x + 1) * PIECE)
+        out_refs[x][LOCAL * wide :, :] = own_ref[rows, :] + got_ref[rows, :]
+
+
+def merge(ours, own, got):
+    vm = pl.BlockSpec(memory_space=pltpu.VMEM)
+    return pl.pallas_call(
+        merge_kernel,
+        out_shape=[jax.ShapeDtypeStruct((PIECE, HEAD_DIM), BF16)] * X,
+        in_specs=[pl.BlockSpec(memory_space=pltpu.SMEM), vm, vm],
+        out_specs=[vm] * X,
+        compiler_params=PARAMS,
+        name="merge_cores",
+    )(ours, own, got)
 
 
 def combine_kernel(x_ref, *refs):
@@ -389,58 +423,62 @@
         return value.reshape(LOCAL, heads * STEPS, HEAD_DIM)
 
     splits = split(at_x, head_rows(queries))
-    mine = build_cache(prefix_length, prefix_keys, prefix_values)
+    mine = build_cache(prefix_length, prefix_keys, prefix_values, splits[0])
     arrived = [splits[0]] + [turn_x(splits[s], s) for s in range(1, X)]
-
-    ids = group_ids[:, 0]
-    ids = lax.dynamic_slice_in_dim(jnp.concatenate([ids, ids]), x * LOCAL, REQUESTS)
-    index = jnp.arange(REQUESTS, dtype=jnp.int32)
-    same = jnp.logical_and(ids[:, None] == ids[None, :], index[:, None] > index[None, :])
-    position = jnp.sum(same, axis=1, dtype=jnp.int32)
+    own_queries = stack([arrived[-s % X] for s in range(X)])
+
+    block_ids = group_ids[:, 0]
+    ids = jnp.stack([block_ids, swap_cores(block_ids)])
+    ids = lax.dynamic_slice_in_dim(
+        jnp.concatenate([ids, ids], axis=1), x * LOCAL, X * LOCAL, axis=1
+    ).reshape(COLUMN)
+    index = jnp.arange(COLUMN, dtype=jnp.int32)
+    block = index // (X * LOCAL)
+    same = jnp.logical_and(ids[:, None] == ids[None, :], block[:, None] == block[None, :])
+    position = jnp.sum(
+        jnp.logical_and(same, index[:, None] > index[None, :]), axis=1, dtype=jnp.int32
+    )
     turn = ((ids // CORES) % Y - lax.axis_index("y") + Y) % Y
-    foreign = (ids % CORES != core).astype(jnp.int32)
-    ahead = ids // (CORES * Y) - z
-    ahead = (jnp.where(core == 0, -ahead, ahead) + Z) % Z
-    near = jnp.where(ahead < Z // 2, 4 * ahead - 2 + foreign, 4 * (Z - ahead) + 1 - foreign)
-    arrival = jnp.where(
-        ahead == 0, foreign, jnp.where(ahead == Z // 2, OWNED - 2 + foreign, near)
-    )
-    unit = arrival * (HELD * PER_GROUP) + position
+    owner_core = ids % CORES
+    ahead = (ids // (CORES * Y) - z + Z) % Z
+    half = Z // 2
+    side = jnp.where(ahead % half == 0, owner_core, (ahead < half).astype(jnp.int32))
+    steps = jnp.where(ahead > half, Z - ahead, ahead)
+    arrival = jnp.where(steps == 0, 0, 2 * steps - (owner_core == side).astype(jnp.int32))
+    slot = block * (PER_GROUP // CORES) + position
+    unit = arrival * (HELD * PER_GROUP) + slot
     place = turn * (UNITS * PER_GROUP) + unit
+    ours = side == core
     counts = (EARLY * HELD * PER_GROUP, (OWNED - EARLY) * HELD * PER_GROUP)
     late_line = Y * padded(counts[0]) + turn * padded(counts[1]) + unit - counts[0]
     line = jnp.where(arrival < EARLY, turn * padded(counts[0]) + unit, late_line)
-    line = line.reshape(X, 1, LOCAL) + jnp.arange(HELD, dtype=jnp.int32)[:, None] * PER_GROUP
-    line = line.reshape(REQUESTS * HELD, 1)
-
-    packed = pack(place, [arrived[-s % X] for s in range(X)])
+    line = jnp.where(ours, line, -HELD * PER_GROUP).reshape(CORES * X, 1, LOCAL)
+    line = line + jnp.arange(HELD, dtype=jnp.int32)[:, None] * PER_GROUP
+    line = line.reshape(COLUMN * HELD, 1)
+
+    own_1, other_0 = onward(mine), swap_cores(mine)
+    other_queries = swap_cores(own_queries)
+    own_2, other_1 = onward(own_1), onward(other_0)
+    packed = pack(jnp.where(ours, place, DUMP), own_queries, other_queries)
     received = [packed[0]] + [shift(packed[s], s) for s in range(1, Y)]
-
-    pair_0 = stack([mine, swap_cores(mine)])
-    pair_1 = onward(pair_0)
-    pair_2 = onward(pair_1)
-    pair_2, received[1], received[3] = lax.optimization_barrier((pair_2, received[1], received[3]))
-    pair_3 = onward(pair_2)
-    local_queries, received[1] = lax.optimization_barrier((head_rows(queries), received[1]))
+    own_3, other_2 = onward(own_2), onward(other_1)
+    early = attend_prefix(0, received, [mine, own_1, other_1, own_2, other_2])
+    own_4, other_3 = onward(own_3), onward(other_2)
+    late = attend_prefix(EARLY, received, [own_3, other_3, own_4])
+    parts = []
+    for results in (early, late):
+        parts += [results[0]] + [shift(results[s], -s) for s in range(1, Y)]
+
     local_out, stats = attend_local(
         suffix_length,
-        local_queries,
+        head_rows(queries),
         suffix_keys,
         suffix_values,
         head_rows(new_keys),
         head_rows(new_values),
     )
-    pair_3, local_out, stats, *received = lax.optimization_barrier(
-        (pair_3, local_out, stats, *received)
-    )
-    pair_4 = onward(pair_3)
-    early = attend_prefix(0, received, [pair_0, pair_1, swap_cores(pair_1), pair_2, swap_cores(pair_2)])
-    late = attend_prefix(EARLY, received, [pair_3, swap_cores(pair_3), pair_4])
-    parts = []
-    for results in (early, late):
-        parts += [results[0]] + [shift(results[s], -s) for s in range(1, Y)]
-
-    pieces = unpack(place, line, parts)
+    own_back, other_back = unpack(jnp.where(ours, place, 0), line, parts)
+    pieces = merge(ours.astype(jnp.int32), own_back, swap_cores(other_back))
     got = [pieces[0]] + [turn_x(pieces[s], s) for s in range(1, X)]
     out = combine(at_x, got, local_out, stats)
     out = out.reshape(LOCAL, HEADS, STEPS, HEAD_DIM).transpose(0, 2, 1, 3)

time: 73.9 us -> 73.5 us (level); the launches traced: 73.7 us -> 72.4 us
  starting transfers between devices: 25.1 us -> 28.9 us
  local copies, waits for them, and re-layouts: 5.11 us -> 2.27 us
  waiting for transfers between devices: 30.7 us -> 29.4 us
  Pallas kernels: 11.6 us -> 10.5 us
    ppermute x4, starting transfers between devices: 0.61 us -> 4.36 us  [swap_cores(): return lax.ppermute(value, 'core', [(i, 1 - i) for i in range(CORES)])]
    unnamed x26 -> x20, local copies, waits for them, and re-layouts: 4.87 us -> 1.88 us
    pallas_call x2, Pallas kernels: 4.9 us -> 3.16 us  [attend_prefix(): pl.pallas_call(functools.partial(prefix_kernel, first, count), out_shape=...]
    ppermute x9, starting transfers between devices: 14.9 us -> 13.8 us  [shift(): return lax.ppermute(value, 'y', [(i, (i + turns) % Y) for i in range(Y)])]
    ppermute x6, waiting for transfers between devices: 5.52 us -> 4.54 us  [turn_x(): return lax.ppermute(value, 'x', [(i, (i + turns) % X) for i in range(X)])]
    ppermute x4 -> x7, starting transfers between devices: 2.42 us -> 3.11 us  [onward(): return lax.ppermute(value, ('z', 'core'), pairs)]
    ppermute x4 -> x7, waiting for transfers between devices: 8.19 us -> 7.82 us  [onward(): return lax.ppermute(value, ('z', 'core'), pairs)]
  transfers between devices with their start and end apart: 23 -> 26, of which waited for: 13 -> 16; matrix products, arithmetic and copies ran while one was open for 1% -> 1% of each run, Pallas kernels for 12% -> 9%
where the time goes in v3:
time: 73.5 us; the launch traced here: 72.4 us
  waiting for transfers between devices  29.4 us (40%)
  starting transfers between devices  28.9 us (39%)
  Pallas kernels  10.5 us (14%)
  local copies, waits for them, and re-layouts  2.27 us (3%)
  between operations  0.84 us (1%)
    ppermute x9, waiting for transfers between devices, shift(): return lax.ppermute(value, 'y', [(i, (i + turns) % Y) for i in range(Y)])  15.5 us
    ppermute x9, starting transfers between devices, shift(): return lax.ppermute(value, 'y', [(i, (i + turns) % Y) for i in range(Y)])  13.8 us
    ppermute x7, waiting for transfers between devices, onward(): return lax.ppermute(value, ('z', 'core'), pairs)  7.82 us
    ppermute x6, starting transfers between devices, turn_x(): return lax.ppermute(value, 'x', [(i, (i + turns) % X) for i in range(X)])  7.66 us
    ppermute x6, waiting for transfers between devices, turn_x(): return lax.ppermute(value, 'x', [(i, (i + turns) % X) for i in range(X)])  4.54 us
    ppermute x4, starting transfers between devices, swap_cores(): return lax.ppermute(value, 'core', [(i, 1 - i) for i in range(CORES)])  4.36 us
    pallas_call x2, Pallas kernels, attend_prefix(): pl.pallas_call(functools.partial(prefix_kernel, first, count), out_shape=...  3.16 us
    ppermute x7, starting transfers between devices, onward(): return lax.ppermute(value, ('z', 'core'), pairs)  3.11 us
  transfers between devices with their start and end apart: 26, of which 16 were waited for; matrix products, arithmetic and copies ran while one was open for 1% of the time, Pallas kernels for 9%

profile of v3, /device:TPU:6, one launch (start us, length us, event | category | flops | bytes accessed | tf_op | source)
XLA Modules:
  0.0 72.4 jit_solution(5600246552403597594)
XLA Ops:
  2.8 2.0 %collective-permute-start.8 = (bf16[1040,128]{1,0:T(8,128)(2,1)S(1)}, bf16[1040,128]{1,0:T(8,128)(2,1)S(1)}, u32[]{:S(2)}, u32[]{:S(2)}) collective-permute-start(bf16[1040,128]{1,0:T(8,128)(2,1)S(1)} %build_cache.1.refs_4_), channel_id=1, source_target_pairs={{0,32},{4,228},{32,64},{36,4},{64,96},{68,36},{96,128},{100,68},{1... | collective-permute-start | bytes 798728 | tf_op jit(solution)/shard_map/ppermute | solution.py:400
  4.8 4.1 %collective-permute-start = (s32[32]{0:T(128)S(1)}, s32[32]{0:T(128)S(1)}, u32[]{:S(2)}, u32[]{:S(2)}) collective-permute-start(s32[32]{0:T(128)S(1)} %bitcast.28), channel_id=1, source_target_pairs={{0,4},{4,0},{1,5},{5,1},{2,6},{6,2},{3,7},{7,3},{8,12},{12,8},{9,1... | collective-permute-start | bytes 392 | tf_op jit(solution)/shard_map/ppermute | solution.py:392
  10.8 2.1 %collective-permute-start.3 = (bf16[256,128]{1,0:T(8,128)(2,1)S(1)}, bf16[256,128]{1,0:T(8,128)(2,1)S(1)}, u32[]{:S(2)}, u32[]{:S(2)}) collective-permute-start(bf16[256,128]{1,0:T(8,128)(2,1)S(1)} %get-tuple-element.32), channel_id=1, source_target_pairs={{0,1},{1,2},{2,3},{3,0},{4,5},{5,6},{6,7},{7,4},{8,9},{9,10},{10,1... | collective-permute-start | bytes 196616 | tf_op jit(solution)/shard_map/ppermute | solution.py:384
  13.4 2.3 %collective-permute-done.1.refs_1_ = bf16[256,128]{1,0:T(8,128)(2,1)S(1)} collective-permute-done((bf16[256,128]{1,0:T(8,128)(2,1)S(1)}, bf16[256,128]{1,0:T(8,128)(2,1)S(1)}, u32[]{:S(2)}, u32[]{:S(2)}) %collective-permute-start.1) | collective-permute-done | bytes 65568 | tf_op jit(solution)/shard_map/ppermute | solution.py:384
  16.4 4.2 %collective-permute-done.10.refs_6_ = bf16[1040,128]{1,0:T(8,128)(2,1)S(1)} collective-permute-done((bf16[1040,128]{1,0:T(8,128)(2,1)S(1)}, bf16[1040,128]{1,0:T(8,128)(2,1)S(1)}, u32[]{:S(2)}, u32[]{:S(2)}) %collective-permute-start.10) | collective-permute-done | bytes 266272 | tf_op jit(solution)/shard_map/ppermute | solution.py:400
  20.5 2.8 %collective-permute-done.11.refs_7_ = bf16[1040,128]{1,0:T(8,128)(2,1)S(1)} collective-permute-done((bf16[1040,128]{1,0:T(8,128)(2,1)S(1)}, bf16[1040,128]{1,0:T(8,128)(2,1)S(1)}, u32[]{:S(2)}, u32[]{:S(2)}) %collective-permute-start.11) | collective-permute-done | bytes 266272 | tf_op jit(solution)/shard_map/ppermute | solution.py:400
  24.3 1.7 %collective-permute-start.5 = (bf16[1024,128]{1,0:T(8,128)(2,1)S(1)}, bf16[1024,128]{1,0:T(8,128)(2,1)S(1)}, u32[]{:S(2)}, u32[]{:S(2)}) collective-permute-start(bf16[1024,128]{1,0:T(8,128)(2,1)S(1)} %get-tuple-element.34), channel_id=1, source_target_pairs={{0,8},{8,16},{16,24},{24,0},{1,9},{9,17},{17,25},{25,1},{2,10},{10... | collective-permute-start | bytes 786440 | tf_op jit(solution)/shard_map/ppermute | solution.py:388
  26.0 2.9 %collective-permute-start.6 = (bf16[1024,128]{1,0:T(8,128)(2,1)S(1)}, bf16[1024,128]{1,0:T(8,128)(2,1)S(1)}, u32[]{:S(2)}, u32[]{:S(2)}) collective-permute-start(bf16[1024,128]{1,0:T(8,128)(2,1)S(1)} %get-tuple-element.35), channel_id=1, source_target_pairs={{0,16},{8,24},{16,0},{24,8},{1,17},{9,25},{17,1},{25,9},{2,18},{10... | collective-permute-start | bytes 786440 | tf_op jit(solution)/shard_map/ppermute | solution.py:388
  28.9 1.3 %collective-permute-start.7 = (bf16[1024,128]{1,0:T(8,128)(2,1)S(1)}, bf16[1024,128]{1,0:T(8,128)(2,1)S(1)}, u32[]{:S(2)}, u32[]{:S(2)}) collective-permute-start(bf16[1024,128]{1,0:T(8,128)(2,1)S(1)} %get-tuple-element.36), channel_id=1, source_target_pairs={{0,24},{8,0},{16,8},{24,16},{1,25},{9,1},{17,9},{25,17},{2,26},{10... | collective-permute-start | bytes 786440 | tf_op jit(solution)/shard_map/ppermute | solution.py:388
  32.1 1.6 %collective-permute-done.5.refs_1_ = bf16[1024,128]{1,0:T(8,128)(2,1)S(1)} collective-permute-done((bf16[1024,128]{1,0:T(8,128)(2,1)S(1)}, bf16[1024,128]{1,0:T(8,128)(2,1)S(1)}, u32[]{:S(2)}, u32[]{:S(2)}) %collective-permute-start.5) | collective-permute-done | bytes 262176 | tf_op jit(solution)/shard_map/ppermute | solution.py:388
  33.8 5.7 %collective-permute-done.6.refs_2_ = bf16[1024,128]{1,0:T(8,128)(2,1)S(1)} collective-permute-done((bf16[1024,128]{1,0:T(8,128)(2,1)S(1)}, bf16[1024,128]{1,0:T(8,128)(2,1)S(1)}, u32[]{:S(2)}, u32[]{:S(2)}) %collective-permute-start.6) | collective-permute-done | bytes 262176 | tf_op jit(solution)/shard_map/ppermute | solution.py:388
  39.4 1.9 %prefix_attention_0.1 = (bf16[688,128]{1,0:T(8,128)(2,1)S(1)}, bf16[688,128]{1,0:T(8,128)(2,1)S(1)}, bf16[688,128]{1,0:T(8,128)(2,1)S(1)}, bf16[688,128]{1,0:T(8,128)(2,1)S(1)}) custom-call(bf16[1024,128]{1,0:T(8,128)(2,1)S(1)} %get-tuple-element.33.refs_0_, bf16[1024,128]{1,0:T(8,128)(2,1)S(1)} %collective-permute-done.5.refs_1_, ...), custom_call_target="tpu_custom_call" | custom-call | tf_op jit(solution)/shard_map/prefix_attention_0/pallas_call | solution.py:258
  41.3 2.2 %collective-permute-start.13 = (bf16[688,128]{1,0:T(8,128)(2,1)S(1)}, bf16[688,128]{1,0:T(8,128)(2,1)S(1)}, u32[]{:S(2)}, u32[]{:S(2)}) collective-permute-start(bf16[688,128]{1,0:T(8,128)(2,1)S(1)} %get-tuple-element.38), channel_id=1, source_target_pairs={{0,24},{8,0},{16,8},{24,16},{1,25},{9,1},{17,9},{25,17},{2,26},{10... | collective-permute-start | bytes 528392 | tf_op jit(solution)/shard_map/ppermute | solution.py:388
  45.5 1.3 %prefix_attention_5.1 = (bf16[416,128]{1,0:T(8,128)(2,1)S(1)}, bf16[416,128]{1,0:T(8,128)(2,1)S(1)}, bf16[416,128]{1,0:T(8,128)(2,1)S(1)}, bf16[416,128]{1,0:T(8,128)(2,1)S(1)}) custom-call(bf16[1024,128]{1,0:T(8,128)(2,1)S(1)} %get-tuple-element.33.refs_0_, bf16[1024,128]{1,0:T(8,128)(2,1)S(1)} %collective-permute-done.5.refs_1_, ...), custom_call_target="tpu_custom_call" | custom-call | tf_op jit(solution)/shard_map/prefix_attention_5/pallas_call | solution.py:258
  46.8 2.6 %collective-permute-start.19 = (bf16[416,128]{1,0:T(8,128)(2,1)S(1)}, bf16[416,128]{1,0:T(8,128)(2,1)S(1)}, u32[]{:S(2)}, u32[]{:S(2)}) collective-permute-start(bf16[416,128]{1,0:T(8,128)(2,1)S(1)} %get-tuple-element.42), channel_id=1, source_target_pairs={{0,24},{8,0},{16,8},{24,16},{1,25},{9,1},{17,9},{25,17},{2,26},{10... | collective-permute-start | bytes 319496 | tf_op jit(solution)/shard_map/ppermute | solution.py:388
  49.4 1.2 %collective-permute-start.20 = (bf16[416,128]{1,0:T(8,128)(2,1)S(1)}, bf16[416,128]{1,0:T(8,128)(2,1)S(1)}, u32[]{:S(2)}, u32[]{:S(2)}) collective-permute-start(bf16[416,128]{1,0:T(8,128)(2,1)S(1)} %get-tuple-element.43), channel_id=1, source_target_pairs={{0,16},{8,24},{16,0},{24,8},{1,17},{9,25},{17,1},{25,9},{2,18},{10... | collective-permute-start | bytes 319496 | tf_op jit(solution)/shard_map/ppermute | solution.py:388
  50.6 1.7 %collective-permute-done.13.refs_1_ = bf16[688,128]{1,0:T(8,128)(2,1)S(1)} collective-permute-done((bf16[688,128]{1,0:T(8,128)(2,1)S(1)}, bf16[688,128]{1,0:T(8,128)(2,1)S(1)}, u32[]{:S(2)}, u32[]{:S(2)}) %collective-permute-start.13) | collective-permute-done | bytes 176160 | tf_op jit(solution)/shard_map/ppermute | solution.py:388
  52.6 3.5 %collective-permute-done.15.refs_3_ = bf16[688,128]{1,0:T(8,128)(2,1)S(1)} collective-permute-done((bf16[688,128]{1,0:T(8,128)(2,1)S(1)}, bf16[688,128]{1,0:T(8,128)(2,1)S(1)}, u32[]{:S(2)}, u32[]{:S(2)}) %collective-permute-start.15) | collective-permute-done | bytes 176160 | tf_op jit(solution)/shard_map/ppermute | solution.py:388
  56.0 1.7 %collective-permute-done.20.refs_6_ = bf16[416,128]{1,0:T(8,128)(2,1)S(1)} collective-permute-done((bf16[416,128]{1,0:T(8,128)(2,1)S(1)}, bf16[416,128]{1,0:T(8,128)(2,1)S(1)}, u32[]{:S(2)}, u32[]{:S(2)}) %collective-permute-start.20) | collective-permute-done | bytes 106528 | tf_op jit(solution)/shard_map/ppermute | solution.py:388
  59.8 1.5 %collective-permute-done.22.got_ref = bf16[1088,128]{1,0:T(8,128)(2,1)S(1)} collective-permute-done((bf16[1088,128]{1,0:T(8,128)(2,1)S(1)}, bf16[1088,128]{1,0:T(8,128)(2,1)S(1)}, u32[]{:S(2)}, u32[]{:S(2)}) %collective-permute-start.22) | collective-permute-done | bytes 278560 | tf_op jit(solution)/shard_map/ppermute | solution.py:392
  62.9 2.4 %collective-permute-start.24 = (bf16[272,128]{1,0:T(8,128)(2,1)S(1)}, bf16[272,128]{1,0:T(8,128)(2,1)S(1)}, u32[]{:S(2)}, u32[]{:S(2)}) collective-permute-start(bf16[272,128]{1,0:T(8,128)(2,1)S(1)} %get-tuple-element.49), channel_id=1, source_target_pairs={{0,2},{1,3},{2,0},{3,1},{4,6},{5,7},{6,4},{7,5},{8,10},{9,11},{10,... | collective-permute-start | bytes 208904 | tf_op jit(solution)/shard_map/ppermute | solution.py:384
  66.3 2.8 %local_attention.1 = (f32[8,128,128]{2,1,0:T(8,128)S(1)}, f32[16,128]{1,0:T(8,128)S(1)}) custom-call(s32[8]{0:T(128)S(1)} %copy-done.8, bf16[8,128,128]{2,1,0:T(8,128)(2,1)S(1)} %bitcast.25, bf16[8,32,1024]{2,1,0:T(8,128)(2,1)S(1)} %copy-done.2, bf16[8,32,1024]{2,1,0:T(8,128)(2,1)S(1)} %copy-done.3, bf16[8,16,128]{2,1,0:T(8,128)(2,1)S(1)} %bitcast.26, ...), custom_call_target="tpu_custom_call" | custom-call | tf_op jit(solution)/shard_map/local_attention/pallas_call | solution.py:88
  69.2 1.7 %collective-permute-done.25.refs_3_ = bf16[272,128]{1,0:T(8,128)(2,1)S(1)} collective-permute-done((bf16[272,128]{1,0:T(8,128)(2,1)S(1)}, bf16[272,128]{1,0:T(8,128)(2,1)S(1)}, u32[]{:S(2)}, u32[]{:S(2)}) %collective-permute-start.25) | collective-permute-done | bytes 69664 | tf_op jit(solution)/shard_map/ppermute | solution.py:384
  70.9 1.5 %combine_parts.1 = bf16[8,128,128]{2,1,0:T(8,128)(2,1)} custom-call(s32[1]{0:T(128)} %bitcast.x_ref, bf16[272,128]{1,0:T(8,128)(2,1)S(1)} %get-tuple-element.47.refs_0_, bf16[272,128]{1,0:T(8,128)(2,1)S(1)} %collective-permute-done.23.refs_1_, bf16[272,128]{1,0:T(8,128)(2,1)S(1)} %collective-permute-done.24.refs_2_, ...), custom_call_target="tpu_custom_call" | custom-call | tf_op jit(solution)/shard_map/combine_parts/pallas_call | solution.py:372
  (72 shorter events, 14.9 us)
Async XLA Ops:
  2.7 10.2 %collective-permute-start.9 = (bf16[1040,128]{1,0:T(8,128)(2,1)S(1)}, bf16[1040,128]{1,0:T(8,128)(2,1)S(1)}, u32[]{:S(2)}, u32[]{:S(2)}) collective-permute-start(bf16[1040,128]{1,0:T(8,128)(2,1)S(1)} %build_cache.1.refs_4_), channel_id=1, source_target_pairs={{0,4},{4,0},{1,5},{5,1},{2,6},{6,2},{3,7},{7,3},{8,12},{12,8},{9,1... | collective-permute-start | bytes 798728 | tf_op jit(solution)/shard_map/ppermute | solution.py:392
  2.8 10.3 %collective-permute-start.8 = (bf16[1040,128]{1,0:T(8,128)(2,1)S(1)}, bf16[1040,128]{1,0:T(8,128)(2,1)S(1)}, u32[]{:S(2)}, u32[]{:S(2)}) collective-permute-start(bf16[1040,128]{1,0:T(8,128)(2,1)S(1)} %build_cache.1.refs_4_), channel_id=1, source_target_pairs={{0,32},{4,228},{32,64},{36,4},{64,96},{68,36},{96,128},{100,68},{1... | collective-permute-start | bytes 798728 | tf_op jit(solution)/shard_map/ppermute | solution.py:400
  4.8 6.0 %collective-permute-start = (s32[32]{0:T(128)S(1)}, s32[32]{0:T(128)S(1)}, u32[]{:S(2)}, u32[]{:S(2)}) collective-permute-start(s32[32]{0:T(128)S(1)} %bitcast.28), channel_id=1, source_target_pairs={{0,4},{4,0},{1,5},{5,1},{2,6},{6,2},{3,7},{7,3},{8,12},{12,8},{9,1... | collective-permute-start | bytes 392 | tf_op jit(solution)/shard_map/ppermute | solution.py:392
  8.9 6.8 %collective-permute-start.1 = (bf16[256,128]{1,0:T(8,128)(2,1)S(1)}, bf16[256,128]{1,0:T(8,128)(2,1)S(1)}, u32[]{:S(2)}, u32[]{:S(2)}) collective-permute-start(bf16[256,128]{1,0:T(8,128)(2,1)S(1)} %get-tuple-element.30), channel_id=1, source_target_pairs={{0,3},{1,0},{2,1},{3,2},{4,7},{5,4},{6,5},{7,6},{8,11},{9,8},{10,9... | collective-permute-start | bytes 196616 | tf_op jit(solution)/shard_map/ppermute | solution.py:384
  9.7 5.9 %collective-permute-start.2 = (bf16[256,128]{1,0:T(8,128)(2,1)S(1)}, bf16[256,128]{1,0:T(8,128)(2,1)S(1)}, u32[]{:S(2)}, u32[]{:S(2)}) collective-permute-start(bf16[256,128]{1,0:T(8,128)(2,1)S(1)} %get-tuple-element.31), channel_id=1, source_target_pairs={{0,2},{1,3},{2,0},{3,1},{4,6},{5,7},{6,4},{7,5},{8,10},{9,11},{10,... | collective-permute-start | bytes 196616 | tf_op jit(solution)/shard_map/ppermute | solution.py:384
  12.9 7.6 %collective-permute-start.10 = (bf16[1040,128]{1,0:T(8,128)(2,1)S(1)}, bf16[1040,128]{1,0:T(8,128)(2,1)S(1)}, u32[]{:S(2)}, u32[]{:S(2)}) collective-permute-start(bf16[1040,128]{1,0:T(8,128)(2,1)S(1)} %collective-permute-done.9), channel_id=1, source_target_pairs={{0,32},{4,228},{32,64},{36,4},{64,96},{68,36},{96,128},{100,68},{1... | collective-permute-start | bytes 798728 | tf_op jit(solution)/shard_map/ppermute | solution.py:400
  13.1 10.3 %collective-permute-start.11 = (bf16[1040,128]{1,0:T(8,128)(2,1)S(1)}, bf16[1040,128]{1,0:T(8,128)(2,1)S(1)}, u32[]{:S(2)}, u32[]{:S(2)}) collective-permute-start(bf16[1040,128]{1,0:T(8,128)(2,1)S(1)} %collective-permute-done.8.refs_5_), channel_id=1, source_target_pairs={{0,32},{4,228},{32,64},{36,4},{64,96},{68,36},{96,128},{100,68},{1... | collective-permute-start | bytes 798728 | tf_op jit(solution)/shard_map/ppermute | solution.py:400
  16.1 7.4 %collective-permute-start.4 = (bf16[1024,128]{1,0:T(8,128)(2,1)S(1)}, bf16[1024,128]{1,0:T(8,128)(2,1)S(1)}, u32[]{:S(2)}, u32[]{:S(2)}) collective-permute-start(bf16[1024,128]{1,0:T(8,128)(2,1)S(1)} %stack_queries.1.own_ref), channel_id=1, source_target_pairs={{0,4},{4,0},{1,5},{5,1},{2,6},{6,2},{3,7},{7,3},{8,12},{12,8},{9,1... | collective-permute-start | bytes 786440 | tf_op jit(solution)/shard_map/ppermute | solution.py:392
  20.5 9.9 %collective-permute-start.12 = (bf16[1040,128]{1,0:T(8,128)(2,1)S(1)}, bf16[1040,128]{1,0:T(8,128)(2,1)S(1)}, u32[]{:S(2)}, u32[]{:S(2)}) collective-permute-start(bf16[1040,128]{1,0:T(8,128)(2,1)S(1)} %collective-permute-done.10.refs_6_), channel_id=1, source_target_pairs={{0,32},{4,228},{32,64},{36,4},{64,96},{68,36},{96,128},{100,68},{1... | collective-permute-start | bytes 798728 | tf_op jit(solution)/shard_map/ppermute | solution.py:400
  23.4 7.6 %collective-permute-start.16 = (bf16[1040,128]{1,0:T(8,128)(2,1)S(1)}, bf16[1040,128]{1,0:T(8,128)(2,1)S(1)}, u32[]{:S(2)}, u32[]{:S(2)}) collective-permute-start(bf16[1040,128]{1,0:T(8,128)(2,1)S(1)} %collective-permute-done.11.refs_7_), channel_id=1, source_target_pairs={{0,32},{4,228},{32,64},{36,4},{64,96},{68,36},{96,128},{100,68},{1... | collective-permute-start | bytes 798728 | tf_op jit(solution)/shard_map/ppermute | solution.py:400
  24.3 9.4 %collective-permute-start.5 = (bf16[1024,128]{1,0:T(8,128)(2,1)S(1)}, bf16[1024,128]{1,0:T(8,128)(2,1)S(1)}, u32[]{:S(2)}, u32[]{:S(2)}) collective-permute-start(bf16[1024,128]{1,0:T(8,128)(2,1)S(1)} %get-tuple-element.34), channel_id=1, source_target_pairs={{0,8},{8,16},{16,24},{24,0},{1,9},{9,17},{17,25},{25,1},{2,10},{10... | collective-permute-start | bytes 786440 | tf_op jit(solution)/shard_map/ppermute | solution.py:388
  26.0 13.4 %collective-permute-start.6 = (bf16[1024,128]{1,0:T(8,128)(2,1)S(1)}, bf16[1024,128]{1,0:T(8,128)(2,1)S(1)}, u32[]{:S(2)}, u32[]{:S(2)}) collective-permute-start(bf16[1024,128]{1,0:T(8,128)(2,1)S(1)} %get-tuple-element.35), channel_id=1, source_target_pairs={{0,16},{8,24},{16,0},{24,8},{1,17},{9,25},{17,1},{25,9},{2,18},{10... | collective-permute-start | bytes 786440 | tf_op jit(solution)/shard_map/ppermute | solution.py:388
  28.9 10.5 %collective-permute-start.7 = (bf16[1024,128]{1,0:T(8,128)(2,1)S(1)}, bf16[1024,128]{1,0:T(8,128)(2,1)S(1)}, u32[]{:S(2)}, u32[]{:S(2)}) collective-permute-start(bf16[1024,128]{1,0:T(8,128)(2,1)S(1)} %get-tuple-element.36), channel_id=1, source_target_pairs={{0,24},{8,0},{16,8},{24,16},{1,25},{9,1},{17,9},{25,17},{2,26},{10... | collective-permute-start | bytes 786440 | tf_op jit(solution)/shard_map/ppermute | solution.py:388
  30.4 15.1 %collective-permute-start.17 = (bf16[1040,128]{1,0:T(8,128)(2,1)S(1)}, bf16[1040,128]{1,0:T(8,128)(2,1)S(1)}, u32[]{:S(2)}, u32[]{:S(2)}) collective-permute-start(bf16[1040,128]{1,0:T(8,128)(2,1)S(1)} %collective-permute-done.12.refs_8_), channel_id=1, source_target_pairs={{0,32},{4,228},{32,64},{36,4},{64,96},{68,36},{96,128},{100,68},{1... | collective-permute-start | bytes 798728 | tf_op jit(solution)/shard_map/ppermute | solution.py:400
  31.0 14.4 %collective-permute-start.18 = (bf16[1040,128]{1,0:T(8,128)(2,1)S(1)}, bf16[1040,128]{1,0:T(8,128)(2,1)S(1)}, u32[]{:S(2)}, u32[]{:S(2)}) collective-permute-start(bf16[1040,128]{1,0:T(8,128)(2,1)S(1)} %collective-permute-done.16.refs_4_), channel_id=1, source_target_pairs={{0,32},{4,228},{32,64},{36,4},{64,96},{68,36},{96,128},{100,68},{1... | collective-permute-start | bytes 798728 | tf_op jit(solution)/shard_map/ppermute | solution.py:400
  41.3 10.9 %collective-permute-start.13 = (bf16[688,128]{1,0:T(8,128)(2,1)S(1)}, bf16[688,128]{1,0:T(8,128)(2,1)S(1)}, u32[]{:S(2)}, u32[]{:S(2)}) collective-permute-start(bf16[688,128]{1,0:T(8,128)(2,1)S(1)} %get-tuple-element.38), channel_id=1, source_target_pairs={{0,24},{8,0},{16,8},{24,16},{1,25},{9,1},{17,9},{25,17},{2,26},{10... | collective-permute-start | bytes 528392 | tf_op jit(solution)/shard_map/ppermute | solution.py:388
  43.6 8.9 %collective-permute-start.14 = (bf16[688,128]{1,0:T(8,128)(2,1)S(1)}, bf16[688,128]{1,0:T(8,128)(2,1)S(1)}, u32[]{:S(2)}, u32[]{:S(2)}) collective-permute-start(bf16[688,128]{1,0:T(8,128)(2,1)S(1)} %get-tuple-element.39), channel_id=1, source_target_pairs={{0,16},{8,24},{16,0},{24,8},{1,17},{9,25},{17,1},{25,9},{2,18},{10... | collective-permute-start | bytes 528392 | tf_op jit(solution)/shard_map/ppermute | solution.py:388
  44.8 11.2 %collective-permute-start.15 = (bf16[688,128]{1,0:T(8,128)(2,1)S(1)}, bf16[688,128]{1,0:T(8,128)(2,1)S(1)}, u32[]{:S(2)}, u32[]{:S(2)}) collective-permute-start(bf16[688,128]{1,0:T(8,128)(2,1)S(1)} %get-tuple-element.40), channel_id=1, source_target_pairs={{0,8},{8,16},{16,24},{24,0},{1,9},{9,17},{17,25},{25,1},{2,10},{10... | collective-permute-start | bytes 528392 | tf_op jit(solution)/shard_map/ppermute | solution.py:388
  46.8 9.3 %collective-permute-start.19 = (bf16[416,128]{1,0:T(8,128)(2,1)S(1)}, bf16[416,128]{1,0:T(8,128)(2,1)S(1)}, u32[]{:S(2)}, u32[]{:S(2)}) collective-permute-start(bf16[416,128]{1,0:T(8,128)(2,1)S(1)} %get-tuple-element.42), channel_id=1, source_target_pairs={{0,24},{8,0},{16,8},{24,16},{1,25},{9,1},{17,9},{25,17},{2,26},{10... | collective-permute-start | bytes 319496 | tf_op jit(solution)/shard_map/ppermute | solution.py:388
  49.4 8.4 %collective-permute-start.20 = (bf16[416,128]{1,0:T(8,128)(2,1)S(1)}, bf16[416,128]{1,0:T(8,128)(2,1)S(1)}, u32[]{:S(2)}, u32[]{:S(2)}) collective-permute-start(bf16[416,128]{1,0:T(8,128)(2,1)S(1)} %get-tuple-element.43), channel_id=1, source_target_pairs={{0,16},{8,24},{16,0},{24,8},{1,17},{9,25},{17,1},{25,9},{2,18},{10... | collective-permute-start | bytes 319496 | tf_op jit(solution)/shard_map/ppermute | solution.py:388
  52.3 6.6 %collective-permute-start.21 = (bf16[416,128]{1,0:T(8,128)(2,1)S(1)}, bf16[416,128]{1,0:T(8,128)(2,1)S(1)}, u32[]{:S(2)}, u32[]{:S(2)}) collective-permute-start(bf16[416,128]{1,0:T(8,128)(2,1)S(1)} %get-tuple-element.44), channel_id=1, source_target_pairs={{0,8},{8,16},{16,24},{24,0},{1,9},{9,17},{17,25},{25,1},{2,10},{10... | collective-permute-start | bytes 319496 | tf_op jit(solution)/shard_map/ppermute | solution.py:388
  62.0 7.1 %collective-permute-start.23 = (bf16[272,128]{1,0:T(8,128)(2,1)S(1)}, bf16[272,128]{1,0:T(8,128)(2,1)S(1)}, u32[]{:S(2)}, u32[]{:S(2)}) collective-permute-start(bf16[272,128]{1,0:T(8,128)(2,1)S(1)} %get-tuple-element.48), channel_id=1, source_target_pairs={{0,1},{1,2},{2,3},{3,0},{4,5},{5,6},{6,7},{7,4},{8,9},{9,10},{10,1... | collective-permute-start | bytes 208904 | tf_op jit(solution)/shard_map/ppermute | solution.py:384
  62.9 6.3 %collective-permute-start.24 = (bf16[272,128]{1,0:T(8,128)(2,1)S(1)}, bf16[272,128]{1,0:T(8,128)(2,1)S(1)}, u32[]{:S(2)}, u32[]{:S(2)}) collective-permute-start(bf16[272,128]{1,0:T(8,128)(2,1)S(1)} %get-tuple-element.49), channel_id=1, source_target_pairs={{0,2},{1,3},{2,0},{3,1},{4,6},{5,7},{6,4},{7,5},{8,10},{9,11},{10,... | collective-permute-start | bytes 208904 | tf_op jit(solution)/shard_map/ppermute | solution.py:384
  65.4 5.5 %collective-permute-start.25 = (bf16[272,128]{1,0:T(8,128)(2,1)S(1)}, bf16[272,128]{1,0:T(8,128)(2,1)S(1)}, u32[]{:S(2)}, u32[]{:S(2)}) collective-permute-start(bf16[272,128]{1,0:T(8,128)(2,1)S(1)} %get-tuple-element.50), channel_id=1, source_target_pairs={{0,3},{1,0},{2,1},{3,2},{4,7},{5,4},{6,5},{7,6},{8,11},{9,8},{10,9... | collective-permute-start | bytes 208904 | tf_op jit(solution)/shard_map/ppermute | solution.py:384
  (12 other events, 38.8 us)

commit v4 on v3

--- a/solution.py
+++ b/solution.py
@@ -32,6 +32,7 @@
 CACHE_ROWS = 2 * HELD * PREFIX_MAX
 F32 = jnp.float32
 BF16 = jnp.bfloat16
+TURNS = (0, 1, 3, 2)
 PARAMS = pltpu.CompilerParams(vmem_limit_bytes=32 * 1024 * 1024)
 
 
@@ -439,6 +440,7 @@
         jnp.logical_and(same, index[:, None] > index[None, :]), axis=1, dtype=jnp.int32
     )
     turn = ((ids // CORES) % Y - lax.axis_index("y") + Y) % Y
+    turn = jnp.where(turn < 2, turn, Y + 1 - turn)
     owner_core = ids % CORES
     ahead = (ids // (CORES * Y) - z + Z) % Z
     half = Z // 2
@@ -460,14 +462,14 @@
     other_queries = swap_cores(own_queries)
     own_2, other_1 = onward(own_1), onward(other_0)
     packed = pack(jnp.where(ours, place, DUMP), own_queries, other_queries)
-    received = [packed[0]] + [shift(packed[s], s) for s in range(1, Y)]
+    received = [packed[0]] + [shift(packed[s], TURNS[s]) for s in range(1, Y)]
     own_3, other_2 = onward(own_2), onward(other_1)
     early = attend_prefix(0, received, [mine, own_1, other_1, own_2, other_2])
     own_4, other_3 = onward(own_3), onward(other_2)
     late = attend_prefix(EARLY, received, [own_3, other_3, own_4])
     parts = []
     for results in (early, late):
-        parts += [results[0]] + [shift(results[s], -s) for s in range(1, Y)]
+        parts += [results[0]] + [shift(results[s], -TURNS[s]) for s in range(1, Y)]
 
     local_out, stats = attend_local(
         suffix_length,

time: 73.5 us -> 72.7 us (0.989)
  the two profiles are of different devices: /device:TPU:6 before, /device:TPU:24 now
where the time goes in v4:
time: 72.7 us; the launch traced here: 72.5 us
  waiting for transfers between devices  30.5 us (42%)
  starting transfers between devices  28 us (39%)
  Pallas kernels  10.5 us (14%)
  local copies, waits for them, and re-layouts  2.27 us (3%)
  between operations  0.88 us (1%)
    ppermute x9, waiting for transfers between devices, shift(): return lax.ppermute(value, 'y', [(i, (i + turns) % Y) for i in range(Y)])  15.9 us
    ppermute x9, starting transfers between devices, shift(): return lax.ppermute(value, 'y', [(i, (i + turns) % Y) for i in range(Y)])  11.6 us
    ppermute x6, starting transfers between devices, turn_x(): return lax.ppermute(value, 'x', [(i, (i + turns) % X) for i in range(X)])  9.88 us
    ppermute x7, waiting for transfers between devices, onward(): return lax.ppermute(value, ('z', 'core'), pairs)  8.43 us
    ppermute x6, waiting for transfers between devices, turn_x(): return lax.ppermute(value, 'x', [(i, (i + turns) % X) for i in range(X)])  4.6 us
    ppermute x4, starting transfers between devices, swap_cores(): return lax.ppermute(value, 'core', [(i, 1 - i) for i in range(CORES)])  4.36 us
    pallas_call x2, Pallas kernels, attend_prefix(): pl.pallas_call(functools.partial(prefix_kernel, first, count), out_shape=...  3.16 us
    pallas_call x1, Pallas kernels, attend_local(): pl.pallas_call(local_kernel, out_shape=(shape, jax.ShapeDtypeStruct((2 *...  2.78 us
  transfers between devices with their start and end apart: 26, of which 13 were waited for; matrix products, arithmetic and copies ran while one was open for 1% of the time, Pallas kernels for 9%

profile of v4, /device:TPU:24, one launch (start us, length us, event | category | flops | bytes accessed | tf_op | source)
XLA Modules:
  0.0 72.5 jit_solution(11114081404229859656)
XLA Ops:
  0.7 0.9 %copy-done = bf16[8,2,8192]{2,1,0:T(2,128)(2,1)S(1)} copy-done((bf16[8,2,8192]{2,1,0:T(2,128)(2,1)S(1)}, bf16[8,2,8192]{2,1,0:T(2,128)(2,1)}, u32[]{:S(2)}) %copy-start) | copy-done | bytes 262168
  2.8 2.0 %collective-permute-start.8 = (bf16[1040,128]{1,0:T(8,128)(2,1)S(1)}, bf16[1040,128]{1,0:T(8,128)(2,1)S(1)}, u32[]{:S(2)}, u32[]{:S(2)}) collective-permute-start(bf16[1040,128]{1,0:T(8,128)(2,1)S(1)} %build_cache.1.refs_4_), channel_id=1, source_target_pairs={{0,32},{4,228},{32,64},{36,4},{64,96},{68,36},{96,128},{100,68},{1... | collective-permute-start | bytes 798728 | tf_op jit(solution)/shard_map/ppermute | solution.py:401
  4.8 4.1 %collective-permute-start = (s32[32]{0:T(128)S(1)}, s32[32]{0:T(128)S(1)}, u32[]{:S(2)}, u32[]{:S(2)}) collective-permute-start(s32[32]{0:T(128)S(1)} %bitcast.28), channel_id=1, source_target_pairs={{0,4},{4,0},{1,5},{5,1},{2,6},{6,2},{3,7},{7,3},{8,12},{12,8},{9,1... | collective-permute-start | bytes 392 | tf_op jit(solution)/shard_map/ppermute | solution.py:393
  8.9 2.8 %collective-permute-start.1 = (bf16[256,128]{1,0:T(8,128)(2,1)S(1)}, bf16[256,128]{1,0:T(8,128)(2,1)S(1)}, u32[]{:S(2)}, u32[]{:S(2)}) collective-permute-start(bf16[256,128]{1,0:T(8,128)(2,1)S(1)} %get-tuple-element.30), channel_id=1, source_target_pairs={{0,3},{1,0},{2,1},{3,2},{4,7},{5,4},{6,5},{7,6},{8,11},{9,8},{10,9... | collective-permute-start | bytes 196616 | tf_op jit(solution)/shard_map/ppermute | solution.py:385
  14.0 3.6 %collective-permute-done.2.refs_2_ = bf16[256,128]{1,0:T(8,128)(2,1)S(1)} collective-permute-done((bf16[256,128]{1,0:T(8,128)(2,1)S(1)}, bf16[256,128]{1,0:T(8,128)(2,1)S(1)}, u32[]{:S(2)}, u32[]{:S(2)}) %collective-permute-start.2) | collective-permute-done | bytes 65568 | tf_op jit(solution)/shard_map/ppermute | solution.py:385
  18.6 2.4 %collective-permute-done.10.refs_6_ = bf16[1040,128]{1,0:T(8,128)(2,1)S(1)} collective-permute-done((bf16[1040,128]{1,0:T(8,128)(2,1)S(1)}, bf16[1040,128]{1,0:T(8,128)(2,1)S(1)}, u32[]{:S(2)}, u32[]{:S(2)}) %collective-permute-start.10) | collective-permute-done | bytes 266272 | tf_op jit(solution)/shard_map/ppermute | solution.py:401
  20.9 2.8 %collective-permute-done.11.refs_7_ = bf16[1040,128]{1,0:T(8,128)(2,1)S(1)} collective-permute-done((bf16[1040,128]{1,0:T(8,128)(2,1)S(1)}, bf16[1040,128]{1,0:T(8,128)(2,1)S(1)}, u32[]{:S(2)}, u32[]{:S(2)}) %collective-permute-start.11) | collective-permute-done | bytes 266272 | tf_op jit(solution)/shard_map/ppermute | solution.py:401
  25.0 1.8 %collective-permute-start.6 = (bf16[1024,128]{1,0:T(8,128)(2,1)S(1)}, bf16[1024,128]{1,0:T(8,128)(2,1)S(1)}, u32[]{:S(2)}, u32[]{:S(2)}) collective-permute-start(bf16[1024,128]{1,0:T(8,128)(2,1)S(1)} %get-tuple-element.35), channel_id=1, source_target_pairs={{0,24},{8,0},{16,8},{24,16},{1,25},{9,1},{17,9},{25,17},{2,26},{10... | collective-permute-start | bytes 786440 | tf_op jit(solution)/shard_map/ppermute | solution.py:389
  26.9 1.2 %collective-permute-start.7 = (bf16[1024,128]{1,0:T(8,128)(2,1)S(1)}, bf16[1024,128]{1,0:T(8,128)(2,1)S(1)}, u32[]{:S(2)}, u32[]{:S(2)}) collective-permute-start(bf16[1024,128]{1,0:T(8,128)(2,1)S(1)} %get-tuple-element.36), channel_id=1, source_target_pairs={{0,16},{8,24},{16,0},{24,8},{1,17},{9,25},{17,1},{25,9},{2,18},{10... | collective-permute-start | bytes 786440 | tf_op jit(solution)/shard_map/ppermute | solution.py:389
  28.6 2.8 %collective-permute-done.16.refs_4_ = bf16[1040,128]{1,0:T(8,128)(2,1)S(1)} collective-permute-done((bf16[1040,128]{1,0:T(8,128)(2,1)S(1)}, bf16[1040,128]{1,0:T(8,128)(2,1)S(1)}, u32[]{:S(2)}, u32[]{:S(2)}) %collective-permute-start.16) | collective-permute-done | bytes 266272 | tf_op jit(solution)/shard_map/ppermute | solution.py:401
  31.5 2.6 %collective-permute-done.5.refs_1_ = bf16[1024,128]{1,0:T(8,128)(2,1)S(1)} collective-permute-done((bf16[1024,128]{1,0:T(8,128)(2,1)S(1)}, bf16[1024,128]{1,0:T(8,128)(2,1)S(1)}, u32[]{:S(2)}, u32[]{:S(2)}) %collective-permute-start.5) | collective-permute-done | bytes 262176 | tf_op jit(solution)/shard_map/ppermute | solution.py:389
  34.1 4.6 %collective-permute-done.6.refs_2_ = bf16[1024,128]{1,0:T(8,128)(2,1)S(1)} collective-permute-done((bf16[1024,128]{1,0:T(8,128)(2,1)S(1)}, bf16[1024,128]{1,0:T(8,128)(2,1)S(1)}, u32[]{:S(2)}, u32[]{:S(2)}) %collective-permute-start.6) | collective-permute-done | bytes 262176 | tf_op jit(solution)/shard_map/ppermute | solution.py:389
  38.7 1.9 %prefix_attention_0.1 = (bf16[688,128]{1,0:T(8,128)(2,1)S(1)}, bf16[688,128]{1,0:T(8,128)(2,1)S(1)}, bf16[688,128]{1,0:T(8,128)(2,1)S(1)}, bf16[688,128]{1,0:T(8,128)(2,1)S(1)}) custom-call(bf16[1024,128]{1,0:T(8,128)(2,1)S(1)} %get-tuple-element.33.refs_0_, bf16[1024,128]{1,0:T(8,128)(2,1)S(1)} %collective-permute-done.5.refs_1_, ...), custom_call_target="tpu_custom_call" | custom-call | tf_op jit(solution)/shard_map/prefix_attention_0/pallas_call | solution.py:259
  40.7 3.2 %collective-permute-start.14 = (bf16[688,128]{1,0:T(8,128)(2,1)S(1)}, bf16[688,128]{1,0:T(8,128)(2,1)S(1)}, u32[]{:S(2)}, u32[]{:S(2)}) collective-permute-start(bf16[688,128]{1,0:T(8,128)(2,1)S(1)} %get-tuple-element.39), channel_id=1, source_target_pairs={{0,8},{8,16},{16,24},{24,0},{1,9},{9,17},{17,25},{25,1},{2,10},{10... | collective-permute-start | bytes 528392 | tf_op jit(solution)/shard_map/ppermute | solution.py:389
  44.7 1.3 %prefix_attention_5.1 = (bf16[416,128]{1,0:T(8,128)(2,1)S(1)}, bf16[416,128]{1,0:T(8,128)(2,1)S(1)}, bf16[416,128]{1,0:T(8,128)(2,1)S(1)}, bf16[416,128]{1,0:T(8,128)(2,1)S(1)}) custom-call(bf16[1024,128]{1,0:T(8,128)(2,1)S(1)} %get-tuple-element.33.refs_0_, bf16[1024,128]{1,0:T(8,128)(2,1)S(1)} %collective-permute-done.5.refs_1_, ...), custom_call_target="tpu_custom_call" | custom-call | tf_op jit(solution)/shard_map/prefix_attention_5/pallas_call | solution.py:259
  46.4 3.0 %collective-permute-start.20 = (bf16[416,128]{1,0:T(8,128)(2,1)S(1)}, bf16[416,128]{1,0:T(8,128)(2,1)S(1)}, u32[]{:S(2)}, u32[]{:S(2)}) collective-permute-start(bf16[416,128]{1,0:T(8,128)(2,1)S(1)} %get-tuple-element.43), channel_id=1, source_target_pairs={{0,8},{8,16},{16,24},{24,0},{1,9},{9,17},{17,25},{25,1},{2,10},{10... | collective-permute-start | bytes 319496 | tf_op jit(solution)/shard_map/ppermute | solution.py:389
  49.3 3.5 %collective-permute-done.13.refs_1_ = bf16[688,128]{1,0:T(8,128)(2,1)S(1)} collective-permute-done((bf16[688,128]{1,0:T(8,128)(2,1)S(1)}, bf16[688,128]{1,0:T(8,128)(2,1)S(1)}, u32[]{:S(2)}, u32[]{:S(2)}) %collective-permute-start.13) | collective-permute-done | bytes 176160 | tf_op jit(solution)/shard_map/ppermute | solution.py:389
  54.0 5.1 %collective-permute-done.21.refs_7_ = bf16[416,128]{1,0:T(8,128)(2,1)S(1)} collective-permute-done((bf16[416,128]{1,0:T(8,128)(2,1)S(1)}, bf16[416,128]{1,0:T(8,128)(2,1)S(1)}, u32[]{:S(2)}, u32[]{:S(2)}) %collective-permute-start.21) | collective-permute-done | bytes 106528 | tf_op jit(solution)/shard_map/ppermute | solution.py:389
  60.0 1.5 %collective-permute-done.22.got_ref = bf16[1088,128]{1,0:T(8,128)(2,1)S(1)} collective-permute-done((bf16[1088,128]{1,0:T(8,128)(2,1)S(1)}, bf16[1088,128]{1,0:T(8,128)(2,1)S(1)}, u32[]{:S(2)}, u32[]{:S(2)}) %collective-permute-start.22) | collective-permute-done | bytes 278560 | tf_op jit(solution)/shard_map/ppermute | solution.py:393
  62.1 1.9 %collective-permute-start.23 = (bf16[272,128]{1,0:T(8,128)(2,1)S(1)}, bf16[272,128]{1,0:T(8,128)(2,1)S(1)}, u32[]{:S(2)}, u32[]{:S(2)}) collective-permute-start(bf16[272,128]{1,0:T(8,128)(2,1)S(1)} %get-tuple-element.48), channel_id=1, source_target_pairs={{0,1},{1,2},{2,3},{3,0},{4,5},{5,6},{6,7},{7,4},{8,9},{9,10},{10,1... | collective-permute-start | bytes 208904 | tf_op jit(solution)/shard_map/ppermute | solution.py:385
  64.0 2.0 %collective-permute-start.24 = (bf16[272,128]{1,0:T(8,128)(2,1)S(1)}, bf16[272,128]{1,0:T(8,128)(2,1)S(1)}, u32[]{:S(2)}, u32[]{:S(2)}) collective-permute-start(bf16[272,128]{1,0:T(8,128)(2,1)S(1)} %get-tuple-element.49), channel_id=1, source_target_pairs={{0,2},{1,3},{2,0},{3,1},{4,6},{5,7},{6,4},{7,5},{8,10},{9,11},{10,... | collective-permute-start | bytes 208904 | tf_op jit(solution)/shard_map/ppermute | solution.py:385
  66.0 1.5 %collective-permute-start.25 = (bf16[272,128]{1,0:T(8,128)(2,1)S(1)}, bf16[272,128]{1,0:T(8,128)(2,1)S(1)}, u32[]{:S(2)}, u32[]{:S(2)}) collective-permute-start(bf16[272,128]{1,0:T(8,128)(2,1)S(1)} %get-tuple-element.50), channel_id=1, source_target_pairs={{0,3},{1,0},{2,1},{3,2},{4,7},{5,4},{6,5},{7,6},{8,11},{9,8},{10,9... | collective-permute-start | bytes 208904 | tf_op jit(solution)/shard_map/ppermute | solution.py:385
  68.2 2.8 %local_attention.1 = (f32[8,128,128]{2,1,0:T(8,128)S(1)}, f32[16,128]{1,0:T(8,128)S(1)}) custom-call(s32[8]{0:T(128)S(1)} %copy-done.8, bf16[8,128,128]{2,1,0:T(8,128)(2,1)S(1)} %bitcast.25, bf16[8,32,1024]{2,1,0:T(8,128)(2,1)S(1)} %copy-done.2, bf16[8,32,1024]{2,1,0:T(8,128)(2,1)S(1)} %copy-done.3, bf16[8,16,128]{2,1,0:T(8,128)(2,1)S(1)} %bitcast.26, ...), custom_call_target="tpu_custom_call" | custom-call | tf_op jit(solution)/shard_map/local_attention/pallas_call | solution.py:89
  71.0 1.5 %combine_parts.1 = bf16[8,128,128]{2,1,0:T(8,128)(2,1)} custom-call(s32[1]{0:T(128)} %bitcast.x_ref, bf16[272,128]{1,0:T(8,128)(2,1)S(1)} %get-tuple-element.47.refs_0_, bf16[272,128]{1,0:T(8,128)(2,1)S(1)} %collective-permute-done.23.refs_1_, bf16[272,128]{1,0:T(8,128)(2,1)S(1)} %collective-permute-done.24.refs_2_, ...), custom_call_target="tpu_custom_call" | custom-call | tf_op jit(solution)/shard_map/combine_parts/pallas_call | solution.py:373
  (72 shorter events, 10.8 us)
Async XLA Ops:
  2.7 10.6 %collective-permute-start.9 = (bf16[1040,128]{1,0:T(8,128)(2,1)S(1)}, bf16[1040,128]{1,0:T(8,128)(2,1)S(1)}, u32[]{:S(2)}, u32[]{:S(2)}) collective-permute-start(bf16[1040,128]{1,0:T(8,128)(2,1)S(1)} %build_cache.1.refs_4_), channel_id=1, source_target_pairs={{0,4},{4,0},{1,5},{5,1},{2,6},{6,2},{3,7},{7,3},{8,12},{12,8},{9,1... | collective-permute-start | bytes 798728 | tf_op jit(solution)/shard_map/ppermute | solution.py:393
  2.8 10.5 %collective-permute-start.8 = (bf16[1040,128]{1,0:T(8,128)(2,1)S(1)}, bf16[1040,128]{1,0:T(8,128)(2,1)S(1)}, u32[]{:S(2)}, u32[]{:S(2)}) collective-permute-start(bf16[1040,128]{1,0:T(8,128)(2,1)S(1)} %build_cache.1.refs_4_), channel_id=1, source_target_pairs={{0,32},{4,228},{32,64},{36,4},{64,96},{68,36},{96,128},{100,68},{1... | collective-permute-start | bytes 798728 | tf_op jit(solution)/shard_map/ppermute | solution.py:401
  4.8 7.6 %collective-permute-start = (s32[32]{0:T(128)S(1)}, s32[32]{0:T(128)S(1)}, u32[]{:S(2)}, u32[]{:S(2)}) collective-permute-start(s32[32]{0:T(128)S(1)} %bitcast.28), channel_id=1, source_target_pairs={{0,4},{4,0},{1,5},{5,1},{2,6},{6,2},{3,7},{7,3},{8,12},{12,8},{9,1... | collective-permute-start | bytes 392 | tf_op jit(solution)/shard_map/ppermute | solution.py:393
  8.9 5.2 %collective-permute-start.1 = (bf16[256,128]{1,0:T(8,128)(2,1)S(1)}, bf16[256,128]{1,0:T(8,128)(2,1)S(1)}, u32[]{:S(2)}, u32[]{:S(2)}) collective-permute-start(bf16[256,128]{1,0:T(8,128)(2,1)S(1)} %get-tuple-element.30), channel_id=1, source_target_pairs={{0,3},{1,0},{2,1},{3,2},{4,7},{5,4},{6,5},{7,6},{8,11},{9,8},{10,9... | collective-permute-start | bytes 196616 | tf_op jit(solution)/shard_map/ppermute | solution.py:385
  11.6 6.0 %collective-permute-start.2 = (bf16[256,128]{1,0:T(8,128)(2,1)S(1)}, bf16[256,128]{1,0:T(8,128)(2,1)S(1)}, u32[]{:S(2)}, u32[]{:S(2)}) collective-permute-start(bf16[256,128]{1,0:T(8,128)(2,1)S(1)} %get-tuple-element.31), channel_id=1, source_target_pairs={{0,2},{1,3},{2,0},{3,1},{4,6},{5,7},{6,4},{7,5},{8,10},{9,11},{10,... | collective-permute-start | bytes 196616 | tf_op jit(solution)/shard_map/ppermute | solution.py:385
  12.4 5.8 %collective-permute-start.3 = (bf16[256,128]{1,0:T(8,128)(2,1)S(1)}, bf16[256,128]{1,0:T(8,128)(2,1)S(1)}, u32[]{:S(2)}, u32[]{:S(2)}) collective-permute-start(bf16[256,128]{1,0:T(8,128)(2,1)S(1)} %get-tuple-element.32), channel_id=1, source_target_pairs={{0,1},{1,2},{2,3},{3,0},{4,5},{5,6},{6,7},{7,4},{8,9},{9,10},{10,1... | collective-permute-start | bytes 196616 | tf_op jit(solution)/shard_map/ppermute | solution.py:385
  13.3 7.6 %collective-permute-start.10 = (bf16[1040,128]{1,0:T(8,128)(2,1)S(1)}, bf16[1040,128]{1,0:T(8,128)(2,1)S(1)}, u32[]{:S(2)}, u32[]{:S(2)}) collective-permute-start(bf16[1040,128]{1,0:T(8,128)(2,1)S(1)} %collective-permute-done.9), channel_id=1, source_target_pairs={{0,32},{4,228},{32,64},{36,4},{64,96},{68,36},{96,128},{100,68},{1... | collective-permute-start | bytes 798728 | tf_op jit(solution)/shard_map/ppermute | solution.py:401
  13.3 10.5 %collective-permute-start.11 = (bf16[1040,128]{1,0:T(8,128)(2,1)S(1)}, bf16[1040,128]{1,0:T(8,128)(2,1)S(1)}, u32[]{:S(2)}, u32[]{:S(2)}) collective-permute-start(bf16[1040,128]{1,0:T(8,128)(2,1)S(1)} %collective-permute-done.8.refs_5_), channel_id=1, source_target_pairs={{0,32},{4,228},{32,64},{36,4},{64,96},{68,36},{96,128},{100,68},{1... | collective-permute-start | bytes 798728 | tf_op jit(solution)/shard_map/ppermute | solution.py:401
  18.3 5.6 %collective-permute-start.4 = (bf16[1024,128]{1,0:T(8,128)(2,1)S(1)}, bf16[1024,128]{1,0:T(8,128)(2,1)S(1)}, u32[]{:S(2)}, u32[]{:S(2)}) collective-permute-start(bf16[1024,128]{1,0:T(8,128)(2,1)S(1)} %stack_queries.1.own_ref), channel_id=1, source_target_pairs={{0,4},{4,0},{1,5},{5,1},{2,6},{6,2},{3,7},{7,3},{8,12},{12,8},{9,1... | collective-permute-start | bytes 786440 | tf_op jit(solution)/shard_map/ppermute | solution.py:393
  20.9 7.6 %collective-permute-start.12 = (bf16[1040,128]{1,0:T(8,128)(2,1)S(1)}, bf16[1040,128]{1,0:T(8,128)(2,1)S(1)}, u32[]{:S(2)}, u32[]{:S(2)}) collective-permute-start(bf16[1040,128]{1,0:T(8,128)(2,1)S(1)} %collective-permute-done.10.refs_6_), channel_id=1, source_target_pairs={{0,32},{4,228},{32,64},{36,4},{64,96},{68,36},{96,128},{100,68},{1... | collective-permute-start | bytes 798728 | tf_op jit(solution)/shard_map/ppermute | solution.py:401
  23.8 7.6 %collective-permute-start.16 = (bf16[1040,128]{1,0:T(8,128)(2,1)S(1)}, bf16[1040,128]{1,0:T(8,128)(2,1)S(1)}, u32[]{:S(2)}, u32[]{:S(2)}) collective-permute-start(bf16[1040,128]{1,0:T(8,128)(2,1)S(1)} %collective-permute-done.11.refs_7_), channel_id=1, source_target_pairs={{0,32},{4,228},{32,64},{36,4},{64,96},{68,36},{96,128},{100,68},{1... | collective-permute-start | bytes 798728 | tf_op jit(solution)/shard_map/ppermute | solution.py:401
  24.7 9.3 %collective-permute-start.5 = (bf16[1024,128]{1,0:T(8,128)(2,1)S(1)}, bf16[1024,128]{1,0:T(8,128)(2,1)S(1)}, u32[]{:S(2)}, u32[]{:S(2)}) collective-permute-start(bf16[1024,128]{1,0:T(8,128)(2,1)S(1)} %get-tuple-element.34), channel_id=1, source_target_pairs={{0,8},{8,16},{16,24},{24,0},{1,9},{9,17},{17,25},{25,1},{2,10},{10... | collective-permute-start | bytes 786440 | tf_op jit(solution)/shard_map/ppermute | solution.py:389
  25.0 13.6 %collective-permute-start.6 = (bf16[1024,128]{1,0:T(8,128)(2,1)S(1)}, bf16[1024,128]{1,0:T(8,128)(2,1)S(1)}, u32[]{:S(2)}, u32[]{:S(2)}) collective-permute-start(bf16[1024,128]{1,0:T(8,128)(2,1)S(1)} %get-tuple-element.35), channel_id=1, source_target_pairs={{0,24},{8,0},{16,8},{24,16},{1,25},{9,1},{17,9},{25,17},{2,26},{10... | collective-permute-start | bytes 786440 | tf_op jit(solution)/shard_map/ppermute | solution.py:389
  26.9 11.8 %collective-permute-start.7 = (bf16[1024,128]{1,0:T(8,128)(2,1)S(1)}, bf16[1024,128]{1,0:T(8,128)(2,1)S(1)}, u32[]{:S(2)}, u32[]{:S(2)}) collective-permute-start(bf16[1024,128]{1,0:T(8,128)(2,1)S(1)} %get-tuple-element.36), channel_id=1, source_target_pairs={{0,16},{8,24},{16,0},{24,8},{1,17},{9,25},{17,1},{25,9},{2,18},{10... | collective-permute-start | bytes 786440 | tf_op jit(solution)/shard_map/ppermute | solution.py:389
  28.6 16.1 %collective-permute-start.17 = (bf16[1040,128]{1,0:T(8,128)(2,1)S(1)}, bf16[1040,128]{1,0:T(8,128)(2,1)S(1)}, u32[]{:S(2)}, u32[]{:S(2)}) collective-permute-start(bf16[1040,128]{1,0:T(8,128)(2,1)S(1)} %collective-permute-done.12.refs_8_), channel_id=1, source_target_pairs={{0,32},{4,228},{32,64},{36,4},{64,96},{68,36},{96,128},{100,68},{1... | collective-permute-start | bytes 798728 | tf_op jit(solution)/shard_map/ppermute | solution.py:401
  31.4 13.3 %collective-permute-start.18 = (bf16[1040,128]{1,0:T(8,128)(2,1)S(1)}, bf16[1040,128]{1,0:T(8,128)(2,1)S(1)}, u32[]{:S(2)}, u32[]{:S(2)}) collective-permute-start(bf16[1040,128]{1,0:T(8,128)(2,1)S(1)} %collective-permute-done.16.refs_4_), channel_id=1, source_target_pairs={{0,32},{4,228},{32,64},{36,4},{64,96},{68,36},{96,128},{100,68},{1... | collective-permute-start | bytes 798728 | tf_op jit(solution)/shard_map/ppermute | solution.py:401
  40.6 12.3 %collective-permute-start.13 = (bf16[688,128]{1,0:T(8,128)(2,1)S(1)}, bf16[688,128]{1,0:T(8,128)(2,1)S(1)}, u32[]{:S(2)}, u32[]{:S(2)}) collective-permute-start(bf16[688,128]{1,0:T(8,128)(2,1)S(1)} %get-tuple-element.38), channel_id=1, source_target_pairs={{0,24},{8,0},{16,8},{24,16},{1,25},{9,1},{17,9},{25,17},{2,26},{10... | collective-permute-start | bytes 528392 | tf_op jit(solution)/shard_map/ppermute | solution.py:389
  40.7 13.1 %collective-permute-start.14 = (bf16[688,128]{1,0:T(8,128)(2,1)S(1)}, bf16[688,128]{1,0:T(8,128)(2,1)S(1)}, u32[]{:S(2)}, u32[]{:S(2)}) collective-permute-start(bf16[688,128]{1,0:T(8,128)(2,1)S(1)} %get-tuple-element.39), channel_id=1, source_target_pairs={{0,8},{8,16},{16,24},{24,0},{1,9},{9,17},{17,25},{25,1},{2,10},{10... | collective-permute-start | bytes 528392 | tf_op jit(solution)/shard_map/ppermute | solution.py:389
  44.0 9.9 %collective-permute-start.15 = (bf16[688,128]{1,0:T(8,128)(2,1)S(1)}, bf16[688,128]{1,0:T(8,128)(2,1)S(1)}, u32[]{:S(2)}, u32[]{:S(2)}) collective-permute-start(bf16[688,128]{1,0:T(8,128)(2,1)S(1)} %get-tuple-element.40), channel_id=1, source_target_pairs={{0,16},{8,24},{16,0},{24,8},{1,17},{9,25},{17,1},{25,9},{2,18},{10... | collective-permute-start | bytes 528392 | tf_op jit(solution)/shard_map/ppermute | solution.py:389
  46.0 8.0 %collective-permute-start.19 = (bf16[416,128]{1,0:T(8,128)(2,1)S(1)}, bf16[416,128]{1,0:T(8,128)(2,1)S(1)}, u32[]{:S(2)}, u32[]{:S(2)}) collective-permute-start(bf16[416,128]{1,0:T(8,128)(2,1)S(1)} %get-tuple-element.42), channel_id=1, source_target_pairs={{0,24},{8,0},{16,8},{24,16},{1,25},{9,1},{17,9},{25,17},{2,26},{10... | collective-permute-start | bytes 319496 | tf_op jit(solution)/shard_map/ppermute | solution.py:389
  46.4 7.6 %collective-permute-start.20 = (bf16[416,128]{1,0:T(8,128)(2,1)S(1)}, bf16[416,128]{1,0:T(8,128)(2,1)S(1)}, u32[]{:S(2)}, u32[]{:S(2)}) collective-permute-start(bf16[416,128]{1,0:T(8,128)(2,1)S(1)} %get-tuple-element.43), channel_id=1, source_target_pairs={{0,8},{8,16},{16,24},{24,0},{1,9},{9,17},{17,25},{25,1},{2,10},{10... | collective-permute-start | bytes 319496 | tf_op jit(solution)/shard_map/ppermute | solution.py:389
  52.8 6.2 %collective-permute-start.21 = (bf16[416,128]{1,0:T(8,128)(2,1)S(1)}, bf16[416,128]{1,0:T(8,128)(2,1)S(1)}, u32[]{:S(2)}, u32[]{:S(2)}) collective-permute-start(bf16[416,128]{1,0:T(8,128)(2,1)S(1)} %get-tuple-element.44), channel_id=1, source_target_pairs={{0,16},{8,24},{16,0},{24,8},{1,17},{9,25},{17,1},{25,9},{2,18},{10... | collective-permute-start | bytes 319496 | tf_op jit(solution)/shard_map/ppermute | solution.py:389
  62.1 8.9 %collective-permute-start.23 = (bf16[272,128]{1,0:T(8,128)(2,1)S(1)}, bf16[272,128]{1,0:T(8,128)(2,1)S(1)}, u32[]{:S(2)}, u32[]{:S(2)}) collective-permute-start(bf16[272,128]{1,0:T(8,128)(2,1)S(1)} %get-tuple-element.48), channel_id=1, source_target_pairs={{0,1},{1,2},{2,3},{3,0},{4,5},{5,6},{6,7},{7,4},{8,9},{9,10},{10,1... | collective-permute-start | bytes 208904 | tf_op jit(solution)/shard_map/ppermute | solution.py:385
  64.0 7.0 %collective-permute-start.24 = (bf16[272,128]{1,0:T(8,128)(2,1)S(1)}, bf16[272,128]{1,0:T(8,128)(2,1)S(1)}, u32[]{:S(2)}, u32[]{:S(2)}) collective-permute-start(bf16[272,128]{1,0:T(8,128)(2,1)S(1)} %get-tuple-element.49), channel_id=1, source_target_pairs={{0,2},{1,3},{2,0},{3,1},{4,6},{5,7},{6,4},{7,5},{8,10},{9,11},{10,... | collective-permute-start | bytes 208904 | tf_op jit(solution)/shard_map/ppermute | solution.py:385
  (12 other events, 47.6 us)

commit v5 on v4

--- a/solution.py
+++ b/solution.py
@@ -96,34 +96,22 @@
     )(lengths, q, sk, sv, nk, nv)
 
 
-def split_kernel(x_ref, q_ref, *refs):
-    out_refs, sems = refs[:X], refs[X]
+def split_kernel(x_ref, q_ref, *out_refs):
     wide = HELD * ROWS
-    copies = []
     for s in range(X):
         head = pl.multiple_of(lax.rem(x_ref[0] + s, X) * wide, wide)
         for r in range(LOCAL):
-            copies.append(
-                pltpu.make_async_copy(
-                    q_ref.at[r, pl.ds(head, wide), :],
-                    out_refs[s].at[pl.ds(r * wide, wide), :],
-                    sems.at[s, r],
-                )
-            )
-    for copy in copies:
-        copy.start()
-    for copy in copies:
-        copy.wait()
+            out_refs[s][r * wide : (r + 1) * wide, :] = q_ref[r, pl.ds(head, wide), :]
 
 
 def split(x, q):
+    vm = pl.BlockSpec(memory_space=pltpu.VMEM)
     part = jax.ShapeDtypeStruct((LOCAL * HELD * ROWS, HEAD_DIM), BF16)
     return pl.pallas_call(
         split_kernel,
         out_shape=[part] * X,
-        in_specs=[pl.BlockSpec(memory_space=pltpu.SMEM), pl.BlockSpec(memory_space=pl.ANY)],
-        out_specs=[pl.BlockSpec(memory_space=pltpu.VMEM)] * X,
-        scratch_shapes=[pltpu.SemaphoreType.DMA((X, LOCAL))],
+        in_specs=[pl.BlockSpec(memory_space=pltpu.SMEM), vm],
+        out_specs=[vm] * X,
         compiler_params=PARAMS,
         name="split_queries",
     )(x, q)
@@ -165,7 +153,8 @@
 def stack_kernel(*refs):
     parts, out_ref = refs[:-1], refs[-1]
     size = parts[0].shape[0]
-    for i, ref in enumerate(parts):
+    for turn, ref in zip(TURNS, parts):
+        i = -turn % X
         out_ref[i * size : (i + 1) * size, :] = ref[...]
 
 
@@ -339,6 +328,7 @@
 
 def combine_kernel(x_ref, *refs):
     parts, (local_ref, stat_ref, out_ref, weight_ref) = refs[:X], refs[X:]
+    parts = [parts[TURNS.index(s)] for s in range(X)]
     wide = HELD * ROWS
     lane_head = iota((LOCAL, HEAD_DIM), 1) // ROWS
     heads = [lax.rem(x_ref[0] + (X - s), X) * HELD for s in range(X)]
@@ -426,7 +416,7 @@
     splits = split(at_x, head_rows(queries))
     mine = build_cache(prefix_length, prefix_keys, prefix_values, splits[0])
     arrived = [splits[0]] + [turn_x(splits[s], s) for s in range(1, X)]
-    own_queries = stack([arrived[-s % X] for s in range(X)])
+    own_queries = stack([arrived[s] for s in TURNS])
 
     block_ids = group_ids[:, 0]
     ids = jnp.stack([block_ids, swap_cores(block_ids)])
@@ -482,7 +472,7 @@
     own_back, other_back = unpack(jnp.where(ours, place, 0), line, parts)
     pieces = merge(ours.astype(jnp.int32), own_back, swap_cores(other_back))
     got = [pieces[0]] + [turn_x(pieces[s], s) for s in range(1, X)]
-    out = combine(at_x, got, local_out, stats)
+    out = combine(at_x, [got[s] for s in TURNS], local_out, stats)
     out = out.reshape(LOCAL, HEADS, STEPS, HEAD_DIM).transpose(0, 2, 1, 3)
     return out.reshape(LOCAL, STEPS, HEADS * HEAD_DIM)
 

time: 72.7 us -> 73.5 us (1.011)
  waiting for transfers between devices: 30.5 us -> 32.3 us
  starting transfers between devices: 28 us -> 26.9 us
    ppermute x6, starting transfers between devices: 9.88 us -> 8.87 us  [turn_x(): return lax.ppermute(value, 'x', [(i, (i + turns) % X) for i in range(X)])]
    ppermute x7, waiting for transfers between devices: 8.43 us -> 9.41 us  [onward(): return lax.ppermute(value, ('z', 'core'), pairs)]
    ppermute x6, waiting for transfers between devices: 4.6 us -> 5.47 us  [turn_x(): return lax.ppermute(value, 'x', [(i, (i + turns) % X) for i in range(X)])]
  transfers between devices with their start and end apart: 26 -> 26, of which waited for: 13 -> 14; matrix products, arithmetic and copies ran while one was open for 1% -> 1% of each run, Pallas kernels for 9% -> 9%
where the time goes in v5:
time: 73.5 us; the launch traced here: 73.3 us
  waiting for transfers between devices  32.3 us (44%)
  starting transfers between devices  26.9 us (37%)
  Pallas kernels  9.87 us (13%)
  local copies, waits for them, and re-layouts  2.93 us (4%)
  between operations  0.87 us (1%)
    ppermute x9, waiting for transfers between devices, shift(): return lax.ppermute(value, 'y', [(i, (i + turns) % Y) for i in range(Y)])  15.9 us
    ppermute x9, starting transfers between devices, shift(): return lax.ppermute(value, 'y', [(i, (i + turns) % Y) for i in range(Y)])  11.6 us
    ppermute x7, waiting for transfers between devices, onward(): return lax.ppermute(value, ('z', 'core'), pairs)  9.41 us
    ppermute x6, starting transfers between devices, turn_x(): return lax.ppermute(value, 'x', [(i, (i + turns) % X) for i in range(X)])  8.87 us
    ppermute x6, waiting for transfers between devices, turn_x(): return lax.ppermute(value, 'x', [(i, (i + turns) % X) for i in range(X)])  5.47 us
    ppermute x4, starting transfers between devices, swap_cores(): return lax.ppermute(value, 'core', [(i, 1 - i) for i in range(CORES)])  4.36 us
    pallas_call x2, Pallas kernels, attend_prefix(): pl.pallas_call(functools.partial(prefix_kernel, first, count), out_shape=...  3.16 us
    pallas_call x1, Pallas kernels, attend_local(): pl.pallas_call(local_kernel, out_shape=(shape, jax.ShapeDtypeStruct((2 *...  2.78 us
  transfers between devices with their start and end apart: 26, of which 14 were waited for; matrix products, arithmetic and copies ran while one was open for 1% of the time, Pallas kernels for 9%

profile of v5, /device:TPU:24, one launch (start us, length us, event | category | flops | bytes accessed | tf_op | source)
XLA Modules:
  0.0 73.3 jit_solution(3408403376716223410)
XLA Ops:
  2.8 2.0 %collective-permute-start.8 = (bf16[1040,128]{1,0:T(8,128)(2,1)S(1)}, bf16[1040,128]{1,0:T(8,128)(2,1)S(1)}, u32[]{:S(2)}, u32[]{:S(2)}) collective-permute-start(bf16[1040,128]{1,0:T(8,128)(2,1)S(1)} %build_cache.1.refs_4_), channel_id=1, source_target_pairs={{0,32},{4,228},{32,64},{36,4},{64,96},{68,36},{96,128},{100,68},{1... | collective-permute-start | bytes 798728 | tf_op jit(solution)/shard_map/ppermute | solution.py:391
  4.8 4.1 %collective-permute-start = (s32[32]{0:T(128)S(1)}, s32[32]{0:T(128)S(1)}, u32[]{:S(2)}, u32[]{:S(2)}) collective-permute-start(s32[32]{0:T(128)S(1)} %bitcast.28), channel_id=1, source_target_pairs={{0,4},{4,0},{1,5},{5,1},{2,6},{6,2},{3,7},{7,3},{8,12},{12,8},{9,1... | collective-permute-start | bytes 392 | tf_op jit(solution)/shard_map/ppermute | solution.py:383
  8.9 1.5 %collective-permute-start.1 = (bf16[256,128]{1,0:T(8,128)(2,1)S(1)}, bf16[256,128]{1,0:T(8,128)(2,1)S(1)}, u32[]{:S(2)}, u32[]{:S(2)}) collective-permute-start(bf16[256,128]{1,0:T(8,128)(2,1)S(1)} %get-tuple-element.30), channel_id=1, source_target_pairs={{0,1},{1,2},{2,3},{3,0},{4,5},{5,6},{6,7},{7,4},{8,9},{9,10},{10,1... | collective-permute-start | bytes 196616 | tf_op jit(solution)/shard_map/ppermute | solution.py:375
  10.4 1.7 %collective-permute-start.2 = (bf16[256,128]{1,0:T(8,128)(2,1)S(1)}, bf16[256,128]{1,0:T(8,128)(2,1)S(1)}, u32[]{:S(2)}, u32[]{:S(2)}) collective-permute-start(bf16[256,128]{1,0:T(8,128)(2,1)S(1)} %get-tuple-element.31), channel_id=1, source_target_pairs={{0,3},{1,0},{2,1},{3,2},{4,7},{5,4},{6,5},{7,6},{8,11},{9,8},{10,9... | collective-permute-start | bytes 196616 | tf_op jit(solution)/shard_map/ppermute | solution.py:375
  12.1 1.8 %collective-permute-start.3 = (bf16[256,128]{1,0:T(8,128)(2,1)S(1)}, bf16[256,128]{1,0:T(8,128)(2,1)S(1)}, u32[]{:S(2)}, u32[]{:S(2)}) collective-permute-start(bf16[256,128]{1,0:T(8,128)(2,1)S(1)} %get-tuple-element.32), channel_id=1, source_target_pairs={{0,2},{1,3},{2,0},{3,1},{4,6},{5,7},{6,4},{7,5},{8,10},{9,11},{10,... | collective-permute-start | bytes 196616 | tf_op jit(solution)/shard_map/ppermute | solution.py:375
  14.8 3.1 %collective-permute-done.3.refs_3_ = bf16[256,128]{1,0:T(8,128)(2,1)S(1)} collective-permute-done((bf16[256,128]{1,0:T(8,128)(2,1)S(1)}, bf16[256,128]{1,0:T(8,128)(2,1)S(1)}, u32[]{:S(2)}, u32[]{:S(2)}) %collective-permute-start.3) | collective-permute-done | bytes 65568 | tf_op jit(solution)/shard_map/ppermute | solution.py:375
  18.2 3.4 %collective-permute-done.10.refs_6_ = bf16[1040,128]{1,0:T(8,128)(2,1)S(1)} collective-permute-done((bf16[1040,128]{1,0:T(8,128)(2,1)S(1)}, bf16[1040,128]{1,0:T(8,128)(2,1)S(1)}, u32[]{:S(2)}, u32[]{:S(2)}) %collective-permute-start.10) | collective-permute-done | bytes 266272 | tf_op jit(solution)/shard_map/ppermute | solution.py:391
  21.6 2.8 %collective-permute-done.11.refs_7_ = bf16[1040,128]{1,0:T(8,128)(2,1)S(1)} collective-permute-done((bf16[1040,128]{1,0:T(8,128)(2,1)S(1)}, bf16[1040,128]{1,0:T(8,128)(2,1)S(1)}, u32[]{:S(2)}, u32[]{:S(2)}) %collective-permute-start.11) | collective-permute-done | bytes 266272 | tf_op jit(solution)/shard_map/ppermute | solution.py:391
  25.7 1.8 %collective-permute-start.6 = (bf16[1024,128]{1,0:T(8,128)(2,1)S(1)}, bf16[1024,128]{1,0:T(8,128)(2,1)S(1)}, u32[]{:S(2)}, u32[]{:S(2)}) collective-permute-start(bf16[1024,128]{1,0:T(8,128)(2,1)S(1)} %get-tuple-element.35), channel_id=1, source_target_pairs={{0,24},{8,0},{16,8},{24,16},{1,25},{9,1},{17,9},{25,17},{2,26},{10... | collective-permute-start | bytes 786440 | tf_op jit(solution)/shard_map/ppermute | solution.py:379
  27.5 1.2 %collective-permute-start.7 = (bf16[1024,128]{1,0:T(8,128)(2,1)S(1)}, bf16[1024,128]{1,0:T(8,128)(2,1)S(1)}, u32[]{:S(2)}, u32[]{:S(2)}) collective-permute-start(bf16[1024,128]{1,0:T(8,128)(2,1)S(1)} %get-tuple-element.36), channel_id=1, source_target_pairs={{0,16},{8,24},{16,0},{24,8},{1,17},{9,25},{17,1},{25,9},{2,18},{10... | collective-permute-start | bytes 786440 | tf_op jit(solution)/shard_map/ppermute | solution.py:379
  29.2 2.8 %collective-permute-done.16.refs_4_ = bf16[1040,128]{1,0:T(8,128)(2,1)S(1)} collective-permute-done((bf16[1040,128]{1,0:T(8,128)(2,1)S(1)}, bf16[1040,128]{1,0:T(8,128)(2,1)S(1)}, u32[]{:S(2)}, u32[]{:S(2)}) %collective-permute-start.16) | collective-permute-done | bytes 266272 | tf_op jit(solution)/shard_map/ppermute | solution.py:391
  32.1 2.6 %collective-permute-done.5.refs_1_ = bf16[1024,128]{1,0:T(8,128)(2,1)S(1)} collective-permute-done((bf16[1024,128]{1,0:T(8,128)(2,1)S(1)}, bf16[1024,128]{1,0:T(8,128)(2,1)S(1)}, u32[]{:S(2)}, u32[]{:S(2)}) %collective-permute-start.5) | collective-permute-done | bytes 262176 | tf_op jit(solution)/shard_map/ppermute | solution.py:379
  34.7 4.6 %collective-permute-done.6.refs_2_ = bf16[1024,128]{1,0:T(8,128)(2,1)S(1)} collective-permute-done((bf16[1024,128]{1,0:T(8,128)(2,1)S(1)}, bf16[1024,128]{1,0:T(8,128)(2,1)S(1)}, u32[]{:S(2)}, u32[]{:S(2)}) %collective-permute-start.6) | collective-permute-done | bytes 262176 | tf_op jit(solution)/shard_map/ppermute | solution.py:379
  39.3 1.9 %prefix_attention_0.1 = (bf16[688,128]{1,0:T(8,128)(2,1)S(1)}, bf16[688,128]{1,0:T(8,128)(2,1)S(1)}, bf16[688,128]{1,0:T(8,128)(2,1)S(1)}, bf16[688,128]{1,0:T(8,128)(2,1)S(1)}) custom-call(bf16[1024,128]{1,0:T(8,128)(2,1)S(1)} %get-tuple-element.33.refs_0_, bf16[1024,128]{1,0:T(8,128)(2,1)S(1)} %collective-permute-done.5.refs_1_, ...), custom_call_target="tpu_custom_call" | custom-call | tf_op jit(solution)/shard_map/prefix_attention_0/pallas_call | solution.py:248
  41.3 3.2 %collective-permute-start.14 = (bf16[688,128]{1,0:T(8,128)(2,1)S(1)}, bf16[688,128]{1,0:T(8,128)(2,1)S(1)}, u32[]{:S(2)}, u32[]{:S(2)}) collective-permute-start(bf16[688,128]{1,0:T(8,128)(2,1)S(1)} %get-tuple-element.39), channel_id=1, source_target_pairs={{0,8},{8,16},{16,24},{24,0},{1,9},{9,17},{17,25},{25,1},{2,10},{10... | collective-permute-start | bytes 528392 | tf_op jit(solution)/shard_map/ppermute | solution.py:379
  45.3 1.3 %prefix_attention_5.1 = (bf16[416,128]{1,0:T(8,128)(2,1)S(1)}, bf16[416,128]{1,0:T(8,128)(2,1)S(1)}, bf16[416,128]{1,0:T(8,128)(2,1)S(1)}, bf16[416,128]{1,0:T(8,128)(2,1)S(1)}) custom-call(bf16[1024,128]{1,0:T(8,128)(2,1)S(1)} %get-tuple-element.33.refs_0_, bf16[1024,128]{1,0:T(8,128)(2,1)S(1)} %collective-permute-done.5.refs_1_, ...), custom_call_target="tpu_custom_call" | custom-call | tf_op jit(solution)/shard_map/prefix_attention_5/pallas_call | solution.py:248
  47.0 3.0 %collective-permute-start.20 = (bf16[416,128]{1,0:T(8,128)(2,1)S(1)}, bf16[416,128]{1,0:T(8,128)(2,1)S(1)}, u32[]{:S(2)}, u32[]{:S(2)}) collective-permute-start(bf16[416,128]{1,0:T(8,128)(2,1)S(1)} %get-tuple-element.43), channel_id=1, source_target_pairs={{0,8},{8,16},{16,24},{24,0},{1,9},{9,17},{17,25},{25,1},{2,10},{10... | collective-permute-start | bytes 319496 | tf_op jit(solution)/shard_map/ppermute | solution.py:379
  49.9 3.5 %collective-permute-done.13.refs_1_ = bf16[688,128]{1,0:T(8,128)(2,1)S(1)} collective-permute-done((bf16[688,128]{1,0:T(8,128)(2,1)S(1)}, bf16[688,128]{1,0:T(8,128)(2,1)S(1)}, u32[]{:S(2)}, u32[]{:S(2)}) %collective-permute-start.13) | collective-permute-done | bytes 176160 | tf_op jit(solution)/shard_map/ppermute | solution.py:379
  54.6 5.1 %collective-permute-done.21.refs_7_ = bf16[416,128]{1,0:T(8,128)(2,1)S(1)} collective-permute-done((bf16[416,128]{1,0:T(8,128)(2,1)S(1)}, bf16[416,128]{1,0:T(8,128)(2,1)S(1)}, u32[]{:S(2)}, u32[]{:S(2)}) %collective-permute-start.21) | collective-permute-done | bytes 106528 | tf_op jit(solution)/shard_map/ppermute | solution.py:379
  60.6 1.5 %collective-permute-done.22.got_ref = bf16[1088,128]{1,0:T(8,128)(2,1)S(1)} collective-permute-done((bf16[1088,128]{1,0:T(8,128)(2,1)S(1)}, bf16[1088,128]{1,0:T(8,128)(2,1)S(1)}, u32[]{:S(2)}, u32[]{:S(2)}) %collective-permute-start.22) | collective-permute-done | bytes 278560 | tf_op jit(solution)/shard_map/ppermute | solution.py:383
  63.4 2.6 %collective-permute-start.24 = (bf16[272,128]{1,0:T(8,128)(2,1)S(1)}, bf16[272,128]{1,0:T(8,128)(2,1)S(1)}, u32[]{:S(2)}, u32[]{:S(2)}) collective-permute-start(bf16[272,128]{1,0:T(8,128)(2,1)S(1)} %get-tuple-element.49), channel_id=1, source_target_pairs={{0,3},{1,0},{2,1},{3,2},{4,7},{5,4},{6,5},{7,6},{8,11},{9,8},{10,9... | collective-permute-start | bytes 208904 | tf_op jit(solution)/shard_map/ppermute | solution.py:375
  67.2 2.8 %local_attention.1 = (f32[8,128,128]{2,1,0:T(8,128)S(1)}, f32[16,128]{1,0:T(8,128)S(1)}) custom-call(s32[8]{0:T(128)S(1)} %copy-done.8, bf16[8,128,128]{2,1,0:T(8,128)(2,1)S(1)} %bitcast.25, bf16[8,32,1024]{2,1,0:T(8,128)(2,1)S(1)} %copy-done.2, bf16[8,32,1024]{2,1,0:T(8,128)(2,1)S(1)} %copy-done.3, bf16[8,16,128]{2,1,0:T(8,128)(2,1)S(1)} %bitcast.26, ...), custom_call_target="tpu_custom_call" | custom-call | tf_op jit(solution)/shard_map/local_attention/pallas_call | solution.py:89
  70.0 1.8 %collective-permute-done.25.refs_3_ = bf16[272,128]{1,0:T(8,128)(2,1)S(1)} collective-permute-done((bf16[272,128]{1,0:T(8,128)(2,1)S(1)}, bf16[272,128]{1,0:T(8,128)(2,1)S(1)}, u32[]{:S(2)}, u32[]{:S(2)}) %collective-permute-start.25) | collective-permute-done | bytes 69664 | tf_op jit(solution)/shard_map/ppermute | solution.py:375
  71.9 1.5 %combine_parts.1 = bf16[8,128,128]{2,1,0:T(8,128)(2,1)} custom-call(s32[1]{0:T(128)} %bitcast.x_ref, bf16[272,128]{1,0:T(8,128)(2,1)S(1)} %get-tuple-element.47.refs_0_, bf16[272,128]{1,0:T(8,128)(2,1)S(1)} %collective-permute-done.23.refs_1_, bf16[272,128]{1,0:T(8,128)(2,1)S(1)} %collective-permute-done.24.refs_2_, ...), custom_call_target="tpu_custom_call" | custom-call | tf_op jit(solution)/shard_map/combine_parts/pallas_call | solution.py:363
  (72 shorter events, 10.7 us)
Async XLA Ops:
  2.7 11.2 %collective-permute-start.9 = (bf16[1040,128]{1,0:T(8,128)(2,1)S(1)}, bf16[1040,128]{1,0:T(8,128)(2,1)S(1)}, u32[]{:S(2)}, u32[]{:S(2)}) collective-permute-start(bf16[1040,128]{1,0:T(8,128)(2,1)S(1)} %build_cache.1.refs_4_), channel_id=1, source_target_pairs={{0,4},{4,0},{1,5},{5,1},{2,6},{6,2},{3,7},{7,3},{8,12},{12,8},{9,1... | collective-permute-start | bytes 798728 | tf_op jit(solution)/shard_map/ppermute | solution.py:383
  2.8 11.1 %collective-permute-start.8 = (bf16[1040,128]{1,0:T(8,128)(2,1)S(1)}, bf16[1040,128]{1,0:T(8,128)(2,1)S(1)}, u32[]{:S(2)}, u32[]{:S(2)}) collective-permute-start(bf16[1040,128]{1,0:T(8,128)(2,1)S(1)} %build_cache.1.refs_4_), channel_id=1, source_target_pairs={{0,32},{4,228},{32,64},{36,4},{64,96},{68,36},{96,128},{100,68},{1... | collective-permute-start | bytes 798728 | tf_op jit(solution)/shard_map/ppermute | solution.py:391
  4.8 7.3 %collective-permute-start = (s32[32]{0:T(128)S(1)}, s32[32]{0:T(128)S(1)}, u32[]{:S(2)}, u32[]{:S(2)}) collective-permute-start(s32[32]{0:T(128)S(1)} %bitcast.28), channel_id=1, source_target_pairs={{0,4},{4,0},{1,5},{5,1},{2,6},{6,2},{3,7},{7,3},{8,12},{12,8},{9,1... | collective-permute-start | bytes 392 | tf_op jit(solution)/shard_map/ppermute | solution.py:383
  8.9 5.5 %collective-permute-start.1 = (bf16[256,128]{1,0:T(8,128)(2,1)S(1)}, bf16[256,128]{1,0:T(8,128)(2,1)S(1)}, u32[]{:S(2)}, u32[]{:S(2)}) collective-permute-start(bf16[256,128]{1,0:T(8,128)(2,1)S(1)} %get-tuple-element.30), channel_id=1, source_target_pairs={{0,1},{1,2},{2,3},{3,0},{4,5},{5,6},{6,7},{7,4},{8,9},{9,10},{10,1... | collective-permute-start | bytes 196616 | tf_op jit(solution)/shard_map/ppermute | solution.py:375
  12.1 5.8 %collective-permute-start.3 = (bf16[256,128]{1,0:T(8,128)(2,1)S(1)}, bf16[256,128]{1,0:T(8,128)(2,1)S(1)}, u32[]{:S(2)}, u32[]{:S(2)}) collective-permute-start(bf16[256,128]{1,0:T(8,128)(2,1)S(1)} %get-tuple-element.32), channel_id=1, source_target_pairs={{0,2},{1,3},{2,0},{3,1},{4,6},{5,7},{6,4},{7,5},{8,10},{9,11},{10,... | collective-permute-start | bytes 196616 | tf_op jit(solution)/shard_map/ppermute | solution.py:375
  13.9 7.6 %collective-permute-start.10 = (bf16[1040,128]{1,0:T(8,128)(2,1)S(1)}, bf16[1040,128]{1,0:T(8,128)(2,1)S(1)}, u32[]{:S(2)}, u32[]{:S(2)}) collective-permute-start(bf16[1040,128]{1,0:T(8,128)(2,1)S(1)} %collective-permute-done.9), channel_id=1, source_target_pairs={{0,32},{4,228},{32,64},{36,4},{64,96},{68,36},{96,128},{100,68},{1... | collective-permute-start | bytes 798728 | tf_op jit(solution)/shard_map/ppermute | solution.py:391
  13.9 10.5 %collective-permute-start.11 = (bf16[1040,128]{1,0:T(8,128)(2,1)S(1)}, bf16[1040,128]{1,0:T(8,128)(2,1)S(1)}, u32[]{:S(2)}, u32[]{:S(2)}) collective-permute-start(bf16[1040,128]{1,0:T(8,128)(2,1)S(1)} %collective-permute-done.8.refs_5_), channel_id=1, source_target_pairs={{0,32},{4,228},{32,64},{36,4},{64,96},{68,36},{96,128},{100,68},{1... | collective-permute-start | bytes 798728 | tf_op jit(solution)/shard_map/ppermute | solution.py:391
  17.9 6.5 %collective-permute-start.4 = (bf16[1024,128]{1,0:T(8,128)(2,1)S(1)}, bf16[1024,128]{1,0:T(8,128)(2,1)S(1)}, u32[]{:S(2)}, u32[]{:S(2)}) collective-permute-start(bf16[1024,128]{1,0:T(8,128)(2,1)S(1)} %stack_queries.1.own_ref), channel_id=1, source_target_pairs={{0,4},{4,0},{1,5},{5,1},{2,6},{6,2},{3,7},{7,3},{8,12},{12,8},{9,1... | collective-permute-start | bytes 786440 | tf_op jit(solution)/shard_map/ppermute | solution.py:383
  21.6 7.6 %collective-permute-start.12 = (bf16[1040,128]{1,0:T(8,128)(2,1)S(1)}, bf16[1040,128]{1,0:T(8,128)(2,1)S(1)}, u32[]{:S(2)}, u32[]{:S(2)}) collective-permute-start(bf16[1040,128]{1,0:T(8,128)(2,1)S(1)} %collective-permute-done.10.refs_6_), channel_id=1, source_target_pairs={{0,32},{4,228},{32,64},{36,4},{64,96},{68,36},{96,128},{100,68},{1... | collective-permute-start | bytes 798728 | tf_op jit(solution)/shard_map/ppermute | solution.py:391
  24.4 7.6 %collective-permute-start.16 = (bf16[1040,128]{1,0:T(8,128)(2,1)S(1)}, bf16[1040,128]{1,0:T(8,128)(2,1)S(1)}, u32[]{:S(2)}, u32[]{:S(2)}) collective-permute-start(bf16[1040,128]{1,0:T(8,128)(2,1)S(1)} %collective-permute-done.11.refs_7_), channel_id=1, source_target_pairs={{0,32},{4,228},{32,64},{36,4},{64,96},{68,36},{96,128},{100,68},{1... | collective-permute-start | bytes 798728 | tf_op jit(solution)/shard_map/ppermute | solution.py:391
  25.4 9.3 %collective-permute-start.5 = (bf16[1024,128]{1,0:T(8,128)(2,1)S(1)}, bf16[1024,128]{1,0:T(8,128)(2,1)S(1)}, u32[]{:S(2)}, u32[]{:S(2)}) collective-permute-start(bf16[1024,128]{1,0:T(8,128)(2,1)S(1)} %get-tuple-element.34), channel_id=1, source_target_pairs={{0,8},{8,16},{16,24},{24,0},{1,9},{9,17},{17,25},{25,1},{2,10},{10... | collective-permute-start | bytes 786440 | tf_op jit(solution)/shard_map/ppermute | solution.py:379
  25.7 13.6 %collective-permute-start.6 = (bf16[1024,128]{1,0:T(8,128)(2,1)S(1)}, bf16[1024,128]{1,0:T(8,128)(2,1)S(1)}, u32[]{:S(2)}, u32[]{:S(2)}) collective-permute-start(bf16[1024,128]{1,0:T(8,128)(2,1)S(1)} %get-tuple-element.35), channel_id=1, source_target_pairs={{0,24},{8,0},{16,8},{24,16},{1,25},{9,1},{17,9},{25,17},{2,26},{10... | collective-permute-start | bytes 786440 | tf_op jit(solution)/shard_map/ppermute | solution.py:379
  27.5 11.8 %collective-permute-start.7 = (bf16[1024,128]{1,0:T(8,128)(2,1)S(1)}, bf16[1024,128]{1,0:T(8,128)(2,1)S(1)}, u32[]{:S(2)}, u32[]{:S(2)}) collective-permute-start(bf16[1024,128]{1,0:T(8,128)(2,1)S(1)} %get-tuple-element.36), channel_id=1, source_target_pairs={{0,16},{8,24},{16,0},{24,8},{1,17},{9,25},{17,1},{25,9},{2,18},{10... | collective-permute-start | bytes 786440 | tf_op jit(solution)/shard_map/ppermute | solution.py:379
  29.2 16.1 %collective-permute-start.17 = (bf16[1040,128]{1,0:T(8,128)(2,1)S(1)}, bf16[1040,128]{1,0:T(8,128)(2,1)S(1)}, u32[]{:S(2)}, u32[]{:S(2)}) collective-permute-start(bf16[1040,128]{1,0:T(8,128)(2,1)S(1)} %collective-permute-done.12.refs_8_), channel_id=1, source_target_pairs={{0,32},{4,228},{32,64},{36,4},{64,96},{68,36},{96,128},{100,68},{1... | collective-permute-start | bytes 798728 | tf_op jit(solution)/shard_map/ppermute | solution.py:391
  32.0 13.3 %collective-permute-start.18 = (bf16[1040,128]{1,0:T(8,128)(2,1)S(1)}, bf16[1040,128]{1,0:T(8,128)(2,1)S(1)}, u32[]{:S(2)}, u32[]{:S(2)}) collective-permute-start(bf16[1040,128]{1,0:T(8,128)(2,1)S(1)} %collective-permute-done.16.refs_4_), channel_id=1, source_target_pairs={{0,32},{4,228},{32,64},{36,4},{64,96},{68,36},{96,128},{100,68},{1... | collective-permute-start | bytes 798728 | tf_op jit(solution)/shard_map/ppermute | solution.py:391
  41.2 12.3 %collective-permute-start.13 = (bf16[688,128]{1,0:T(8,128)(2,1)S(1)}, bf16[688,128]{1,0:T(8,128)(2,1)S(1)}, u32[]{:S(2)}, u32[]{:S(2)}) collective-permute-start(bf16[688,128]{1,0:T(8,128)(2,1)S(1)} %get-tuple-element.38), channel_id=1, source_target_pairs={{0,24},{8,0},{16,8},{24,16},{1,25},{9,1},{17,9},{25,17},{2,26},{10... | collective-permute-start | bytes 528392 | tf_op jit(solution)/shard_map/ppermute | solution.py:379
  41.3 13.1 %collective-permute-start.14 = (bf16[688,128]{1,0:T(8,128)(2,1)S(1)}, bf16[688,128]{1,0:T(8,128)(2,1)S(1)}, u32[]{:S(2)}, u32[]{:S(2)}) collective-permute-start(bf16[688,128]{1,0:T(8,128)(2,1)S(1)} %get-tuple-element.39), channel_id=1, source_target_pairs={{0,8},{8,16},{16,24},{24,0},{1,9},{9,17},{17,25},{25,1},{2,10},{10... | collective-permute-start | bytes 528392 | tf_op jit(solution)/shard_map/ppermute | solution.py:379
  44.6 9.9 %collective-permute-start.15 = (bf16[688,128]{1,0:T(8,128)(2,1)S(1)}, bf16[688,128]{1,0:T(8,128)(2,1)S(1)}, u32[]{:S(2)}, u32[]{:S(2)}) collective-permute-start(bf16[688,128]{1,0:T(8,128)(2,1)S(1)} %get-tuple-element.40), channel_id=1, source_target_pairs={{0,16},{8,24},{16,0},{24,8},{1,17},{9,25},{17,1},{25,9},{2,18},{10... | collective-permute-start | bytes 528392 | tf_op jit(solution)/shard_map/ppermute | solution.py:379
  46.6 8.0 %collective-permute-start.19 = (bf16[416,128]{1,0:T(8,128)(2,1)S(1)}, bf16[416,128]{1,0:T(8,128)(2,1)S(1)}, u32[]{:S(2)}, u32[]{:S(2)}) collective-permute-start(bf16[416,128]{1,0:T(8,128)(2,1)S(1)} %get-tuple-element.42), channel_id=1, source_target_pairs={{0,24},{8,0},{16,8},{24,16},{1,25},{9,1},{17,9},{25,17},{2,26},{10... | collective-permute-start | bytes 319496 | tf_op jit(solution)/shard_map/ppermute | solution.py:379
  47.0 7.6 %collective-permute-start.20 = (bf16[416,128]{1,0:T(8,128)(2,1)S(1)}, bf16[416,128]{1,0:T(8,128)(2,1)S(1)}, u32[]{:S(2)}, u32[]{:S(2)}) collective-permute-start(bf16[416,128]{1,0:T(8,128)(2,1)S(1)} %get-tuple-element.43), channel_id=1, source_target_pairs={{0,8},{8,16},{16,24},{24,0},{1,9},{9,17},{17,25},{25,1},{2,10},{10... | collective-permute-start | bytes 319496 | tf_op jit(solution)/shard_map/ppermute | solution.py:379
  53.4 6.2 %collective-permute-start.21 = (bf16[416,128]{1,0:T(8,128)(2,1)S(1)}, bf16[416,128]{1,0:T(8,128)(2,1)S(1)}, u32[]{:S(2)}, u32[]{:S(2)}) collective-permute-start(bf16[416,128]{1,0:T(8,128)(2,1)S(1)} %get-tuple-element.44), channel_id=1, source_target_pairs={{0,16},{8,24},{16,0},{24,8},{1,17},{9,25},{17,1},{25,9},{2,18},{10... | collective-permute-start | bytes 319496 | tf_op jit(solution)/shard_map/ppermute | solution.py:379
  62.7 7.3 %collective-permute-start.23 = (bf16[272,128]{1,0:T(8,128)(2,1)S(1)}, bf16[272,128]{1,0:T(8,128)(2,1)S(1)}, u32[]{:S(2)}, u32[]{:S(2)}) collective-permute-start(bf16[272,128]{1,0:T(8,128)(2,1)S(1)} %get-tuple-element.48), channel_id=1, source_target_pairs={{0,1},{1,2},{2,3},{3,0},{4,5},{5,6},{6,7},{7,4},{8,9},{9,10},{10,1... | collective-permute-start | bytes 208904 | tf_op jit(solution)/shard_map/ppermute | solution.py:375
  63.4 6.6 %collective-permute-start.24 = (bf16[272,128]{1,0:T(8,128)(2,1)S(1)}, bf16[272,128]{1,0:T(8,128)(2,1)S(1)}, u32[]{:S(2)}, u32[]{:S(2)}) collective-permute-start(bf16[272,128]{1,0:T(8,128)(2,1)S(1)} %get-tuple-element.49), channel_id=1, source_target_pairs={{0,3},{1,0},{2,1},{3,2},{4,7},{5,4},{6,5},{7,6},{8,11},{9,8},{10,9... | collective-permute-start | bytes 208904 | tf_op jit(solution)/shard_map/ppermute | solution.py:375
  66.1 5.8 %collective-permute-start.25 = (bf16[272,128]{1,0:T(8,128)(2,1)S(1)}, bf16[272,128]{1,0:T(8,128)(2,1)S(1)}, u32[]{:S(2)}, u32[]{:S(2)}) collective-permute-start(bf16[272,128]{1,0:T(8,128)(2,1)S(1)} %get-tuple-element.50), channel_id=1, source_target_pairs={{0,2},{1,3},{2,0},{3,1},{4,6},{5,7},{6,4},{7,5},{8,10},{9,11},{10,... | collective-permute-start | bytes 208904 | tf_op jit(solution)/shard_map/ppermute | solution.py:375
  (12 other events, 38.9 us)

commit v6 on v4

--- a/solution.py
+++ b/solution.py
@@ -339,6 +339,7 @@
 
 def combine_kernel(x_ref, *refs):
     parts, (local_ref, stat_ref, out_ref, weight_ref) = refs[:X], refs[X:]
+    parts = [parts[TURNS.index(s)] for s in range(X)]
     wide = HELD * ROWS
     lane_head = iota((LOCAL, HEAD_DIM), 1) // ROWS
     heads = [lax.rem(x_ref[0] + (X - s), X) * HELD for s in range(X)]
@@ -471,18 +472,20 @@
     for results in (early, late):
         parts += [results[0]] + [shift(results[s], -TURNS[s]) for s in range(1, Y)]
 
+    local_queries, parts[Y] = lax.optimization_barrier((head_rows(queries), parts[Y]))
     local_out, stats = attend_local(
         suffix_length,
-        head_rows(queries),
+        local_queries,
         suffix_keys,
         suffix_values,
         head_rows(new_keys),
         head_rows(new_values),
     )
+    *parts, local_out, stats = lax.optimization_barrier((*parts, local_out, stats))
     own_back, other_back = unpack(jnp.where(ours, place, 0), line, parts)
     pieces = merge(ours.astype(jnp.int32), own_back, swap_cores(other_back))
     got = [pieces[0]] + [turn_x(pieces[s], s) for s in range(1, X)]
-    out = combine(at_x, got, local_out, stats)
+    out = combine(at_x, [got[s] for s in TURNS], local_out, stats)
     out = out.reshape(LOCAL, HEADS, STEPS, HEAD_DIM).transpose(0, 2, 1, 3)
     return out.reshape(LOCAL, STEPS, HEADS * HEAD_DIM)
 

time: 72.7 us -> 72 us (level)
  the two profiles are of different devices: /device:TPU:24 before, /device:TPU:6 now
where the time goes in v6:
time: 72 us; the launch traced here: 70.8 us
  starting transfers between devices  28.7 us (40%)
  waiting for transfers between devices  25.5 us (35%)
  Pallas kernels  13 us (18%)
  local copies, waits for them, and re-layouts  2.28 us (3%)
  between operations  0.85 us (1%)
    ppermute x9, starting transfers between devices, shift(): return lax.ppermute(value, 'y', [(i, (i + turns) % Y) for i in range(Y)])  13 us
    ppermute x9, waiting for transfers between devices, shift(): return lax.ppermute(value, 'y', [(i, (i + turns) % Y) for i in range(Y)])  9.68 us
    ppermute x6, starting transfers between devices, turn_x(): return lax.ppermute(value, 'x', [(i, (i + turns) % X) for i in range(X)])  8.26 us
    ppermute x7, waiting for transfers between devices, onward(): return lax.ppermute(value, ('z', 'core'), pairs)  7.84 us
    ppermute x6, waiting for transfers between devices, turn_x(): return lax.ppermute(value, 'x', [(i, (i + turns) % X) for i in range(X)])  6.47 us
    pallas_call x2, Pallas kernels, attend_prefix(): pl.pallas_call(functools.partial(prefix_kernel, first, count), out_shape=...  4.58 us
    ppermute x4, starting transfers between devices, swap_cores(): return lax.ppermute(value, 'core', [(i, 1 - i) for i in range(CORES)])  4.36 us
    ppermute x7, starting transfers between devices, onward(): return lax.ppermute(value, ('z', 'core'), pairs)  3.09 us
  transfers between devices with their start and end apart: 26, of which 14 were waited for; matrix products, arithmetic and copies ran while one was open for 1% of the time, Pallas kernels for 13%

profile of v6, /device:TPU:6, one launch (start us, length us, event | category | flops | bytes accessed | tf_op | source)
XLA Modules:
  0.0 70.8 jit_solution(18078932260809875815)
XLA Ops:
  2.8 2.0 %collective-permute-start.8 = (bf16[1040,128]{1,0:T(8,128)(2,1)S(1)}, bf16[1040,128]{1,0:T(8,128)(2,1)S(1)}, u32[]{:S(2)}, u32[]{:S(2)}) collective-permute-start(bf16[1040,128]{1,0:T(8,128)(2,1)S(1)} %build_cache.1.refs_4_), channel_id=1, source_target_pairs={{0,32},{4,228},{32,64},{36,4},{64,96},{68,36},{96,128},{100,68},{1... | collective-permute-start | bytes 798728 | tf_op jit(solution)/shard_map/ppermute | solution.py:402
  4.8 4.1 %collective-permute-start = (s32[32]{0:T(128)S(1)}, s32[32]{0:T(128)S(1)}, u32[]{:S(2)}, u32[]{:S(2)}) collective-permute-start(s32[32]{0:T(128)S(1)} %bitcast.28), channel_id=1, source_target_pairs={{0,4},{4,0},{1,5},{5,1},{2,6},{6,2},{3,7},{7,3},{8,12},{12,8},{9,1... | collective-permute-start | bytes 392 | tf_op jit(solution)/shard_map/ppermute | solution.py:394
  10.8 2.1 %collective-permute-start.3 = (bf16[256,128]{1,0:T(8,128)(2,1)S(1)}, bf16[256,128]{1,0:T(8,128)(2,1)S(1)}, u32[]{:S(2)}, u32[]{:S(2)}) collective-permute-start(bf16[256,128]{1,0:T(8,128)(2,1)S(1)} %get-tuple-element.44), channel_id=1, source_target_pairs={{0,1},{1,2},{2,3},{3,0},{4,5},{5,6},{6,7},{7,4},{8,9},{9,10},{10,1... | collective-permute-start | bytes 196616 | tf_op jit(solution)/shard_map/ppermute | solution.py:386
  13.4 2.3 %collective-permute-done.1.refs_1_ = bf16[256,128]{1,0:T(8,128)(2,1)S(1)} collective-permute-done((bf16[256,128]{1,0:T(8,128)(2,1)S(1)}, bf16[256,128]{1,0:T(8,128)(2,1)S(1)}, u32[]{:S(2)}, u32[]{:S(2)}) %collective-permute-start.1) | collective-permute-done | bytes 65568 | tf_op jit(solution)/shard_map/ppermute | solution.py:386
  16.4 4.2 %collective-permute-done.10.refs_6_ = bf16[1040,128]{1,0:T(8,128)(2,1)S(1)} collective-permute-done((bf16[1040,128]{1,0:T(8,128)(2,1)S(1)}, bf16[1040,128]{1,0:T(8,128)(2,1)S(1)}, u32[]{:S(2)}, u32[]{:S(2)}) %collective-permute-start.10) | collective-permute-done | bytes 266272 | tf_op jit(solution)/shard_map/ppermute | solution.py:402
  20.5 2.8 %collective-permute-done.11.refs_7_ = bf16[1040,128]{1,0:T(8,128)(2,1)S(1)} collective-permute-done((bf16[1040,128]{1,0:T(8,128)(2,1)S(1)}, bf16[1040,128]{1,0:T(8,128)(2,1)S(1)}, u32[]{:S(2)}, u32[]{:S(2)}) %collective-permute-start.11) | collective-permute-done | bytes 266272 | tf_op jit(solution)/shard_map/ppermute | solution.py:402
  23.4 1.6 %pack_queries.1 = (bf16[1024,128]{1,0:T(8,128)(2,1)S(1)}, bf16[1024,128]{1,0:T(8,128)(2,1)}, bf16[1024,128]{1,0:T(8,128)(2,1)S(1)}, bf16[1024,128]{1,0:T(8,128)(2,1)S(1)}) custom-call(s32[64]{0:T(128)S(1)} %get-tuple-element.77.place_ref, bf16[1024,128]{1,0:T(8,128)(2,1)S(1)} %stack_queries.1.own_ref, bf16[1024,128]{1,0:T(8,128)(2,1)S(1)} %collective-permute-done.4.other_ref), custom_call_target="tpu_custom_call" | custom-call | tf_op jit(solution)/shard_map/pack_queries/pallas_call | solution.py:201
  25.0 1.6 %collective-permute-start.5 = (bf16[1024,128]{1,0:T(8,128)(2,1)}, bf16[1024,128]{1,0:T(8,128)(2,1)S(1)}, u32[]{:S(2)}, u32[]{:S(2)}) collective-permute-start(bf16[1024,128]{1,0:T(8,128)(2,1)} %get-tuple-element.46), channel_id=1, source_target_pairs={{0,8},{8,16},{16,24},{24,0},{1,9},{9,17},{17,25},{25,1},{2,10},{10... | collective-permute-start | bytes 786440 | tf_op jit(solution)/shard_map/ppermute | solution.py:390
  26.6 1.7 %collective-permute-start.6 = (bf16[1024,128]{1,0:T(8,128)(2,1)S(1)}, bf16[1024,128]{1,0:T(8,128)(2,1)S(1)}, u32[]{:S(2)}, u32[]{:S(2)}) collective-permute-start(bf16[1024,128]{1,0:T(8,128)(2,1)S(1)} %get-tuple-element.47), channel_id=1, source_target_pairs={{0,24},{8,0},{16,8},{24,16},{1,25},{9,1},{17,9},{25,17},{2,26},{10... | collective-permute-start | bytes 786440 | tf_op jit(solution)/shard_map/ppermute | solution.py:390
  28.2 2.0 %collective-permute-start.7 = (bf16[1024,128]{1,0:T(8,128)(2,1)S(1)}, bf16[1024,128]{1,0:T(8,128)(2,1)S(1)}, u32[]{:S(2)}, u32[]{:S(2)}) collective-permute-start(bf16[1024,128]{1,0:T(8,128)(2,1)S(1)} %get-tuple-element.48), channel_id=1, source_target_pairs={{0,16},{8,24},{16,0},{24,8},{1,17},{9,25},{17,1},{25,9},{2,18},{10... | collective-permute-start | bytes 786440 | tf_op jit(solution)/shard_map/ppermute | solution.py:390
  32.1 2.4 %collective-permute-done.5.refs_1_ = bf16[1024,128]{1,0:T(8,128)(2,1)S(1)} collective-permute-done((bf16[1024,128]{1,0:T(8,128)(2,1)}, bf16[1024,128]{1,0:T(8,128)(2,1)S(1)}, u32[]{:S(2)}, u32[]{:S(2)}) %collective-permute-start.5) | collective-permute-done | bytes 262176 | tf_op jit(solution)/shard_map/ppermute | solution.py:390
  34.5 1.3 %collective-permute-done.6.refs_2_ = bf16[1024,128]{1,0:T(8,128)(2,1)S(1)} collective-permute-done((bf16[1024,128]{1,0:T(8,128)(2,1)S(1)}, bf16[1024,128]{1,0:T(8,128)(2,1)S(1)}, u32[]{:S(2)}, u32[]{:S(2)}) %collective-permute-start.6) | collective-permute-done | bytes 262176 | tf_op jit(solution)/shard_map/ppermute | solution.py:390
  35.8 4.4 %collective-permute-done.7.refs_3_ = bf16[1024,128]{1,0:T(8,128)(2,1)S(1)} collective-permute-done((bf16[1024,128]{1,0:T(8,128)(2,1)S(1)}, bf16[1024,128]{1,0:T(8,128)(2,1)S(1)}, u32[]{:S(2)}, u32[]{:S(2)}) %collective-permute-start.7) | collective-permute-done | bytes 262176 | tf_op jit(solution)/shard_map/ppermute | solution.py:390
  40.2 2.6 %prefix_attention_0.1 = (bf16[688,128]{1,0:T(8,128)(2,1)S(1)}, bf16[688,128]{1,0:T(8,128)(2,1)S(1)}, bf16[688,128]{1,0:T(8,128)(2,1)}, bf16[688,128]{1,0:T(8,128)(2,1)}) custom-call(bf16[1024,128]{1,0:T(8,128)(2,1)S(1)} %get-tuple-element.45.refs_0_, bf16[1024,128]{1,0:T(8,128)(2,1)S(1)} %collective-permute-done.5.refs_1_, ...), custom_call_target="tpu_custom_call" | custom-call | tf_op jit(solution)/shard_map/prefix_attention_0/pallas_call | solution.py:259
  42.8 1.6 %collective-permute-start.13 = (bf16[688,128]{1,0:T(8,128)(2,1)S(1)}, bf16[688,128]{1,0:T(8,128)(2,1)S(1)}, u32[]{:S(2)}, u32[]{:S(2)}) collective-permute-start(bf16[688,128]{1,0:T(8,128)(2,1)S(1)} %get-tuple-element.50), channel_id=1, source_target_pairs={{0,24},{8,0},{16,8},{24,16},{1,25},{9,1},{17,9},{25,17},{2,26},{10... | collective-permute-start | bytes 528392 | tf_op jit(solution)/shard_map/ppermute | solution.py:390
  46.0 2.0 %prefix_attention_5.1 = (bf16[416,128]{1,0:T(8,128)(2,1)S(1)}, bf16[416,128]{1,0:T(8,128)(2,1)}, bf16[416,128]{1,0:T(8,128)(2,1)}, bf16[416,128]{1,0:T(8,128)(2,1)S(1)}) custom-call(bf16[1024,128]{1,0:T(8,128)(2,1)S(1)} %get-tuple-element.45.refs_0_, bf16[1024,128]{1,0:T(8,128)(2,1)S(1)} %collective-permute-done.5.refs_1_, ...), custom_call_target="tpu_custom_call" | custom-call | tf_op jit(solution)/shard_map/prefix_attention_5/pallas_call | solution.py:259
  48.0 2.5 %collective-permute-start.19 = (bf16[416,128]{1,0:T(8,128)(2,1)}, bf16[416,128]{1,0:T(8,128)(2,1)S(1)}, u32[]{:S(2)}, u32[]{:S(2)}) collective-permute-start(bf16[416,128]{1,0:T(8,128)(2,1)} %get-tuple-element.55), channel_id=1, source_target_pairs={{0,24},{8,0},{16,8},{24,16},{1,25},{9,1},{17,9},{25,17},{2,26},{10... | collective-permute-start | bytes 319496 | tf_op jit(solution)/shard_map/ppermute | solution.py:390
  50.6 2.1 %collective-permute-start.21 = (bf16[416,128]{1,0:T(8,128)(2,1)S(1)}, bf16[416,128]{1,0:T(8,128)(2,1)S(1)}, u32[]{:S(2)}, u32[]{:S(2)}) collective-permute-start(bf16[416,128]{1,0:T(8,128)(2,1)S(1)} %get-tuple-element.57), channel_id=1, source_target_pairs={{0,16},{8,24},{16,0},{24,8},{1,17},{9,25},{17,1},{25,9},{2,18},{10... | collective-permute-start | bytes 319496 | tf_op jit(solution)/shard_map/ppermute | solution.py:390
  53.4 2.8 %local_attention.1 = (f32[8,128,128]{2,1,0:T(8,128)S(1)}, f32[16,128]{1,0:T(8,128)S(1)}) custom-call(s32[8]{0:T(128)S(1)} %copy-done.8, bf16[8,128,128]{2,1,0:T(8,128)(2,1)S(1)} %bitcast.25, bf16[8,32,1024]{2,1,0:T(8,128)(2,1)S(1)} %copy-done.2, bf16[8,32,1024]{2,1,0:T(8,128)(2,1)S(1)} %copy-done.3, bf16[8,16,128]{2,1,0:T(8,128)(2,1)S(1)} %bitcast.26, ...), custom_call_target="tpu_custom_call" | custom-call | tf_op jit(solution)/shard_map/local_attention/pallas_call | solution.py:89
  56.2 1.6 %collective-permute-done.20.refs_6_ = bf16[416,128]{1,0:T(8,128)(2,1)S(1)} collective-permute-done((bf16[416,128]{1,0:T(8,128)(2,1)}, bf16[416,128]{1,0:T(8,128)(2,1)S(1)}, u32[]{:S(2)}, u32[]{:S(2)}) %collective-permute-start.20) | collective-permute-done | bytes 106528 | tf_op jit(solution)/shard_map/ppermute | solution.py:390
  59.1 1.5 %collective-permute-done.22.got_ref = bf16[1088,128]{1,0:T(8,128)(2,1)S(1)} collective-permute-done((bf16[1088,128]{1,0:T(8,128)(2,1)S(1)}, bf16[1088,128]{1,0:T(8,128)(2,1)S(1)}, u32[]{:S(2)}, u32[]{:S(2)}) %collective-permute-start.22) | collective-permute-done | bytes 278560 | tf_op jit(solution)/shard_map/ppermute | solution.py:394
  63.4 2.1 %collective-permute-start.25 = (bf16[272,128]{1,0:T(8,128)(2,1)S(1)}, bf16[272,128]{1,0:T(8,128)(2,1)S(1)}, u32[]{:S(2)}, u32[]{:S(2)}) collective-permute-start(bf16[272,128]{1,0:T(8,128)(2,1)S(1)} %get-tuple-element.74), channel_id=1, source_target_pairs={{0,2},{1,3},{2,0},{3,1},{4,6},{5,7},{6,4},{7,5},{8,10},{9,11},{10,... | collective-permute-start | bytes 208904 | tf_op jit(solution)/shard_map/ppermute | solution.py:386
  65.7 2.8 %collective-permute-done.24.refs_2_ = bf16[272,128]{1,0:T(8,128)(2,1)S(1)} collective-permute-done((bf16[272,128]{1,0:T(8,128)(2,1)S(1)}, bf16[272,128]{1,0:T(8,128)(2,1)S(1)}, u32[]{:S(2)}, u32[]{:S(2)}) %collective-permute-start.24) | collective-permute-done | bytes 69664 | tf_op jit(solution)/shard_map/ppermute | solution.py:386
  69.3 1.5 %combine_parts.1 = bf16[8,128,128]{2,1,0:T(8,128)(2,1)} custom-call(s32[1]{0:T(128)} %bitcast.x_ref, bf16[272,128]{1,0:T(8,128)(2,1)S(1)} %get-tuple-element.71.refs_0_, bf16[272,128]{1,0:T(8,128)(2,1)S(1)} %collective-permute-done.23.refs_1_, bf16[272,128]{1,0:T(8,128)(2,1)S(1)} %collective-permute-done.24.refs_2_, ...), custom_call_target="tpu_custom_call" | custom-call | tf_op jit(solution)/shard_map/combine_parts/pallas_call | solution.py:374
  (72 shorter events, 14.5 us)
Async XLA Ops:
  2.7 10.2 %collective-permute-start.9 = (bf16[1040,128]{1,0:T(8,128)(2,1)S(1)}, bf16[1040,128]{1,0:T(8,128)(2,1)S(1)}, u32[]{:S(2)}, u32[]{:S(2)}) collective-permute-start(bf16[1040,128]{1,0:T(8,128)(2,1)S(1)} %build_cache.1.refs_4_), channel_id=1, source_target_pairs={{0,4},{4,0},{1,5},{5,1},{2,6},{6,2},{3,7},{7,3},{8,12},{12,8},{9,1... | collective-permute-start | bytes 798728 | tf_op jit(solution)/shard_map/ppermute | solution.py:394
  2.8 10.3 %collective-permute-start.8 = (bf16[1040,128]{1,0:T(8,128)(2,1)S(1)}, bf16[1040,128]{1,0:T(8,128)(2,1)S(1)}, u32[]{:S(2)}, u32[]{:S(2)}) collective-permute-start(bf16[1040,128]{1,0:T(8,128)(2,1)S(1)} %build_cache.1.refs_4_), channel_id=1, source_target_pairs={{0,32},{4,228},{32,64},{36,4},{64,96},{68,36},{96,128},{100,68},{1... | collective-permute-start | bytes 798728 | tf_op jit(solution)/shard_map/ppermute | solution.py:402
  4.8 6.0 %collective-permute-start = (s32[32]{0:T(128)S(1)}, s32[32]{0:T(128)S(1)}, u32[]{:S(2)}, u32[]{:S(2)}) collective-permute-start(s32[32]{0:T(128)S(1)} %bitcast.28), channel_id=1, source_target_pairs={{0,4},{4,0},{1,5},{5,1},{2,6},{6,2},{3,7},{7,3},{8,12},{12,8},{9,1... | collective-permute-start | bytes 392 | tf_op jit(solution)/shard_map/ppermute | solution.py:394
  8.9 6.8 %collective-permute-start.1 = (bf16[256,128]{1,0:T(8,128)(2,1)S(1)}, bf16[256,128]{1,0:T(8,128)(2,1)S(1)}, u32[]{:S(2)}, u32[]{:S(2)}) collective-permute-start(bf16[256,128]{1,0:T(8,128)(2,1)S(1)} %get-tuple-element.42), channel_id=1, source_target_pairs={{0,3},{1,0},{2,1},{3,2},{4,7},{5,4},{6,5},{7,6},{8,11},{9,8},{10,9... | collective-permute-start | bytes 196616 | tf_op jit(solution)/shard_map/ppermute | solution.py:386
  9.7 5.9 %collective-permute-start.2 = (bf16[256,128]{1,0:T(8,128)(2,1)S(1)}, bf16[256,128]{1,0:T(8,128)(2,1)S(1)}, u32[]{:S(2)}, u32[]{:S(2)}) collective-permute-start(bf16[256,128]{1,0:T(8,128)(2,1)S(1)} %get-tuple-element.43), channel_id=1, source_target_pairs={{0,2},{1,3},{2,0},{3,1},{4,6},{5,7},{6,4},{7,5},{8,10},{9,11},{10,... | collective-permute-start | bytes 196616 | tf_op jit(solution)/shard_map/ppermute | solution.py:386
  10.8 5.2 %collective-permute-start.3 = (bf16[256,128]{1,0:T(8,128)(2,1)S(1)}, bf16[256,128]{1,0:T(8,128)(2,1)S(1)}, u32[]{:S(2)}, u32[]{:S(2)}) collective-permute-start(bf16[256,128]{1,0:T(8,128)(2,1)S(1)} %get-tuple-element.44), channel_id=1, source_target_pairs={{0,1},{1,2},{2,3},{3,0},{4,5},{5,6},{6,7},{7,4},{8,9},{9,10},{10,1... | collective-permute-start | bytes 196616 | tf_op jit(solution)/shard_map/ppermute | solution.py:386
  12.9 7.6 %collective-permute-start.10 = (bf16[1040,128]{1,0:T(8,128)(2,1)S(1)}, bf16[1040,128]{1,0:T(8,128)(2,1)S(1)}, u32[]{:S(2)}, u32[]{:S(2)}) collective-permute-start(bf16[1040,128]{1,0:T(8,128)(2,1)S(1)} %collective-permute-done.9), channel_id=1, source_target_pairs={{0,32},{4,228},{32,64},{36,4},{64,96},{68,36},{96,128},{100,68},{1... | collective-permute-start | bytes 798728 | tf_op jit(solution)/shard_map/ppermute | solution.py:402
  13.1 10.3 %collective-permute-start.11 = (bf16[1040,128]{1,0:T(8,128)(2,1)S(1)}, bf16[1040,128]{1,0:T(8,128)(2,1)S(1)}, u32[]{:S(2)}, u32[]{:S(2)}) collective-permute-start(bf16[1040,128]{1,0:T(8,128)(2,1)S(1)} %collective-permute-done.8.refs_5_), channel_id=1, source_target_pairs={{0,32},{4,228},{32,64},{36,4},{64,96},{68,36},{96,128},{100,68},{1... | collective-permute-start | bytes 798728 | tf_op jit(solution)/shard_map/ppermute | solution.py:402
  16.1 7.4 %collective-permute-start.4 = (bf16[1024,128]{1,0:T(8,128)(2,1)S(1)}, bf16[1024,128]{1,0:T(8,128)(2,1)S(1)}, u32[]{:S(2)}, u32[]{:S(2)}) collective-permute-start(bf16[1024,128]{1,0:T(8,128)(2,1)S(1)} %stack_queries.1.own_ref), channel_id=1, source_target_pairs={{0,4},{4,0},{1,5},{5,1},{2,6},{6,2},{3,7},{7,3},{8,12},{12,8},{9,1... | collective-permute-start | bytes 786440 | tf_op jit(solution)/shard_map/ppermute | solution.py:394
  20.5 9.8 %collective-permute-start.12 = (bf16[1040,128]{1,0:T(8,128)(2,1)S(1)}, bf16[1040,128]{1,0:T(8,128)(2,1)S(1)}, u32[]{:S(2)}, u32[]{:S(2)}) collective-permute-start(bf16[1040,128]{1,0:T(8,128)(2,1)S(1)} %collective-permute-done.10.refs_6_), channel_id=1, source_target_pairs={{0,32},{4,228},{32,64},{36,4},{64,96},{68,36},{96,128},{100,68},{1... | collective-permute-start | bytes 798728 | tf_op jit(solution)/shard_map/ppermute | solution.py:402
  23.4 7.6 %collective-permute-start.16 = (bf16[1040,128]{1,0:T(8,128)(2,1)S(1)}, bf16[1040,128]{1,0:T(8,128)(2,1)S(1)}, u32[]{:S(2)}, u32[]{:S(2)}) collective-permute-start(bf16[1040,128]{1,0:T(8,128)(2,1)S(1)} %collective-permute-done.11.refs_7_), channel_id=1, source_target_pairs={{0,32},{4,228},{32,64},{36,4},{64,96},{68,36},{96,128},{100,68},{1... | collective-permute-start | bytes 798728 | tf_op jit(solution)/shard_map/ppermute | solution.py:402
  25.0 9.5 %collective-permute-start.5 = (bf16[1024,128]{1,0:T(8,128)(2,1)}, bf16[1024,128]{1,0:T(8,128)(2,1)S(1)}, u32[]{:S(2)}, u32[]{:S(2)}) collective-permute-start(bf16[1024,128]{1,0:T(8,128)(2,1)} %get-tuple-element.46), channel_id=1, source_target_pairs={{0,8},{8,16},{16,24},{24,0},{1,9},{9,17},{17,25},{25,1},{2,10},{10... | collective-permute-start | bytes 786440 | tf_op jit(solution)/shard_map/ppermute | solution.py:390
  26.6 9.2 %collective-permute-start.6 = (bf16[1024,128]{1,0:T(8,128)(2,1)S(1)}, bf16[1024,128]{1,0:T(8,128)(2,1)S(1)}, u32[]{:S(2)}, u32[]{:S(2)}) collective-permute-start(bf16[1024,128]{1,0:T(8,128)(2,1)S(1)} %get-tuple-element.47), channel_id=1, source_target_pairs={{0,24},{8,0},{16,8},{24,16},{1,25},{9,1},{17,9},{25,17},{2,26},{10... | collective-permute-start | bytes 786440 | tf_op jit(solution)/shard_map/ppermute | solution.py:390
  28.2 12.0 %collective-permute-start.7 = (bf16[1024,128]{1,0:T(8,128)(2,1)S(1)}, bf16[1024,128]{1,0:T(8,128)(2,1)S(1)}, u32[]{:S(2)}, u32[]{:S(2)}) collective-permute-start(bf16[1024,128]{1,0:T(8,128)(2,1)S(1)} %get-tuple-element.48), channel_id=1, source_target_pairs={{0,16},{8,24},{16,0},{24,8},{1,17},{9,25},{17,1},{25,9},{2,18},{10... | collective-permute-start | bytes 786440 | tf_op jit(solution)/shard_map/ppermute | solution.py:390
  30.4 15.6 %collective-permute-start.17 = (bf16[1040,128]{1,0:T(8,128)(2,1)S(1)}, bf16[1040,128]{1,0:T(8,128)(2,1)S(1)}, u32[]{:S(2)}, u32[]{:S(2)}) collective-permute-start(bf16[1040,128]{1,0:T(8,128)(2,1)S(1)} %collective-permute-done.12.refs_8_), channel_id=1, source_target_pairs={{0,32},{4,228},{32,64},{36,4},{64,96},{68,36},{96,128},{100,68},{1... | collective-permute-start | bytes 798728 | tf_op jit(solution)/shard_map/ppermute | solution.py:402
  31.0 15.0 %collective-permute-start.18 = (bf16[1040,128]{1,0:T(8,128)(2,1)S(1)}, bf16[1040,128]{1,0:T(8,128)(2,1)S(1)}, u32[]{:S(2)}, u32[]{:S(2)}) collective-permute-start(bf16[1040,128]{1,0:T(8,128)(2,1)S(1)} %collective-permute-done.16.refs_4_), channel_id=1, source_target_pairs={{0,32},{4,228},{32,64},{36,4},{64,96},{68,36},{96,128},{100,68},{1... | collective-permute-start | bytes 798728 | tf_op jit(solution)/shard_map/ppermute | solution.py:402
  42.8 7.7 %collective-permute-start.13 = (bf16[688,128]{1,0:T(8,128)(2,1)S(1)}, bf16[688,128]{1,0:T(8,128)(2,1)S(1)}, u32[]{:S(2)}, u32[]{:S(2)}) collective-permute-start(bf16[688,128]{1,0:T(8,128)(2,1)S(1)} %get-tuple-element.50), channel_id=1, source_target_pairs={{0,24},{8,0},{16,8},{24,16},{1,25},{9,1},{17,9},{25,17},{2,26},{10... | collective-permute-start | bytes 528392 | tf_op jit(solution)/shard_map/ppermute | solution.py:390
  44.5 11.7 %collective-permute-start.14 = (bf16[688,128]{1,0:T(8,128)(2,1)}, bf16[688,128]{1,0:T(8,128)(2,1)S(1)}, u32[]{:S(2)}, u32[]{:S(2)}) collective-permute-start(bf16[688,128]{1,0:T(8,128)(2,1)} %get-tuple-element.51), channel_id=1, source_target_pairs={{0,8},{8,16},{16,24},{24,0},{1,9},{9,17},{17,25},{25,1},{2,10},{10... | collective-permute-start | bytes 528392 | tf_op jit(solution)/shard_map/ppermute | solution.py:390
  44.9 11.3 %collective-permute-start.15 = (bf16[688,128]{1,0:T(8,128)(2,1)}, bf16[688,128]{1,0:T(8,128)(2,1)}, u32[]{:S(2)}, u32[]{:S(2)}) collective-permute-start(bf16[688,128]{1,0:T(8,128)(2,1)} %get-tuple-element.52), channel_id=1, source_target_pairs={{0,16},{8,24},{16,0},{24,8},{1,17},{9,25},{17,1},{25,9},{2,18},{10... | collective-permute-start | bytes 528392 | tf_op jit(solution)/shard_map/ppermute | solution.py:390
  48.0 8.2 %collective-permute-start.19 = (bf16[416,128]{1,0:T(8,128)(2,1)}, bf16[416,128]{1,0:T(8,128)(2,1)S(1)}, u32[]{:S(2)}, u32[]{:S(2)}) collective-permute-start(bf16[416,128]{1,0:T(8,128)(2,1)} %get-tuple-element.55), channel_id=1, source_target_pairs={{0,24},{8,0},{16,8},{24,16},{1,25},{9,1},{17,9},{25,17},{2,26},{10... | collective-permute-start | bytes 319496 | tf_op jit(solution)/shard_map/ppermute | solution.py:390
  50.5 7.3 %collective-permute-start.20 = (bf16[416,128]{1,0:T(8,128)(2,1)}, bf16[416,128]{1,0:T(8,128)(2,1)S(1)}, u32[]{:S(2)}, u32[]{:S(2)}) collective-permute-start(bf16[416,128]{1,0:T(8,128)(2,1)} %get-tuple-element.56), channel_id=1, source_target_pairs={{0,8},{8,16},{16,24},{24,0},{1,9},{9,17},{17,25},{25,1},{2,10},{10... | collective-permute-start | bytes 319496 | tf_op jit(solution)/shard_map/ppermute | solution.py:390
  50.6 7.2 %collective-permute-start.21 = (bf16[416,128]{1,0:T(8,128)(2,1)S(1)}, bf16[416,128]{1,0:T(8,128)(2,1)S(1)}, u32[]{:S(2)}, u32[]{:S(2)}) collective-permute-start(bf16[416,128]{1,0:T(8,128)(2,1)S(1)} %get-tuple-element.57), channel_id=1, source_target_pairs={{0,16},{8,24},{16,0},{24,8},{1,17},{9,25},{17,1},{25,9},{2,18},{10... | collective-permute-start | bytes 319496 | tf_op jit(solution)/shard_map/ppermute | solution.py:390
  62.3 6.2 %collective-permute-start.24 = (bf16[272,128]{1,0:T(8,128)(2,1)S(1)}, bf16[272,128]{1,0:T(8,128)(2,1)S(1)}, u32[]{:S(2)}, u32[]{:S(2)}) collective-permute-start(bf16[272,128]{1,0:T(8,128)(2,1)S(1)} %get-tuple-element.73), channel_id=1, source_target_pairs={{0,3},{1,0},{2,1},{3,2},{4,7},{5,4},{6,5},{7,6},{8,11},{9,8},{10,9... | collective-permute-start | bytes 208904 | tf_op jit(solution)/shard_map/ppermute | solution.py:386
  63.4 5.9 %collective-permute-start.25 = (bf16[272,128]{1,0:T(8,128)(2,1)S(1)}, bf16[272,128]{1,0:T(8,128)(2,1)S(1)}, u32[]{:S(2)}, u32[]{:S(2)}) collective-permute-start(bf16[272,128]{1,0:T(8,128)(2,1)S(1)} %get-tuple-element.74), channel_id=1, source_target_pairs={{0,2},{1,3},{2,0},{3,1},{4,6},{5,7},{6,4},{7,5},{8,10},{9,11},{10,... | collective-permute-start | bytes 208904 | tf_op jit(solution)/shard_map/ppermute | solution.py:386
  (12 other events, 35.6 us)

commit v7 on v6

--- a/solution.py
+++ b/solution.py
@@ -23,7 +23,7 @@
 COLUMN = PEERS * LOCAL
 HELD = KV_HEADS // X
 OWNED = Z
-EARLY = 5
+EARLY = 4
 PER_GROUP = 4
 BLOCK = PER_GROUP * ROWS
 UNITS = OWNED * HELD
@@ -465,9 +465,9 @@
     packed = pack(jnp.where(ours, place, DUMP), own_queries, other_queries)
     received = [packed[0]] + [shift(packed[s], TURNS[s]) for s in range(1, Y)]
     own_3, other_2 = onward(own_2), onward(other_1)
-    early = attend_prefix(0, received, [mine, own_1, other_1, own_2, other_2])
+    early = attend_prefix(0, received, [mine, own_1, other_1, own_2])
     own_4, other_3 = onward(own_3), onward(other_2)
-    late = attend_prefix(EARLY, received, [own_3, other_3, own_4])
+    late = attend_prefix(EARLY, received, [other_2, own_3, other_3, own_4])
     parts = []
     for results in (early, late):
         parts += [results[0]] + [shift(results[s], -TURNS[s]) for s in range(1, Y)]

time: 72 us -> 72.8 us (1.011)
  Pallas kernels: 13 us -> 11.9 us
  waiting for transfers between devices: 25.5 us -> 26.5 us
    ppermute x9, waiting for transfers between devices: 9.68 us -> 10.7 us  [shift(): return lax.ppermute(value, 'y', [(i, (i + turns) % Y) for i in range(Y)])]
    pallas_call x2, Pallas kernels: 4.58 us -> 3.76 us  [attend_prefix(): pl.pallas_call(functools.partial(prefix_kernel, first, count), out_shape=...]
    unnamed x20 -> x22, local copies, waits for them, and re-layouts: 1.89 us -> 2.52 us
  transfers between devices with their start and end apart: 26 -> 26, of which waited for: 14 -> 14; matrix products, arithmetic and copies ran while one was open for 1% -> 1% of each run, Pallas kernels for 13% -> 11%
where the time goes in v7:
time: 72.8 us; the launch traced here: 71.7 us
  starting transfers between devices  29.1 us (40%)
  waiting for transfers between devices  26.5 us (36%)
  Pallas kernels  11.9 us (16%)
  local copies, waits for them, and re-layouts  2.91 us (4%)
  between operations  0.86 us (1%)
    ppermute x9, starting transfers between devices, shift(): return lax.ppermute(value, 'y', [(i, (i + turns) % Y) for i in range(Y)])  13.3 us
    ppermute x9, waiting for transfers between devices, shift(): return lax.ppermute(value, 'y', [(i, (i + turns) % Y) for i in range(Y)])  10.7 us
    ppermute x6, starting transfers between devices, turn_x(): return lax.ppermute(value, 'x', [(i, (i + turns) % X) for i in range(X)])  8.26 us
    ppermute x7, waiting for transfers between devices, onward(): return lax.ppermute(value, ('z', 'core'), pairs)  7.76 us
    ppermute x6, waiting for transfers between devices, turn_x(): return lax.ppermute(value, 'x', [(i, (i + turns) % X) for i in range(X)])  6.47 us
    ppermute x4, starting transfers between devices, swap_cores(): return lax.ppermute(value, 'core', [(i, 1 - i) for i in range(CORES)])  4.35 us
    pallas_call x2, Pallas kernels, attend_prefix(): pl.pallas_call(functools.partial(prefix_kernel, first, count), out_shape=...  3.76 us
    ppermute x7, starting transfers between devices, onward(): return lax.ppermute(value, ('z', 'core'), pairs)  3.17 us
  transfers between devices with their start and end apart: 26, of which 14 were waited for; matrix products, arithmetic and copies ran while one was open for 1% of the time, Pallas kernels for 11%

profile of v7, /device:TPU:6, one launch (start us, length us, event | category | flops | bytes accessed | tf_op | source)
XLA Modules:
  0.0 71.7 jit_solution(7910750196036690246)
XLA Ops:
  2.8 2.0 %collective-permute-start.8 = (bf16[1040,128]{1,0:T(8,128)(2,1)S(1)}, bf16[1040,128]{1,0:T(8,128)(2,1)S(1)}, u32[]{:S(2)}, u32[]{:S(2)}) collective-permute-start(bf16[1040,128]{1,0:T(8,128)(2,1)S(1)} %build_cache.1.refs_4_), channel_id=1, source_target_pairs={{0,32},{4,228},{32,64},{36,4},{64,96},{68,36},{96,128},{100,68},{1... | collective-permute-start | bytes 798728 | tf_op jit(solution)/shard_map/ppermute | solution.py:402
  4.8 4.1 %collective-permute-start = (s32[32]{0:T(128)S(1)}, s32[32]{0:T(128)S(1)}, u32[]{:S(2)}, u32[]{:S(2)}) collective-permute-start(s32[32]{0:T(128)S(1)} %bitcast.28), channel_id=1, source_target_pairs={{0,4},{4,0},{1,5},{5,1},{2,6},{6,2},{3,7},{7,3},{8,12},{12,8},{9,1... | collective-permute-start | bytes 392 | tf_op jit(solution)/shard_map/ppermute | solution.py:394
  10.8 2.1 %collective-permute-start.3 = (bf16[256,128]{1,0:T(8,128)(2,1)S(1)}, bf16[256,128]{1,0:T(8,128)(2,1)S(1)}, u32[]{:S(2)}, u32[]{:S(2)}) collective-permute-start(bf16[256,128]{1,0:T(8,128)(2,1)S(1)} %get-tuple-element.44), channel_id=1, source_target_pairs={{0,1},{1,2},{2,3},{3,0},{4,5},{5,6},{6,7},{7,4},{8,9},{9,10},{10,1... | collective-permute-start | bytes 196616 | tf_op jit(solution)/shard_map/ppermute | solution.py:386
  13.4 2.3 %collective-permute-done.1.refs_1_ = bf16[256,128]{1,0:T(8,128)(2,1)S(1)} collective-permute-done((bf16[256,128]{1,0:T(8,128)(2,1)S(1)}, bf16[256,128]{1,0:T(8,128)(2,1)S(1)}, u32[]{:S(2)}, u32[]{:S(2)}) %collective-permute-start.1) | collective-permute-done | bytes 65568 | tf_op jit(solution)/shard_map/ppermute | solution.py:386
  16.4 4.2 %collective-permute-done.10.refs_6_ = bf16[1040,128]{1,0:T(8,128)(2,1)S(1)} collective-permute-done((bf16[1040,128]{1,0:T(8,128)(2,1)S(1)}, bf16[1040,128]{1,0:T(8,128)(2,1)S(1)}, u32[]{:S(2)}, u32[]{:S(2)}) %collective-permute-start.10) | collective-permute-done | bytes 266272 | tf_op jit(solution)/shard_map/ppermute | solution.py:402
  20.5 2.8 %collective-permute-done.11.refs_7_ = bf16[1040,128]{1,0:T(8,128)(2,1)S(1)} collective-permute-done((bf16[1040,128]{1,0:T(8,128)(2,1)S(1)}, bf16[1040,128]{1,0:T(8,128)(2,1)S(1)}, u32[]{:S(2)}, u32[]{:S(2)}) %collective-permute-start.11) | collective-permute-done | bytes 266272 | tf_op jit(solution)/shard_map/ppermute | solution.py:402
  23.4 1.6 %pack_queries.1 = (bf16[1024,128]{1,0:T(8,128)(2,1)S(1)}, bf16[1024,128]{1,0:T(8,128)(2,1)}, bf16[1024,128]{1,0:T(8,128)(2,1)}, bf16[1024,128]{1,0:T(8,128)(2,1)S(1)}) custom-call(s32[64]{0:T(128)S(1)} %get-tuple-element.77.place_ref, bf16[1024,128]{1,0:T(8,128)(2,1)S(1)} %stack_queries.1.own_ref, bf16[1024,128]{1,0:T(8,128)(2,1)S(1)} %collective-permute-done.4.other_ref), custom_call_target="tpu_custom_call" | custom-call | tf_op jit(solution)/shard_map/pack_queries/pallas_call | solution.py:201
  25.1 1.6 %collective-permute-start.5 = (bf16[1024,128]{1,0:T(8,128)(2,1)}, bf16[1024,128]{1,0:T(8,128)(2,1)S(1)}, u32[]{:S(2)}, u32[]{:S(2)}) collective-permute-start(bf16[1024,128]{1,0:T(8,128)(2,1)} %get-tuple-element.46), channel_id=1, source_target_pairs={{0,8},{8,16},{16,24},{24,0},{1,9},{9,17},{17,25},{25,1},{2,10},{10... | collective-permute-start | bytes 786440 | tf_op jit(solution)/shard_map/ppermute | solution.py:390
  26.7 1.7 %collective-permute-start.6 = (bf16[1024,128]{1,0:T(8,128)(2,1)}, bf16[1024,128]{1,0:T(8,128)(2,1)S(1)}, u32[]{:S(2)}, u32[]{:S(2)}) collective-permute-start(bf16[1024,128]{1,0:T(8,128)(2,1)} %get-tuple-element.47), channel_id=1, source_target_pairs={{0,24},{8,0},{16,8},{24,16},{1,25},{9,1},{17,9},{25,17},{2,26},{10... | collective-permute-start | bytes 786440 | tf_op jit(solution)/shard_map/ppermute | solution.py:390
  28.3 2.0 %collective-permute-start.7 = (bf16[1024,128]{1,0:T(8,128)(2,1)S(1)}, bf16[1024,128]{1,0:T(8,128)(2,1)S(1)}, u32[]{:S(2)}, u32[]{:S(2)}) collective-permute-start(bf16[1024,128]{1,0:T(8,128)(2,1)S(1)} %get-tuple-element.48), channel_id=1, source_target_pairs={{0,16},{8,24},{16,0},{24,8},{1,17},{9,25},{17,1},{25,9},{2,18},{10... | collective-permute-start | bytes 786440 | tf_op jit(solution)/shard_map/ppermute | solution.py:390
  32.2 2.4 %collective-permute-done.5.refs_1_ = bf16[1024,128]{1,0:T(8,128)(2,1)S(1)} collective-permute-done((bf16[1024,128]{1,0:T(8,128)(2,1)}, bf16[1024,128]{1,0:T(8,128)(2,1)S(1)}, u32[]{:S(2)}, u32[]{:S(2)}) %collective-permute-start.5) | collective-permute-done | bytes 262176 | tf_op jit(solution)/shard_map/ppermute | solution.py:390
  34.6 1.5 %collective-permute-done.6.refs_2_ = bf16[1024,128]{1,0:T(8,128)(2,1)S(1)} collective-permute-done((bf16[1024,128]{1,0:T(8,128)(2,1)}, bf16[1024,128]{1,0:T(8,128)(2,1)S(1)}, u32[]{:S(2)}, u32[]{:S(2)}) %collective-permute-start.6) | collective-permute-done | bytes 262176 | tf_op jit(solution)/shard_map/ppermute | solution.py:390
  36.1 4.2 %collective-permute-done.7.refs_3_ = bf16[1024,128]{1,0:T(8,128)(2,1)S(1)} collective-permute-done((bf16[1024,128]{1,0:T(8,128)(2,1)S(1)}, bf16[1024,128]{1,0:T(8,128)(2,1)S(1)}, u32[]{:S(2)}, u32[]{:S(2)}) %collective-permute-start.7) | collective-permute-done | bytes 262176 | tf_op jit(solution)/shard_map/ppermute | solution.py:390
  40.3 2.2 %prefix_attention_0.1 = (bf16[544,128]{1,0:T(8,128)(2,1)S(1)}, bf16[544,128]{1,0:T(8,128)(2,1)}, bf16[544,128]{1,0:T(8,128)(2,1)S(1)}, bf16[544,128]{1,0:T(8,128)(2,1)S(1)}) custom-call(bf16[1024,128]{1,0:T(8,128)(2,1)S(1)} %get-tuple-element.45.refs_0_, bf16[1024,128]{1,0:T(8,128)(2,1)S(1)} %collective-permute-done.5.refs_1_, ...), custom_call_target="tpu_custom_call" | custom-call | tf_op jit(solution)/shard_map/prefix_attention_0/pallas_call | solution.py:259
  43.1 1.8 %collective-permute-start.12 = (bf16[544,128]{1,0:T(8,128)(2,1)}, bf16[544,128]{1,0:T(8,128)(2,1)S(1)}, u32[]{:S(2)}, u32[]{:S(2)}) collective-permute-start(bf16[544,128]{1,0:T(8,128)(2,1)} %get-tuple-element.50), channel_id=1, source_target_pairs={{0,24},{8,0},{16,8},{24,16},{1,25},{9,1},{17,9},{25,17},{2,26},{10... | collective-permute-start | bytes 417800 | tf_op jit(solution)/shard_map/ppermute | solution.py:390
  46.8 1.6 %prefix_attention_4.1 = (bf16[544,128]{1,0:T(8,128)(2,1)S(1)}, bf16[544,128]{1,0:T(8,128)(2,1)S(1)}, bf16[544,128]{1,0:T(8,128)(2,1)S(1)}, bf16[544,128]{1,0:T(8,128)(2,1)S(1)}) custom-call(bf16[1024,128]{1,0:T(8,128)(2,1)S(1)} %get-tuple-element.45.refs_0_, bf16[1024,128]{1,0:T(8,128)(2,1)S(1)} %collective-permute-done.5.refs_1_, ...), custom_call_target="tpu_custom_call" | custom-call | tf_op jit(solution)/shard_map/prefix_attention_4/pallas_call | solution.py:259
  48.3 2.6 %collective-permute-start.19 = (bf16[544,128]{1,0:T(8,128)(2,1)S(1)}, bf16[544,128]{1,0:T(8,128)(2,1)S(1)}, u32[]{:S(2)}, u32[]{:S(2)}) collective-permute-start(bf16[544,128]{1,0:T(8,128)(2,1)S(1)} %get-tuple-element.55), channel_id=1, source_target_pairs={{0,24},{8,0},{16,8},{24,16},{1,25},{9,1},{17,9},{25,17},{2,26},{10... | collective-permute-start | bytes 417800 | tf_op jit(solution)/shard_map/ppermute | solution.py:390
  51.0 2.0 %collective-permute-start.21 = (bf16[544,128]{1,0:T(8,128)(2,1)S(1)}, bf16[544,128]{1,0:T(8,128)(2,1)S(1)}, u32[]{:S(2)}, u32[]{:S(2)}) collective-permute-start(bf16[544,128]{1,0:T(8,128)(2,1)S(1)} %get-tuple-element.57), channel_id=1, source_target_pairs={{0,16},{8,24},{16,0},{24,8},{1,17},{9,25},{17,1},{25,9},{2,18},{10... | collective-permute-start | bytes 417800 | tf_op jit(solution)/shard_map/ppermute | solution.py:390
  53.7 2.8 %local_attention.1 = (f32[8,128,128]{2,1,0:T(8,128)S(1)}, f32[16,128]{1,0:T(8,128)S(1)}) custom-call(s32[8]{0:T(128)S(1)} %copy-done.8, bf16[8,128,128]{2,1,0:T(8,128)(2,1)S(1)} %bitcast.25, bf16[8,32,1024]{2,1,0:T(8,128)(2,1)S(1)} %copy-done.2, bf16[8,32,1024]{2,1,0:T(8,128)(2,1)S(1)} %copy-done.3, bf16[8,16,128]{2,1,0:T(8,128)(2,1)S(1)} %bitcast.26, ...), custom_call_target="tpu_custom_call" | custom-call | tf_op jit(solution)/shard_map/local_attention/pallas_call | solution.py:89
  56.5 2.6 %collective-permute-done.20.refs_6_ = bf16[544,128]{1,0:T(8,128)(2,1)S(1)} collective-permute-done((bf16[544,128]{1,0:T(8,128)(2,1)S(1)}, bf16[544,128]{1,0:T(8,128)(2,1)S(1)}, u32[]{:S(2)}, u32[]{:S(2)}) %collective-permute-start.20) | collective-permute-done | bytes 139296 | tf_op jit(solution)/shard_map/ppermute | solution.py:390
  60.0 1.5 %collective-permute-done.22.got_ref = bf16[1088,128]{1,0:T(8,128)(2,1)S(1)} collective-permute-done((bf16[1088,128]{1,0:T(8,128)(2,1)S(1)}, bf16[1088,128]{1,0:T(8,128)(2,1)S(1)}, u32[]{:S(2)}, u32[]{:S(2)}) %collective-permute-start.22) | collective-permute-done | bytes 278560 | tf_op jit(solution)/shard_map/ppermute | solution.py:394
  64.3 2.1 %collective-permute-start.25 = (bf16[272,128]{1,0:T(8,128)(2,1)S(1)}, bf16[272,128]{1,0:T(8,128)(2,1)S(1)}, u32[]{:S(2)}, u32[]{:S(2)}) collective-permute-start(bf16[272,128]{1,0:T(8,128)(2,1)S(1)} %get-tuple-element.74), channel_id=1, source_target_pairs={{0,2},{1,3},{2,0},{3,1},{4,6},{5,7},{6,4},{7,5},{8,10},{9,11},{10,... | collective-permute-start | bytes 208904 | tf_op jit(solution)/shard_map/ppermute | solution.py:386
  66.6 2.8 %collective-permute-done.24.refs_2_ = bf16[272,128]{1,0:T(8,128)(2,1)S(1)} collective-permute-done((bf16[272,128]{1,0:T(8,128)(2,1)S(1)}, bf16[272,128]{1,0:T(8,128)(2,1)S(1)}, u32[]{:S(2)}, u32[]{:S(2)}) %collective-permute-start.24) | collective-permute-done | bytes 69664 | tf_op jit(solution)/shard_map/ppermute | solution.py:386
  70.2 1.5 %combine_parts.1 = bf16[8,128,128]{2,1,0:T(8,128)(2,1)} custom-call(s32[1]{0:T(128)} %bitcast.x_ref, bf16[272,128]{1,0:T(8,128)(2,1)S(1)} %get-tuple-element.71.refs_0_, bf16[272,128]{1,0:T(8,128)(2,1)S(1)} %collective-permute-done.23.refs_1_, bf16[272,128]{1,0:T(8,128)(2,1)S(1)} %collective-permute-done.24.refs_2_, ...), custom_call_target="tpu_custom_call" | custom-call | tf_op jit(solution)/shard_map/combine_parts/pallas_call | solution.py:374
  (74 shorter events, 14.9 us)
Async XLA Ops:
  2.7 10.2 %collective-permute-start.9 = (bf16[1040,128]{1,0:T(8,128)(2,1)S(1)}, bf16[1040,128]{1,0:T(8,128)(2,1)S(1)}, u32[]{:S(2)}, u32[]{:S(2)}) collective-permute-start(bf16[1040,128]{1,0:T(8,128)(2,1)S(1)} %build_cache.1.refs_4_), channel_id=1, source_target_pairs={{0,4},{4,0},{1,5},{5,1},{2,6},{6,2},{3,7},{7,3},{8,12},{12,8},{9,1... | collective-permute-start | bytes 798728 | tf_op jit(solution)/shard_map/ppermute | solution.py:394
  2.8 10.3 %collective-permute-start.8 = (bf16[1040,128]{1,0:T(8,128)(2,1)S(1)}, bf16[1040,128]{1,0:T(8,128)(2,1)S(1)}, u32[]{:S(2)}, u32[]{:S(2)}) collective-permute-start(bf16[1040,128]{1,0:T(8,128)(2,1)S(1)} %build_cache.1.refs_4_), channel_id=1, source_target_pairs={{0,32},{4,228},{32,64},{36,4},{64,96},{68,36},{96,128},{100,68},{1... | collective-permute-start | bytes 798728 | tf_op jit(solution)/shard_map/ppermute | solution.py:402
  4.8 6.0 %collective-permute-start = (s32[32]{0:T(128)S(1)}, s32[32]{0:T(128)S(1)}, u32[]{:S(2)}, u32[]{:S(2)}) collective-permute-start(s32[32]{0:T(128)S(1)} %bitcast.28), channel_id=1, source_target_pairs={{0,4},{4,0},{1,5},{5,1},{2,6},{6,2},{3,7},{7,3},{8,12},{12,8},{9,1... | collective-permute-start | bytes 392 | tf_op jit(solution)/shard_map/ppermute | solution.py:394
  8.9 6.8 %collective-permute-start.1 = (bf16[256,128]{1,0:T(8,128)(2,1)S(1)}, bf16[256,128]{1,0:T(8,128)(2,1)S(1)}, u32[]{:S(2)}, u32[]{:S(2)}) collective-permute-start(bf16[256,128]{1,0:T(8,128)(2,1)S(1)} %get-tuple-element.42), channel_id=1, source_target_pairs={{0,3},{1,0},{2,1},{3,2},{4,7},{5,4},{6,5},{7,6},{8,11},{9,8},{10,9... | collective-permute-start | bytes 196616 | tf_op jit(solution)/shard_map/ppermute | solution.py:386
  9.7 5.9 %collective-permute-start.2 = (bf16[256,128]{1,0:T(8,128)(2,1)S(1)}, bf16[256,128]{1,0:T(8,128)(2,1)S(1)}, u32[]{:S(2)}, u32[]{:S(2)}) collective-permute-start(bf16[256,128]{1,0:T(8,128)(2,1)S(1)} %get-tuple-element.43), channel_id=1, source_target_pairs={{0,2},{1,3},{2,0},{3,1},{4,6},{5,7},{6,4},{7,5},{8,10},{9,11},{10,... | collective-permute-start | bytes 196616 | tf_op jit(solution)/shard_map/ppermute | solution.py:386
  10.8 5.2 %collective-permute-start.3 = (bf16[256,128]{1,0:T(8,128)(2,1)S(1)}, bf16[256,128]{1,0:T(8,128)(2,1)S(1)}, u32[]{:S(2)}, u32[]{:S(2)}) collective-permute-start(bf16[256,128]{1,0:T(8,128)(2,1)S(1)} %get-tuple-element.44), channel_id=1, source_target_pairs={{0,1},{1,2},{2,3},{3,0},{4,5},{5,6},{6,7},{7,4},{8,9},{9,10},{10,1... | collective-permute-start | bytes 196616 | tf_op jit(solution)/shard_map/ppermute | solution.py:386
  12.9 7.6 %collective-permute-start.10 = (bf16[1040,128]{1,0:T(8,128)(2,1)S(1)}, bf16[1040,128]{1,0:T(8,128)(2,1)S(1)}, u32[]{:S(2)}, u32[]{:S(2)}) collective-permute-start(bf16[1040,128]{1,0:T(8,128)(2,1)S(1)} %collective-permute-done.9), channel_id=1, source_target_pairs={{0,32},{4,228},{32,64},{36,4},{64,96},{68,36},{96,128},{100,68},{1... | collective-permute-start | bytes 798728 | tf_op jit(solution)/shard_map/ppermute | solution.py:402
  13.1 10.3 %collective-permute-start.11 = (bf16[1040,128]{1,0:T(8,128)(2,1)S(1)}, bf16[1040,128]{1,0:T(8,128)(2,1)S(1)}, u32[]{:S(2)}, u32[]{:S(2)}) collective-permute-start(bf16[1040,128]{1,0:T(8,128)(2,1)S(1)} %collective-permute-done.8.refs_5_), channel_id=1, source_target_pairs={{0,32},{4,228},{32,64},{36,4},{64,96},{68,36},{96,128},{100,68},{1... | collective-permute-start | bytes 798728 | tf_op jit(solution)/shard_map/ppermute | solution.py:402
  16.1 7.4 %collective-permute-start.4 = (bf16[1024,128]{1,0:T(8,128)(2,1)S(1)}, bf16[1024,128]{1,0:T(8,128)(2,1)S(1)}, u32[]{:S(2)}, u32[]{:S(2)}) collective-permute-start(bf16[1024,128]{1,0:T(8,128)(2,1)S(1)} %stack_queries.1.own_ref), channel_id=1, source_target_pairs={{0,4},{4,0},{1,5},{5,1},{2,6},{6,2},{3,7},{7,3},{8,12},{12,8},{9,1... | collective-permute-start | bytes 786440 | tf_op jit(solution)/shard_map/ppermute | solution.py:394
  20.5 9.9 %collective-permute-start.15 = (bf16[1040,128]{1,0:T(8,128)(2,1)S(1)}, bf16[1040,128]{1,0:T(8,128)(2,1)S(1)}, u32[]{:S(2)}, u32[]{:S(2)}) collective-permute-start(bf16[1040,128]{1,0:T(8,128)(2,1)S(1)} %collective-permute-done.10.refs_6_), channel_id=1, source_target_pairs={{0,32},{4,228},{32,64},{36,4},{64,96},{68,36},{96,128},{100,68},{1... | collective-permute-start | bytes 798728 | tf_op jit(solution)/shard_map/ppermute | solution.py:402
  23.4 7.6 %collective-permute-start.16 = (bf16[1040,128]{1,0:T(8,128)(2,1)S(1)}, bf16[1040,128]{1,0:T(8,128)(2,1)S(1)}, u32[]{:S(2)}, u32[]{:S(2)}) collective-permute-start(bf16[1040,128]{1,0:T(8,128)(2,1)S(1)} %collective-permute-done.11.refs_7_), channel_id=1, source_target_pairs={{0,32},{4,228},{32,64},{36,4},{64,96},{68,36},{96,128},{100,68},{1... | collective-permute-start | bytes 798728 | tf_op jit(solution)/shard_map/ppermute | solution.py:402
  25.1 9.5 %collective-permute-start.5 = (bf16[1024,128]{1,0:T(8,128)(2,1)}, bf16[1024,128]{1,0:T(8,128)(2,1)S(1)}, u32[]{:S(2)}, u32[]{:S(2)}) collective-permute-start(bf16[1024,128]{1,0:T(8,128)(2,1)} %get-tuple-element.46), channel_id=1, source_target_pairs={{0,8},{8,16},{16,24},{24,0},{1,9},{9,17},{17,25},{25,1},{2,10},{10... | collective-permute-start | bytes 786440 | tf_op jit(solution)/shard_map/ppermute | solution.py:390
  26.7 9.5 %collective-permute-start.6 = (bf16[1024,128]{1,0:T(8,128)(2,1)}, bf16[1024,128]{1,0:T(8,128)(2,1)S(1)}, u32[]{:S(2)}, u32[]{:S(2)}) collective-permute-start(bf16[1024,128]{1,0:T(8,128)(2,1)} %get-tuple-element.47), channel_id=1, source_target_pairs={{0,24},{8,0},{16,8},{24,16},{1,25},{9,1},{17,9},{25,17},{2,26},{10... | collective-permute-start | bytes 786440 | tf_op jit(solution)/shard_map/ppermute | solution.py:390
  28.3 12.0 %collective-permute-start.7 = (bf16[1024,128]{1,0:T(8,128)(2,1)S(1)}, bf16[1024,128]{1,0:T(8,128)(2,1)S(1)}, u32[]{:S(2)}, u32[]{:S(2)}) collective-permute-start(bf16[1024,128]{1,0:T(8,128)(2,1)S(1)} %get-tuple-element.48), channel_id=1, source_target_pairs={{0,16},{8,24},{16,0},{24,8},{1,17},{9,25},{17,1},{25,9},{2,18},{10... | collective-permute-start | bytes 786440 | tf_op jit(solution)/shard_map/ppermute | solution.py:390
  30.5 16.3 %collective-permute-start.17 = (bf16[1040,128]{1,0:T(8,128)(2,1)S(1)}, bf16[1040,128]{1,0:T(8,128)(2,1)S(1)}, u32[]{:S(2)}, u32[]{:S(2)}) collective-permute-start(bf16[1040,128]{1,0:T(8,128)(2,1)S(1)} %collective-permute-done.15.refs_4_), channel_id=1, source_target_pairs={{0,32},{4,228},{32,64},{36,4},{64,96},{68,36},{96,128},{100,68},{1... | collective-permute-start | bytes 798728 | tf_op jit(solution)/shard_map/ppermute | solution.py:402
  31.0 15.7 %collective-permute-start.18 = (bf16[1040,128]{1,0:T(8,128)(2,1)S(1)}, bf16[1040,128]{1,0:T(8,128)(2,1)S(1)}, u32[]{:S(2)}, u32[]{:S(2)}) collective-permute-start(bf16[1040,128]{1,0:T(8,128)(2,1)S(1)} %collective-permute-done.16.refs_5_), channel_id=1, source_target_pairs={{0,32},{4,228},{32,64},{36,4},{64,96},{68,36},{96,128},{100,68},{1... | collective-permute-start | bytes 798728 | tf_op jit(solution)/shard_map/ppermute | solution.py:402
  43.1 7.9 %collective-permute-start.12 = (bf16[544,128]{1,0:T(8,128)(2,1)}, bf16[544,128]{1,0:T(8,128)(2,1)S(1)}, u32[]{:S(2)}, u32[]{:S(2)}) collective-permute-start(bf16[544,128]{1,0:T(8,128)(2,1)} %get-tuple-element.50), channel_id=1, source_target_pairs={{0,24},{8,0},{16,8},{24,16},{1,25},{9,1},{17,9},{25,17},{2,26},{10... | collective-permute-start | bytes 417800 | tf_op jit(solution)/shard_map/ppermute | solution.py:390
  45.1 11.4 %collective-permute-start.13 = (bf16[544,128]{1,0:T(8,128)(2,1)}, bf16[544,128]{1,0:T(8,128)(2,1)S(1)}, u32[]{:S(2)}, u32[]{:S(2)}) collective-permute-start(bf16[544,128]{1,0:T(8,128)(2,1)} %copy-done.9), channel_id=1, source_target_pairs={{0,8},{8,16},{16,24},{24,0},{1,9},{9,17},{17,25},{25,1},{2,10},{10... | collective-permute-start | bytes 417800 | tf_op jit(solution)/shard_map/ppermute | solution.py:390
  45.4 11.1 %collective-permute-start.14 = (bf16[544,128]{1,0:T(8,128)(2,1)S(1)}, bf16[544,128]{1,0:T(8,128)(2,1)S(1)}, u32[]{:S(2)}, u32[]{:S(2)}) collective-permute-start(bf16[544,128]{1,0:T(8,128)(2,1)S(1)} %get-tuple-element.52), channel_id=1, source_target_pairs={{0,16},{8,24},{16,0},{24,8},{1,17},{9,25},{17,1},{25,9},{2,18},{10... | collective-permute-start | bytes 417800 | tf_op jit(solution)/shard_map/ppermute | solution.py:390
  48.3 8.2 %collective-permute-start.19 = (bf16[544,128]{1,0:T(8,128)(2,1)S(1)}, bf16[544,128]{1,0:T(8,128)(2,1)S(1)}, u32[]{:S(2)}, u32[]{:S(2)}) collective-permute-start(bf16[544,128]{1,0:T(8,128)(2,1)S(1)} %get-tuple-element.55), channel_id=1, source_target_pairs={{0,24},{8,0},{16,8},{24,16},{1,25},{9,1},{17,9},{25,17},{2,26},{10... | collective-permute-start | bytes 417800 | tf_op jit(solution)/shard_map/ppermute | solution.py:390
  50.9 8.2 %collective-permute-start.20 = (bf16[544,128]{1,0:T(8,128)(2,1)S(1)}, bf16[544,128]{1,0:T(8,128)(2,1)S(1)}, u32[]{:S(2)}, u32[]{:S(2)}) collective-permute-start(bf16[544,128]{1,0:T(8,128)(2,1)S(1)} %get-tuple-element.56), channel_id=1, source_target_pairs={{0,8},{8,16},{16,24},{24,0},{1,9},{9,17},{17,25},{25,1},{2,10},{10... | collective-permute-start | bytes 417800 | tf_op jit(solution)/shard_map/ppermute | solution.py:390
  51.0 8.1 %collective-permute-start.21 = (bf16[544,128]{1,0:T(8,128)(2,1)S(1)}, bf16[544,128]{1,0:T(8,128)(2,1)S(1)}, u32[]{:S(2)}, u32[]{:S(2)}) collective-permute-start(bf16[544,128]{1,0:T(8,128)(2,1)S(1)} %get-tuple-element.57), channel_id=1, source_target_pairs={{0,16},{8,24},{16,0},{24,8},{1,17},{9,25},{17,1},{25,9},{2,18},{10... | collective-permute-start | bytes 417800 | tf_op jit(solution)/shard_map/ppermute | solution.py:390
  63.1 6.2 %collective-permute-start.24 = (bf16[272,128]{1,0:T(8,128)(2,1)S(1)}, bf16[272,128]{1,0:T(8,128)(2,1)S(1)}, u32[]{:S(2)}, u32[]{:S(2)}) collective-permute-start(bf16[272,128]{1,0:T(8,128)(2,1)S(1)} %get-tuple-element.73), channel_id=1, source_target_pairs={{0,3},{1,0},{2,1},{3,2},{4,7},{5,4},{6,5},{7,6},{8,11},{9,8},{10,9... | collective-permute-start | bytes 208904 | tf_op jit(solution)/shard_map/ppermute | solution.py:386
  64.3 5.9 %collective-permute-start.25 = (bf16[272,128]{1,0:T(8,128)(2,1)S(1)}, bf16[272,128]{1,0:T(8,128)(2,1)S(1)}, u32[]{:S(2)}, u32[]{:S(2)}) collective-permute-start(bf16[272,128]{1,0:T(8,128)(2,1)S(1)} %get-tuple-element.74), channel_id=1, source_target_pairs={{0,2},{1,3},{2,0},{3,1},{4,6},{5,7},{6,4},{7,5},{8,10},{9,11},{10,... | collective-permute-start | bytes 208904 | tf_op jit(solution)/shard_map/ppermute | solution.py:386
  (13 other events, 47.7 us)
